TPU v7x, 512 devices: a whole 4x4x16 slice. The times are simulated.
512 devices in a mesh: dp: 64 (over y, z), mp: 8 (over x, core).
Axes of the slice: x: 4, y: 4, z: 16, core: 2. Of those that a mesh axis runs over, the one named last changes fastest.
Arguments:
- pre_act: bfloat16 [32768, 16384], P('dp', 'mp'), may hold values from -8 to 8
- out_weight: bfloat16 [16384, 512], P('mp'), may hold values from -0.046875 to 0.046875
- out_grad: bfloat16 [32768, 512], P(('dp', 'mp')), may hold values from -2 to 2
Outputs:
- projected: bfloat16 [32768, 512], P(('dp', 'mp'))
- combined: float32 [16384, 512], P(('mp', 'dp'))
All inputs are finite; a program needn't handle non-finite values.
Results may differ from a plain program's by a relative error of at most 0.0005.
Values may be sent and summed in bfloat16 or wider, within the bound.
No kernel may reach another device: no remote copies, remote signals or barrier semaphores. Data moves between devices by JAX's collectives and lax.ppermute only.
A program may use at most 64 MiB of HBM per device.

v0:
```python
import jax
import jax.numpy as jnp
from jax import lax
from jax.sharding import PartitionSpec as P

epsilon = 1e-06


def from_partner(value, axis, apart):
    mask = 2**apart
    pairs = [(source, source ^ mask) for source in range(lax.axis_size(axis))]
    return lax.ppermute(value, axis, pairs)


def from_everyone(array, axis):
    copies = jnp.broadcast_to(array, (lax.axis_size(axis), *array.shape))
    return lax.all_to_all(copies, axis, split_axis=0, concat_axis=0, tiled=True)


def taken_together(array, axis):
    return from_everyone(array, axis).sum(axis=0)


def split_up(array, dim, peers):
    shape = array.shape
    blocks = array.reshape(*shape[:dim], peers, shape[dim] // peers, *shape[dim + 1 :])
    return jnp.moveaxis(blocks, dim, 0)


def summed_on_arrival(array, axis, dim):
    blocks = split_up(array, dim, lax.axis_size(axis))
    arrived = lax.all_to_all(blocks, axis, split_axis=0, concat_axis=0, tiled=True)
    return arrived.sum(axis=0)


def joined_along(blocks, dim):
    blocks = jnp.moveaxis(blocks, 0, dim)
    shape = blocks.shape
    return blocks.reshape(*shape[:dim], shape[dim] * shape[dim + 1], *shape[dim + 2 :])


def collect(array, axis, dim):
    return joined_along(from_everyone(array, axis), dim)


def contract(left, right):
    return lax.dot_general(
        left, right, (((0,), (0,)), ((), ())), preferred_element_type=jnp.float32
    )


def split_rows(piece, block, which):
    width = piece.shape[1]
    blocks = piece.reshape(piece.shape[0] // (2 * block), 2, block, width)
    kept = lax.dynamic_index_in_dim(blocks, which, 1, False).reshape(-1, width)
    sent = lax.dynamic_index_in_dim(blocks, 1 - which, 1, False).reshape(-1, width)
    return (kept, sent)


def partner_half(sent, level):
    return from_partner(sent, "dp", level)


def level_sums(partial_value, level):
    totals = taken_together(partial_value, "mp")
    for inner_bit in range(level + 1):
        totals = totals + from_partner(totals, "dp", inner_bit)
    return totals


def merge_level(own, other, level, which):
    lower = which == 0
    own_sq = jnp.sum(own * own)
    other_sq = jnp.sum(other * other)
    partial_value = jnp.stack(
        [
            jnp.sum(own * other),
            jnp.where(lower, own_sq, other_sq),
            jnp.where(lower, other_sq, own_sq),
        ]
    )
    totals = level_sums(partial_value, level)
    first_coef = 1.0 - totals[0] / (2.0 * (totals[1] + epsilon))
    second_coef = 1.0 - totals[0] / (2.0 * (totals[2] + epsilon))
    own_coef = jnp.where(lower, first_coef, second_coef)
    other_coef = jnp.where(lower, second_coef, first_coef)
    return own_coef * own + other_coef * other


def local(pre_act, out_weight, out_grad):
    act = jnp.maximum(pre_act, jnp.zeros((), jnp.bfloat16))
    tokens = act.shape[0]
    partial_out = jnp.dot(act, out_weight, preferred_element_type=jnp.float32)
    summed = summed_on_arrival(partial_out, "mp", 0)
    projected = summed.astype(jnp.bfloat16)
    grad_full = collect(out_grad, "mp", 0)
    count = lax.axis_size("dp")
    levels = count.bit_length() - 1
    me = lax.axis_index("dp")
    block = act.shape[1] // count
    first_bit = me & 1
    groups = act.reshape(tokens, act.shape[1] // (2 * block), 2, block)
    kept_act = lax.dynamic_index_in_dim(groups, first_bit, 2, False).reshape(tokens, -1)
    sent_act = lax.dynamic_index_in_dim(groups, 1 - first_bit, 2, False).reshape(tokens, -1)
    packed = jnp.concatenate([sent_act, grad_full], axis=1)
    arrived = from_partner(packed, "dp", 0)
    half = sent_act.shape[1]
    own = contract(kept_act, grad_full)
    other = contract(arrived[:, :half], arrived[:, half:])
    piece = merge_level(own, other, 0, first_bit)
    for level in range(1, levels):
        which = me >> level & 1
        own, sent = split_rows(piece, block, which)
        other = partner_half(sent, level)
        piece = merge_level(own, other, level, which)
    return (projected, piece)


def solution(mesh):
    placed = (P("dp", "mp"), P("mp", None), P(("dp", "mp"), None))
    return jax.shard_map(
        local,
        mesh=mesh,
        in_specs=placed,
        out_specs=(P(("dp", "mp"), None), P(("mp", "dp"), None)),
        check_vma=False,
    )
```

profile of v0, /device:TPU:1, one launch (start us, length us, event | category | flops | bytes accessed | tf_op | source)
XLA Modules:
  0.0 479.8 jit_solution(13337040673294925826)
XLA Ops:
  2.5 10.3 %all-to-all-start.1 = ((bf16[8,64,512]{2,1,0:T(8,128)(2,1)}), bf16[8,64,512]{2,1,0:T(8,128)(2,1)S(1)}, u32[]{:S(2)}, u32[]{:S(2)}) async-start(bf16[8,64,512]{2,1,0:T(8,128)(2,1)} %broadcast_in_dim.21), calls=%async_computation.1 | async-start | bytes 1048576 | tf_op jit(solution)/shard_map/all_to_all | solution.py:17
  12.8 3.9 copy.21
  22.5 2.5 pad_maximum_fusion
  26.9 35.3 %collective-permute-done = bf16[512,1536]{0,1:T(8,128)(2,1)} collective-permute-done((bf16[512,1536]{0,1:T(8,128)(2,1)}, bf16[512,1536]{0,1:T(8,128)(2,1)}, u32[]{:S(2)}, u32[]{:S(2)}) %collective-permute-start) | collective-permute-done | bytes 1572896 | tf_op jit(solution)/shard_map/ppermute | solution.py:12
  64.3 2.7 multiply_reduce_fusion.2
  70.7 5.0 %all-to-all-start.2 = ((f32[8,1,3]{2,1,0:T(1,128)}), f32[8,1,3]{2,1,0:T(1,128)S(1)}, u32[]{:S(2)}, u32[]{:S(2)}) async-start(f32[8,1,3]{2,1,0:T(1,128)} %broadcast_in_dim.22), calls=%async_computation.2 | async-start | bytes 8192 | tf_op jit(solution)/shard_map/all_to_all | solution.py:17
  75.7 4.5 all-to-all-done.2
  82.2 2.4 collective-permute-done.1
  87.6 2.7 multiply_add_fusion
  94.1 48.5 %collective-permute-done.2 = f32[512,512]{1,0:T(8,128)} collective-permute-done((f32[512,512]{1,0:T(8,128)}, f32[512,512]{1,0:T(8,128)}, u32[]{:S(2)}, u32[]{:S(2)}) %collective-permute-start.2) | collective-permute-done | bytes 1048608 | tf_op jit(solution)/shard_map/ppermute | solution.py:12
  148.4 3.7 all-to-all-start.3
  152.1 4.5 all-to-all-done.3
  162.8 3.3 collective-permute-done.4
  172.0 5.4 %collective-permute-start.5 = (f32[256,512]{1,0:T(8,128)}, f32[256,512]{1,0:T(8,128)S(1)}, u32[]{:S(2)}, u32[]{:S(2)}) collective-permute-start(f32[256,512]{1,0:T(8,128)} %bitcast.20), channel_id=1, source_target_pairs={{0,32},{8,40},{16,48},{24,56},{32,0},{40,8},{48,16},{56,24},{64,96... | collective-permute-start | bytes 1572872 | tf_op jit(solution)/shard_map/ppermute | solution.py:12
  177.5 47.8 %collective-permute-done.5 = f32[256,512]{1,0:T(8,128)S(1)} collective-permute-done((f32[256,512]{1,0:T(8,128)}, f32[256,512]{1,0:T(8,128)S(1)}, u32[]{:S(2)}, u32[]{:S(2)}) %collective-permute-start.5) | collective-permute-done | bytes 524320 | tf_op jit(solution)/shard_map/ppermute | solution.py:12
  229.9 3.7 all-to-all-start.4
  233.6 4.5 all-to-all-done.4
  240.1 2.4 collective-permute-done.6
  244.4 3.3 collective-permute-done.7
  247.6 5.1 %collective-permute-start.8 = (f32[3]{0:T(128)S(1)}, f32[3]{0:T(128)S(1)}, u32[]{:S(2)}, u32[]{:S(2)}) collective-permute-start(f32[3]{0:T(128)S(1)} %add.193), channel_id=1, source_target_pairs={{0,32},{8,40},{16,48},{24,56},{32,0},{40,8},{48,16},{56,24},{64,96... | collective-permute-start | bytes 44 | tf_op jit(solution)/shard_map/ppermute | solution.py:12
  252.8 3.0 collective-permute-done.8
  259.7 11.2 %collective-permute-start.9 = (f32[128,512]{1,0:T(8,128)S(1)}, f32[128,512]{1,0:T(8,128)S(1)}, u32[]{:S(2)}, u32[]{:S(2)}) collective-permute-start(f32[128,512]{1,0:T(8,128)S(1)} %bitcast.99), channel_id=1, source_target_pairs={{0,64},{8,72},{16,80},{24,88},{32,96},{40,104},{48,112},{56,120},{... | collective-permute-start | bytes 786440 | tf_op jit(solution)/shard_map/ppermute | solution.py:12
  271.0 4.9 %collective-permute-done.9 = f32[128,512]{1,0:T(8,128)S(1)} collective-permute-done((f32[128,512]{1,0:T(8,128)S(1)}, f32[128,512]{1,0:T(8,128)S(1)}, u32[]{:S(2)}, u32[]{:S(2)}) %collective-permute-start.9) | collective-permute-done | bytes 262176 | tf_op jit(solution)/shard_map/ppermute | solution.py:12
  280.4 13.6 %all-to-all-start.5 = ((f32[8,1,3]{2,1,0:T(1,128)}), f32[8,1,3]{2,1,0:T(1,128)S(1)}, u32[]{:S(2)}, u32[]{:S(2)}) async-start(f32[8,1,3]{2,1,0:T(1,128)} %broadcast_in_dim.25), calls=%async_computation.5 | async-start | bytes 8192 | tf_op jit(solution)/shard_map/all_to_all | solution.py:17
  294.1 4.5 all-to-all-done.5
  298.6 10.0 %collective-permute-start.10 = (f32[3]{0:T(128)S(1)}, f32[3]{0:T(128)S(1)}, u32[]{:S(2)}, u32[]{:S(2)}) collective-permute-start(f32[3]{0:T(128)S(1)} %reduce_sum.241), channel_id=1, source_target_pairs={{0,8},{8,0},{16,24},{24,16},{32,40},{40,32},{48,56},{56,48},{64,72... | collective-permute-start | bytes 44 | tf_op jit(solution)/shard_map/ppermute | solution.py:12
  311.5 3.3 collective-permute-done.11
  314.7 7.9 %collective-permute-start.12 = (f32[3]{0:T(128)S(1)}, f32[3]{0:T(128)S(1)}, u32[]{:S(2)}, u32[]{:S(2)}) collective-permute-start(f32[3]{0:T(128)S(1)} %add.201), channel_id=1, source_target_pairs={{0,32},{8,40},{16,48},{24,56},{32,0},{40,8},{48,16},{56,24},{64,96... | collective-permute-start | bytes 44 | tf_op jit(solution)/shard_map/ppermute | solution.py:12
  323.5 10.4 %collective-permute-start.13 = (f32[3]{0:T(128)S(1)}, f32[3]{0:T(128)S(1)}, u32[]{:S(2)}, u32[]{:S(2)}) collective-permute-start(f32[3]{0:T(128)S(1)} %add.202), channel_id=1, source_target_pairs={{0,64},{8,72},{16,80},{24,88},{32,96},{40,104},{48,112},{56,120},{... | collective-permute-start | bytes 44 | tf_op jit(solution)/shard_map/ppermute | solution.py:12
  333.9 2.6 collective-permute-done.13
  340.3 3.7 collective-permute-start.14
  350.9 9.1 %all-to-all-start.6 = ((f32[8,1,3]{2,1,0:T(1,128)}), f32[8,1,3]{2,1,0:T(1,128)S(1)}, u32[]{:S(2)}, u32[]{:S(2)}) async-start(f32[8,1,3]{2,1,0:T(1,128)} %broadcast_in_dim.26), calls=%async_computation.6 | async-start | bytes 8192 | tf_op jit(solution)/shard_map/all_to_all | solution.py:17
  360.0 3.9 fusion.14
  364.5 4.2 all-to-all-start
  368.7 3.0 collective-permute-start.15
  373.3 4.2 collective-permute-start.16
  378.8 7.4 %collective-permute-start.17 = (f32[3]{0:T(128)S(1)}, f32[3]{0:T(128)S(1)}, u32[]{:S(2)}, u32[]{:S(2)}) collective-permute-start(f32[3]{0:T(128)S(1)} %add.210), channel_id=1, source_target_pairs={{0,32},{8,40},{16,48},{24,56},{32,0},{40,8},{48,16},{56,24},{64,96... | collective-permute-start | bytes 44 | tf_op jit(solution)/shard_map/ppermute | solution.py:12
  387.2 12.2 %collective-permute-start.18 = (f32[3]{0:T(128)S(1)}, f32[3]{0:T(128)S(1)}, u32[]{:S(2)}, u32[]{:S(2)}) collective-permute-start(f32[3]{0:T(128)S(1)} %add.211), channel_id=1, source_target_pairs={{0,64},{8,72},{16,80},{24,88},{32,96},{40,104},{48,112},{56,120},{... | collective-permute-start | bytes 44 | tf_op jit(solution)/shard_map/ppermute | solution.py:12
  400.2 3.6 collective-permute-start.19
  408.2 5.0 %collective-permute-start.20 = (f32[32,512]{1,0:T(8,128)S(1)}, f32[32,512]{1,0:T(8,128)S(1)}, u32[]{:S(2)}, u32[]{:S(2)}) collective-permute-start(f32[32,512]{1,0:T(8,128)S(1)} %dynamic-slice_bitcast_fusion), channel_id=1, source_target_pairs={{0,256},{8,264},{16,272},{24,280},{32,288},{40,296},{48,304},{56,3... | collective-permute-start | bytes 196616 | tf_op jit(solution)/shard_map/ppermute | solution.py:12
  419.6 10.5 %all-to-all-start.7 = ((f32[8,1,3]{2,1,0:T(1,128)}), f32[8,1,3]{2,1,0:T(1,128)S(1)}, u32[]{:S(2)}, u32[]{:S(2)}) async-start(f32[8,1,3]{2,1,0:T(1,128)} %broadcast_in_dim.27), calls=%async_computation.7 | async-start | bytes 8192 | tf_op jit(solution)/shard_map/all_to_all | solution.py:17
  430.8 3.8 all-to-all-done.7
  434.6 2.8 collective-permute-start.21
  438.9 4.1 collective-permute-start.22
  444.1 7.3 %collective-permute-start.23 = (f32[3]{0:T(128)S(1)}, f32[3]{0:T(128)S(1)}, u32[]{:S(2)}, u32[]{:S(2)}) collective-permute-start(f32[3]{0:T(128)S(1)} %add.220), channel_id=1, source_target_pairs={{0,32},{8,40},{16,48},{24,56},{32,0},{40,8},{48,16},{56,24},{64,96... | collective-permute-start | bytes 44 | tf_op jit(solution)/shard_map/ppermute | solution.py:12
  452.3 12.3 %collective-permute-start.24 = (f32[3]{0:T(128)S(1)}, f32[3]{0:T(128)S(1)}, u32[]{:S(2)}, u32[]{:S(2)}) collective-permute-start(f32[3]{0:T(128)S(1)} %add.221), channel_id=1, source_target_pairs={{0,64},{8,72},{16,80},{24,88},{32,96},{40,104},{48,112},{56,120},{... | collective-permute-start | bytes 44 | tf_op jit(solution)/shard_map/ppermute | solution.py:12
  465.5 3.5 collective-permute-start.25
  470.0 5.0 %collective-permute-start.26 = (f32[3]{0:T(128)S(1)}, f32[3]{0:T(128)S(1)}, u32[]{:S(2)}, u32[]{:S(2)}) collective-permute-start(f32[3]{0:T(128)S(1)} %add.223), channel_id=1, source_target_pairs={{0,256},{8,264},{16,272},{24,280},{32,288},{40,296},{48,304},{56,3... | collective-permute-start | bytes 44 | tf_op jit(solution)/shard_map/ppermute | solution.py:12
  (99 shorter events, 70.1 us)
Async XLA Ops:
  0.6 359.4 %copy-start = (bf16[2048,512]{1,0:T(8,128)(2,1)S(1)}, bf16[2048,512]{1,0:T(8,128)(2,1)}, u32[]{:S(2)}) copy-start(bf16[2048,512]{1,0:T(8,128)(2,1)} %param.4) | copy-start | bytes 6291460
  2.5 19.8 %all-to-all-start.1 = ((bf16[8,64,512]{2,1,0:T(8,128)(2,1)}), bf16[8,64,512]{2,1,0:T(8,128)(2,1)S(1)}, u32[]{:S(2)}, u32[]{:S(2)}) async-start(bf16[8,64,512]{2,1,0:T(8,128)(2,1)} %broadcast_in_dim.21), calls=%async_computation.1 | async-start | bytes 1048576 | tf_op jit(solution)/shard_map/all_to_all | solution.py:17
  25.0 37.2 %collective-permute-start = (bf16[512,1536]{0,1:T(8,128)(2,1)}, bf16[512,1536]{0,1:T(8,128)(2,1)}, u32[]{:S(2)}, u32[]{:S(2)}) collective-permute-start(bf16[512,1536]{0,1:T(8,128)(2,1)} %pad_maximum_fusion), channel_id=1, source_target_pairs={{0,8},{8,0},{16,24},{24,16},{32,40},{40,32},{48,56},{56,48},{64,72... | collective-permute-start | bytes 4718600 | tf_op jit(solution)/shard_map/ppermute | solution.py:12
  26.9 37.4 %copy-start.2 = (bf16[512,32,1,32]{0,3,2,1:T(8,128)(2,1)S(1)}, bf16[512,32,1,32]{0,3,2,1:T(8,128)(2,1)}, u32[]{:S(2)}) copy-start(bf16[512,32,1,32]{0,3,2,1:T(8,128)(2,1)} %get-tuple-element.25) | copy-start | bytes 3145732
  64.3 2.7 copy-start.1
  70.7 9.5 %all-to-all-start.2 = ((f32[8,1,3]{2,1,0:T(1,128)}), f32[8,1,3]{2,1,0:T(1,128)S(1)}, u32[]{:S(2)}, u32[]{:S(2)}) async-start(f32[8,1,3]{2,1,0:T(1,128)} %broadcast_in_dim.22), calls=%async_computation.2 | async-start | bytes 8192 | tf_op jit(solution)/shard_map/all_to_all | solution.py:17
  80.3 4.3 collective-permute-start.1
  92.2 50.4 %collective-permute-start.2 = (f32[512,512]{1,0:T(8,128)}, f32[512,512]{1,0:T(8,128)}, u32[]{:S(2)}, u32[]{:S(2)}) collective-permute-start(f32[512,512]{1,0:T(8,128)} %bitcast.12), channel_id=1, source_target_pairs={{0,16},{8,24},{16,0},{24,8},{32,48},{40,56},{48,32},{56,40},{64,80... | collective-permute-start | bytes 3145736 | tf_op jit(solution)/shard_map/ppermute | solution.py:12
  148.4 8.2 %all-to-all-start.3 = ((f32[8,1,3]{2,1,0:T(1,128)}), f32[8,1,3]{2,1,0:T(1,128)S(1)}, u32[]{:S(2)}, u32[]{:S(2)}) async-start(f32[8,1,3]{2,1,0:T(1,128)} %broadcast_in_dim.23), calls=%async_computation.3 | async-start | bytes 8192 | tf_op jit(solution)/shard_map/all_to_all | solution.py:17
  156.6 4.3 collective-permute-start.3
  160.9 5.2 %collective-permute-start.4 = (f32[3]{0:T(128)S(1)}, f32[3]{0:T(128)S(1)}, u32[]{:S(2)}, u32[]{:S(2)}) collective-permute-start(f32[3]{0:T(128)S(1)} %add.185), channel_id=1, source_target_pairs={{0,16},{8,24},{16,0},{24,8},{32,48},{40,56},{48,32},{56,40},{64,80... | collective-permute-start | bytes 44 | tf_op jit(solution)/shard_map/ppermute | solution.py:12
  172.0 53.3 %collective-permute-start.5 = (f32[256,512]{1,0:T(8,128)}, f32[256,512]{1,0:T(8,128)S(1)}, u32[]{:S(2)}, u32[]{:S(2)}) collective-permute-start(f32[256,512]{1,0:T(8,128)} %bitcast.20), channel_id=1, source_target_pairs={{0,32},{8,40},{16,48},{24,56},{32,0},{40,8},{48,16},{56,24},{64,96... | collective-permute-start | bytes 1572872 | tf_op jit(solution)/shard_map/ppermute | solution.py:12
  229.9 8.2 %all-to-all-start.4 = ((f32[8,1,3]{2,1,0:T(1,128)}), f32[8,1,3]{2,1,0:T(1,128)S(1)}, u32[]{:S(2)}, u32[]{:S(2)}) async-start(f32[8,1,3]{2,1,0:T(1,128)} %broadcast_in_dim.24), calls=%async_computation.4 | async-start | bytes 8192 | tf_op jit(solution)/shard_map/all_to_all | solution.py:17
  238.2 4.3 collective-permute-start.6
  242.4 5.2 %collective-permute-start.7 = (f32[3]{0:T(128)S(1)}, f32[3]{0:T(128)S(1)}, u32[]{:S(2)}, u32[]{:S(2)}) collective-permute-start(f32[3]{0:T(128)S(1)} %add.192), channel_id=1, source_target_pairs={{0,16},{8,24},{16,0},{24,8},{32,48},{40,56},{48,32},{56,40},{64,80... | collective-permute-start | bytes 44 | tf_op jit(solution)/shard_map/ppermute | solution.py:12
  247.6 8.2 %collective-permute-start.8 = (f32[3]{0:T(128)S(1)}, f32[3]{0:T(128)S(1)}, u32[]{:S(2)}, u32[]{:S(2)}) collective-permute-start(f32[3]{0:T(128)S(1)} %add.193), channel_id=1, source_target_pairs={{0,32},{8,40},{16,48},{24,56},{32,0},{40,8},{48,16},{56,24},{64,96... | collective-permute-start | bytes 44 | tf_op jit(solution)/shard_map/ppermute | solution.py:12
  259.7 16.1 %collective-permute-start.9 = (f32[128,512]{1,0:T(8,128)S(1)}, f32[128,512]{1,0:T(8,128)S(1)}, u32[]{:S(2)}, u32[]{:S(2)}) collective-permute-start(f32[128,512]{1,0:T(8,128)S(1)} %bitcast.99), channel_id=1, source_target_pairs={{0,64},{8,72},{16,80},{24,88},{32,96},{40,104},{48,112},{56,120},{... | collective-permute-start | bytes 786440 | tf_op jit(solution)/shard_map/ppermute | solution.py:12
  280.4 18.2 %all-to-all-start.5 = ((f32[8,1,3]{2,1,0:T(1,128)}), f32[8,1,3]{2,1,0:T(1,128)S(1)}, u32[]{:S(2)}, u32[]{:S(2)}) async-start(f32[8,1,3]{2,1,0:T(1,128)} %broadcast_in_dim.25), calls=%async_computation.5 | async-start | bytes 8192 | tf_op jit(solution)/shard_map/all_to_all | solution.py:17
  298.6 11.0 %collective-permute-start.10 = (f32[3]{0:T(128)S(1)}, f32[3]{0:T(128)S(1)}, u32[]{:S(2)}, u32[]{:S(2)}) collective-permute-start(f32[3]{0:T(128)S(1)} %reduce_sum.241), channel_id=1, source_target_pairs={{0,8},{8,0},{16,24},{24,16},{32,40},{40,32},{48,56},{56,48},{64,72... | collective-permute-start | bytes 44 | tf_op jit(solution)/shard_map/ppermute | solution.py:12
  309.6 5.2 %collective-permute-start.11 = (f32[3]{0:T(128)S(1)}, f32[3]{0:T(128)S(1)}, u32[]{:S(2)}, u32[]{:S(2)}) collective-permute-start(f32[3]{0:T(128)S(1)} %add.200), channel_id=1, source_target_pairs={{0,16},{8,24},{16,0},{24,8},{32,48},{40,56},{48,32},{56,40},{64,80... | collective-permute-start | bytes 44 | tf_op jit(solution)/shard_map/ppermute | solution.py:12
  314.7 8.8 %collective-permute-start.12 = (f32[3]{0:T(128)S(1)}, f32[3]{0:T(128)S(1)}, u32[]{:S(2)}, u32[]{:S(2)}) collective-permute-start(f32[3]{0:T(128)S(1)} %add.201), channel_id=1, source_target_pairs={{0,32},{8,40},{16,48},{24,56},{32,0},{40,8},{48,16},{56,24},{64,96... | collective-permute-start | bytes 44 | tf_op jit(solution)/shard_map/ppermute | solution.py:12
  323.5 13.0 %collective-permute-start.13 = (f32[3]{0:T(128)S(1)}, f32[3]{0:T(128)S(1)}, u32[]{:S(2)}, u32[]{:S(2)}) collective-permute-start(f32[3]{0:T(128)S(1)} %add.202), channel_id=1, source_target_pairs={{0,64},{8,72},{16,80},{24,88},{32,96},{40,104},{48,112},{56,120},{... | collective-permute-start | bytes 44 | tf_op jit(solution)/shard_map/ppermute | solution.py:12
  340.3 6.1 %collective-permute-start.14 = (f32[64,512]{1,0:T(8,128)S(1)}, f32[64,512]{1,0:T(8,128)S(1)}, u32[]{:S(2)}, u32[]{:S(2)}) collective-permute-start(f32[64,512]{1,0:T(8,128)S(1)} %bitcast.100), channel_id=1, source_target_pairs={{0,128},{8,136},{16,144},{24,152},{32,160},{40,168},{48,176},{56,1... | collective-permute-start | bytes 393224 | tf_op jit(solution)/shard_map/ppermute | solution.py:12
  350.9 13.6 %all-to-all-start.6 = ((f32[8,1,3]{2,1,0:T(1,128)}), f32[8,1,3]{2,1,0:T(1,128)S(1)}, u32[]{:S(2)}, u32[]{:S(2)}) async-start(f32[8,1,3]{2,1,0:T(1,128)} %broadcast_in_dim.26), calls=%async_computation.6 | async-start | bytes 8192 | tf_op jit(solution)/shard_map/all_to_all | solution.py:17
  364.5 54.4 %all-to-all-start = ((f32[8,64,512]{2,1,0:T(8,128)}), f32[8,64,512]{2,1,0:T(8,128)S(1)}, u32[]{:S(2)}, u32[]{:S(2)}) async-start(f32[8,64,512]{2,1,0:T(8,128)} %bitcast), calls=%async_computation | async-start | bytes 2097152 | tf_op jit(solution)/shard_map/all_to_all | solution.py:32
  368.7 4.6 collective-permute-start.15
  373.3 5.5 %collective-permute-start.16 = (f32[3]{0:T(128)S(1)}, f32[3]{0:T(128)S(1)}, u32[]{:S(2)}, u32[]{:S(2)}) collective-permute-start(f32[3]{0:T(128)S(1)} %add.209), channel_id=1, source_target_pairs={{0,16},{8,24},{16,0},{24,8},{32,48},{40,56},{48,32},{56,40},{64,80... | collective-permute-start | bytes 44 | tf_op jit(solution)/shard_map/ppermute | solution.py:12
  378.8 8.4 %collective-permute-start.17 = (f32[3]{0:T(128)S(1)}, f32[3]{0:T(128)S(1)}, u32[]{:S(2)}, u32[]{:S(2)}) collective-permute-start(f32[3]{0:T(128)S(1)} %add.210), channel_id=1, source_target_pairs={{0,32},{8,40},{16,48},{24,56},{32,0},{40,8},{48,16},{56,24},{64,96... | collective-permute-start | bytes 44 | tf_op jit(solution)/shard_map/ppermute | solution.py:12
  387.2 13.1 %collective-permute-start.18 = (f32[3]{0:T(128)S(1)}, f32[3]{0:T(128)S(1)}, u32[]{:S(2)}, u32[]{:S(2)}) collective-permute-start(f32[3]{0:T(128)S(1)} %add.211), channel_id=1, source_target_pairs={{0,64},{8,72},{16,80},{24,88},{32,96},{40,104},{48,112},{56,120},{... | collective-permute-start | bytes 44 | tf_op jit(solution)/shard_map/ppermute | solution.py:12
  400.2 4.6 collective-permute-start.19
  408.2 6.6 %collective-permute-start.20 = (f32[32,512]{1,0:T(8,128)S(1)}, f32[32,512]{1,0:T(8,128)S(1)}, u32[]{:S(2)}, u32[]{:S(2)}) collective-permute-start(f32[32,512]{1,0:T(8,128)S(1)} %dynamic-slice_bitcast_fusion), channel_id=1, source_target_pairs={{0,256},{8,264},{16,272},{24,280},{32,288},{40,296},{48,304},{56,3... | collective-permute-start | bytes 196616 | tf_op jit(solution)/shard_map/ppermute | solution.py:12
  419.6 15.0 %all-to-all-start.7 = ((f32[8,1,3]{2,1,0:T(1,128)}), f32[8,1,3]{2,1,0:T(1,128)S(1)}, u32[]{:S(2)}, u32[]{:S(2)}) async-start(f32[8,1,3]{2,1,0:T(1,128)} %broadcast_in_dim.27), calls=%async_computation.7 | async-start | bytes 8192 | tf_op jit(solution)/shard_map/all_to_all | solution.py:17
  434.6 4.3 collective-permute-start.21
  438.9 5.2 %collective-permute-start.22 = (f32[3]{0:T(128)S(1)}, f32[3]{0:T(128)S(1)}, u32[]{:S(2)}, u32[]{:S(2)}) collective-permute-start(f32[3]{0:T(128)S(1)} %add.219), channel_id=1, source_target_pairs={{0,16},{8,24},{16,0},{24,8},{32,48},{40,56},{48,32},{56,40},{64,80... | collective-permute-start | bytes 44 | tf_op jit(solution)/shard_map/ppermute | solution.py:12
  444.1 8.3 %collective-permute-start.23 = (f32[3]{0:T(128)S(1)}, f32[3]{0:T(128)S(1)}, u32[]{:S(2)}, u32[]{:S(2)}) collective-permute-start(f32[3]{0:T(128)S(1)} %add.220), channel_id=1, source_target_pairs={{0,32},{8,40},{16,48},{24,56},{32,0},{40,8},{48,16},{56,24},{64,96... | collective-permute-start | bytes 44 | tf_op jit(solution)/shard_map/ppermute | solution.py:12
  452.3 13.2 %collective-permute-start.24 = (f32[3]{0:T(128)S(1)}, f32[3]{0:T(128)S(1)}, u32[]{:S(2)}, u32[]{:S(2)}) collective-permute-start(f32[3]{0:T(128)S(1)} %add.221), channel_id=1, source_target_pairs={{0,64},{8,72},{16,80},{24,88},{32,96},{40,104},{48,112},{56,120},{... | collective-permute-start | bytes 44 | tf_op jit(solution)/shard_map/ppermute | solution.py:12
  465.5 4.4 collective-permute-start.25
  470.0 5.9 %collective-permute-start.26 = (f32[3]{0:T(128)S(1)}, f32[3]{0:T(128)S(1)}, u32[]{:S(2)}, u32[]{:S(2)}) collective-permute-start(f32[3]{0:T(128)S(1)} %add.223), channel_id=1, source_target_pairs={{0,256},{8,264},{16,272},{24,280},{32,288},{40,296},{48,304},{56,3... | collective-permute-start | bytes 44 | tf_op jit(solution)/shard_map/ppermute | solution.py:12
where the time goes:
time: 488 us; the launch traced here: 480 us
  waiting for transfers between devices  201 us (41%)
  starting transfers between devices  199 us (41%)
  between operations  31.4 us (6%)
  other arithmetic  24 us (5%)
  local copies, waits for them, and re-layouts  14.9 us (3%)
  matrix products  8.6 us (2%)
    ppermute x27, waiting for transfers between devices, from_partner(): return lax.ppermute(value, axis, pairs)  177 us
    ppermute x27, starting transfers between devices, from_partner(): return lax.ppermute(value, axis, pairs)  139 us
    all_to_all x7, starting transfers between devices, from_everyone(): return lax.all_to_all(copies, axis, split_axis=0, concat_axis=0, tiled=True)  55.9 us
    all_to_all x7, waiting for transfers between devices, from_everyone(): return lax.all_to_all(copies, axis, split_axis=0, concat_axis=0, tiled=True)  24.8 us
  transfers between devices with their start and end apart: 35, of which 34 were waited for; matrix products, arithmetic and copies ran while one was open for 3% of the time, Pallas kernels for 0%

commit v1 on v0

v1 whole, which is shorter than its diff:
```python
import functools

import jax
import jax.numpy as jnp
from jax import lax
from jax.experimental import pallas as pl
from jax.experimental.pallas import tpu as pltpu
from jax.sharding import Mesh, PartitionSpec as P

epsilon = 1e-06
LEAVES = 4
NODES = 16
LIMIT = 64 * 1024 * 1024 * 3 // 4
TOP = 16384.0
FLOOR = 1e-15

f32 = jnp.float32
bf16 = jnp.bfloat16
SMEM = pl.BlockSpec(memory_space=pltpu.SMEM)
VMEM = pl.BlockSpec(memory_space=pltpu.VMEM)


def call(kernel, out_shape, in_specs, flops=0, size=0, scratch=()):
    many = isinstance(out_shape, (list, tuple))
    return pl.pallas_call(
        kernel,
        out_shape=out_shape,
        in_specs=in_specs,
        out_specs=[VMEM] * len(out_shape) if many else VMEM,
        scratch_shapes=list(scratch),
        compiler_params=pltpu.CompilerParams(vmem_limit_bytes=LIMIT),
        cost_estimate=pl.CostEstimate(flops=flops, bytes_accessed=size, transcendentals=0),
    )


def from_everyone(array, axes):
    count = lax.axis_size(axes)
    copies = jnp.broadcast_to(array, (count, *array.shape))
    return lax.all_to_all(copies, axes, split_axis=0, concat_axis=0, tiled=True)


def deal_kernel(me_ref, pre_ref, *out_refs):
    me = me_ref[0]
    width = 512
    row = lax.broadcasted_iota(jnp.int32, (width, width), 0)
    col = lax.broadcasted_iota(jnp.int32, (width, width), 1)
    block = row >> 5
    place = (((block & 3) ^ me) << 7) + ((block >> 2) << 5) + (row & 31)
    deal = jnp.where(place == col, 1.0, 0.0).astype(bf16)
    for group in range(pre_ref.shape[1] // width):
        part = jnp.maximum(pre_ref[:, group * width : (group + 1) * width], jnp.zeros((), bf16))
        dealt = jnp.dot(part, deal, preferred_element_type=f32).astype(bf16)
        for k in range(LEAVES):
            out_refs[k][:, group * 128 : (group + 1) * 128] = dealt[:, k * 128 : (k + 1) * 128]


def leaf_kernel(which, act_ref, grads_ref, out_ref):
    peers, _, rows, width = grads_ref.shape
    out_grad = grads_ref[:, which].reshape(peers * rows, width)
    out_ref[...] = lax.dot_general(
        act_ref[...], out_grad, (((0,), (0,)), ((), ())), preferred_element_type=f32
    )


def lanes_of(total):
    return total[:, :128] + total[:, 128:256] + total[:, 256:384] + total[:, 384:512]


def first_gram_kernel(me_ref, *refs):
    leaf_refs, out_ref, held = refs[:LEAVES], refs[LEAVES], refs[LEAVES + 1]
    me = me_ref[0]
    for a in range(LEAVES):
        for b in range(a, LEAVES):
            partial_sum = lanes_of(jnp.sum(leaf_refs[a][...] * leaf_refs[b][...], axis=0, keepdims=True))
            held[pl.ds(LEAVES * (a ^ me) + (b ^ me), 1), :] = partial_sum
            if a != b:
                held[pl.ds(LEAVES * (b ^ me) + (a ^ me), 1), :] = partial_sum
    whole = held[...]
    for copy in range(out_ref.shape[0]):
        out_ref[copy] = whole


def tree(gram, count):
    coef = [None] * count
    weight = [jnp.ones_like(gram[0][0])] * count
    size = 1
    while size < count:
        for low in range(0, count, 2 * size):
            first, second = range(low, low + size), range(low + size, low + 2 * size)

            def inner(left, right):
                return sum(weight[i] * weight[j] * gram[i][j] for i in left for j in right)

            cross = inner(first, second)
            first_sq = jnp.maximum(inner(first, first), 0.0)
            second_sq = jnp.maximum(inner(second, second), 0.0)
            first_coef = 1.0 - cross / (2.0 * (first_sq + epsilon))
            second_coef = 1.0 - cross / (2.0 * (second_sq + epsilon))
            for i in first:
                coef[i] = weight[i] * first_coef
            for i in second:
                coef[i] = weight[i] * second_coef
        weight = list(coef)
        size *= 2
    return weight


def first_merge_kernel(me_ref, sums_ref, *refs):
    leaf_refs, node_ref, inverse_ref = refs[:LEAVES], refs[LEAVES], refs[LEAVES + 1]
    me = me_ref[0]
    total = jnp.sum(jnp.sum(sums_ref[...], axis=0), axis=1, keepdims=True)
    gram = [
        [total[LEAVES * i + j : LEAVES * i + j + 1, :] for j in range(LEAVES)] for i in range(LEAVES)
    ]
    coef = tree(gram, LEAVES)
    bound = sum(jnp.abs(coef[i]) * jnp.sqrt(gram[i][i]) for i in range(LEAVES))
    bound = jnp.maximum(bound, FLOOR)
    scale = TOP / bound
    inverse_ref[...] = jnp.broadcast_to(bound * (1.0 / TOP), inverse_ref.shape)
    merged = None
    for k in range(LEAVES):
        mine = coef[k]
        for other in range(1, LEAVES):
            mine = jnp.where(me == other, coef[k ^ other], mine)
        term = (mine * scale) * leaf_refs[k][...]
        merged = term if merged is None else merged + term
    node_ref[...] = merged


def second_gram_kernel(copies, share, node_ref, nodes_ref, inverse_ref, out_ref):
    node = node_ref[0]
    total, width = nodes_ref.shape
    rows = total // NODES
    held = nodes_ref[...]
    high = held.astype(bf16)
    low = (held - high.astype(f32)).astype(bf16)
    last = (((1,), (1,)), ((), ()))
    products = (
        lax.dot_general(high, high, last, preferred_element_type=f32)
        + lax.dot_general(high, low, last, preferred_element_type=f32)
        + lax.dot_general(low, high, last, preferred_element_type=f32)
        + lax.dot_general(low, low, last, preferred_element_type=f32)
    )
    row = lax.broadcasted_iota(jnp.int32, (total, total), 0)
    col = lax.broadcasted_iota(jnp.int32, (total, total), 1)
    products = jnp.where((row & (rows - 1)) == (col & (rows - 1)), products, 0.0)
    by_node = jnp.sum(products.reshape(NODES, rows, total), axis=1)
    source = lax.broadcasted_iota(jnp.int32, (total, 128), 0)
    lane = lax.broadcasted_iota(jnp.int32, (total, 128), 1)
    spread = jnp.where(source // rows == (lane & (NODES - 1)), 1.0, 0.0)
    gram = jnp.dot(by_node, spread, preferred_element_type=f32, precision=lax.Precision.HIGHEST)
    place = lax.broadcasted_iota(jnp.int32, (NODES, 128), 0)
    lane = lax.broadcasted_iota(jnp.int32, (NODES, 128), 1)
    packed = jnp.where(lane // NODES == (place & 7), gram, 0.0)
    lane = lane[:1]
    inverse = jnp.where(lane == node, inverse_ref[:1] * share, 0.0)
    whole = jnp.concatenate(
        [
            jnp.sum(packed[:8], axis=0, keepdims=True),
            jnp.sum(packed[8:], axis=0, keepdims=True),
            inverse,
            jnp.zeros_like(inverse),
        ],
        axis=0,
    )
    for copy in range(copies):
        out_ref[copy] = whole


def pass_on_kernel(sums_ref, out_ref):
    whole = jnp.sum(sums_ref[...], axis=0)
    for copy in range(out_ref.shape[0]):
        out_ref[copy] = whole


def second_merge_kernel(sums_ref, nodes_ref, out_ref):
    total = jnp.sum(sums_ref[...], axis=0)
    place = lax.broadcasted_iota(jnp.int32, (NODES, 128), 0)
    lane = lax.broadcasted_iota(jnp.int32, (NODES, 128), 1)
    gram = jnp.where(place < 8, total[0:1], total[1:2])
    gram = jnp.where(lane // NODES == (place & 7), gram, 0.0)
    inverse_row = jnp.where(lane[:1] < NODES, total[2:3], 0.0)
    for turn in (16, 32, 64):
        gram = gram + pltpu.roll(gram, turn, 1)
        inverse_row = inverse_row + pltpu.roll(inverse_row, turn, 1)
    other = lane & (NODES - 1)
    first = lane < NODES

    def column(row):
        return jnp.sum(jnp.where(lane == place, row, 0.0), axis=1, keepdims=True)

    inverse_col = column(inverse_row)
    gram = gram * inverse_row * inverse_col
    size, weight = 1, jnp.ones((NODES, 1), f32)
    while size < NODES:
        mine = (place // size) == (other // size)
        sibling = (place // size) == ((other // size) ^ 1)
        own_col = jnp.sum(jnp.where(mine, gram, 0.0), axis=0, keepdims=True)
        cross_col = jnp.sum(jnp.where(sibling, gram, 0.0), axis=0, keepdims=True)
        here = mine & first
        own = jnp.sum(jnp.where(here, own_col, 0.0), axis=1, keepdims=True)
        cross = jnp.sum(jnp.where(here, cross_col, 0.0), axis=1, keepdims=True)
        coef = 1.0 - cross / (2.0 * (jnp.maximum(own, 0.0) + epsilon))
        coef_row = jnp.sum(jnp.where(place == other, coef, 0.0), axis=0, keepdims=True)
        gram = gram * coef * coef_row
        weight = weight * coef
        size *= 2
    weight = weight * inverse_col
    combined = None
    for node in range(NODES):
        term = weight[node : node + 1, :] * nodes_ref[node]
        combined = term if combined is None else combined + term
    out_ref[...] = combined


def local(pre_act, out_weight, out_grad):
    tokens, hidden = pre_act.shape
    width = out_weight.shape[1]
    mp = ("x", "c")
    hi = ("y", "zh")
    peers = lax.axis_size(mp)
    me = lax.axis_index("zl").astype(jnp.int32).reshape(1)
    node = lax.axis_index(hi).astype(jnp.int32).reshape(1)
    quarter = hidden // LEAVES

    def from_neighbour(value, apart):
        return lax.ppermute(value, "zl", [(i, i ^ apart) for i in range(LEAVES)])

    grad_shards = [out_grad] + [from_neighbour(out_grad, k) for k in range(1, LEAVES)]
    dealt = call(
        deal_kernel,
        [jax.ShapeDtypeStruct((tokens, quarter), bf16)] * LEAVES,
        [SMEM, VMEM],
        flops=2 * tokens * hidden * 512,
        size=4 * tokens * hidden,
    )(me, pre_act)
    acts = [dealt[0]] + [from_neighbour(dealt[k], k) for k in range(1, LEAVES)]
    grads = from_everyone(jnp.stack(grad_shards), mp)

    act = jnp.maximum(pre_act, jnp.zeros((), bf16))
    partial_out = jnp.dot(act, out_weight, preferred_element_type=f32)
    parts = partial_out.reshape(peers, tokens // peers, width)
    arrived = lax.all_to_all(parts, mp, split_axis=0, concat_axis=0, tiled=True)
    projected = arrived.sum(axis=0).astype(bf16)

    leaf_shape = jax.ShapeDtypeStruct((quarter, width), f32)
    leaves = [
        call(
            functools.partial(leaf_kernel, k),
            leaf_shape,
            [VMEM, VMEM],
            flops=2 * tokens * quarter * width,
            size=4 * quarter * width,
        )(acts[k], grads)
        for k in range(LEAVES)
    ]
    group = ("zl", *mp)
    sums = call(
        first_gram_kernel,
        jax.ShapeDtypeStruct((LEAVES * peers, 16, 128), f32),
        [SMEM] + [VMEM] * LEAVES,
        flops=20 * quarter * width,
        size=16 * quarter * width,
        scratch=[pltpu.VMEM((16, 128), f32)],
    )(me, *leaves)
    sums = lax.all_to_all(sums, group, split_axis=0, concat_axis=0, tiled=True)
    scaled, inverse = call(
        first_merge_kernel,
        [leaf_shape, jax.ShapeDtypeStruct((8, 128), f32)],
        [SMEM] + [VMEM] * (LEAVES + 1),
        flops=8 * quarter * width,
        size=20 * quarter * width,
    )(me, sums, *leaves)

    rows = quarter // NODES
    sent = scaled.astype(jnp.float16).reshape(NODES, rows, width)
    nodes = lax.all_to_all(sent, hi, split_axis=0, concat_axis=0, tiled=True).astype(f32)
    share = 1.0 / (LEAVES * peers)
    sums = call(
        functools.partial(second_gram_kernel, peers, share),
        jax.ShapeDtypeStruct((peers, 4, 128), f32),
        [SMEM, VMEM, VMEM],
        flops=8 * quarter * quarter * width,
        size=4 * quarter * width,
    )(node, nodes.reshape(quarter, width), inverse)
    sums = lax.all_to_all(sums, mp, split_axis=0, concat_axis=0, tiled=True)
    dp = ("y", "zh", "zl")
    sums = call(pass_on_kernel, jax.ShapeDtypeStruct((lax.axis_size(dp), 4, 128), f32), [VMEM])(sums)
    sums = lax.all_to_all(sums, dp, split_axis=0, concat_axis=0, tiled=True)
    combined = call(
        second_merge_kernel,
        jax.ShapeDtypeStruct((rows, width), f32),
        [VMEM, VMEM],
        flops=2 * quarter * width,
        size=4 * quarter * width,
    )(sums, nodes)
    return projected, combined


def solution(mesh):
    devices = mesh.devices.reshape(4, 4, LEAVES, 4, 2)
    finer = Mesh(devices, ("y", "zh", "zl", "x", "c"))
    dp, mp = ("y", "zh", "zl"), ("x", "c")
    return jax.shard_map(
        local,
        mesh=finer,
        in_specs=(P(dp, mp), P(mp, None), P((*dp, *mp), None)),
        out_specs=(P((*dp, *mp), None), P((*mp, *dp), None)),
        check_vma=False,
    )
```

time: 488 us -> 209 us (0.43); the launches traced: 480 us -> 207 us
  starting transfers between devices: 199 us -> 58.5 us
  waiting for transfers between devices: 201 us -> 91 us
  between operations: 31.4 us -> 0.78 us
  blocking collectives: 0 us -> 26.3 us
  other arithmetic: 24 us -> 4.87 us
  Pallas kernels: 0 us -> 16.7 us
  local copies, waits for them, and re-layouts: 14.9 us -> 5 us
    ppermute x27 -> x6, waiting for transfers between devices: 177 us -> 34.2 us  [from_neighbour(): return lax.ppermute(value, 'zl', [(i, i ^ apart) for i in range(LEAVES)])]
    ppermute x27 -> x6, starting transfers between devices: 139 us -> 20.9 us  [from_neighbour(): return lax.ppermute(value, 'zl', [(i, i ^ apart) for i in range(LEAVES)])]
    all_to_all x8 -> x5, waiting for transfers between devices: 24.8 us -> 56.8 us  [the longest x1 29.3 us: local(): lax.all_to_all(sent, hi, split_axis=0, concat_axis=0, tiled=True)]
    all_to_all x0 -> x1, blocking collectives: none -> 26.3 us  [local(): sums = lax.all_to_all(sums, group, split_axis=0, concat_axis=0, tiled=True)]
    all_to_all x8 -> x5, starting transfers between devices: 60.1 us -> 37.7 us  [the longest x1 12.3 us: local(): lax.all_to_all(sent, hi, split_axis=0, concat_axis=0, tiled=True)]
    pallas_call x0 -> x10, Pallas kernels: none -> 16.7 us  [the longest x4 8.4 us: local(): call(functools.partial(leaf_kernel, k), leaf_shape, [VMEM, VMEM], flops=2...]
    reduce_sum x16 -> x1, other arithmetic: 10.4 us -> 1.94 us  [local(): projected = arrived.sum(axis=0).astype(bf16)]
    add x27 -> x0, other arithmetic: 5.03 us -> none  [the longest x6 4.97 us: merge_level(): return own_coef * own + other_coef * other]
  transfers between devices with their start and end apart: 35 -> 11, of which waited for: 34 -> 8; matrix products, arithmetic and copies ran while one was open for 3% -> 3% of each run, Pallas kernels for 0% -> 4%
where the time goes in v1:
time: 209 us; the launch traced here: 207 us
  waiting for transfers between devices  91 us (44%)
  starting transfers between devices  58.5 us (28%)
  blocking collectives  26.3 us (13%)
  Pallas kernels  16.7 us (8%)
  local copies, waits for them, and re-layouts  5 us (2%)
  other arithmetic  4.87 us (2%)
  matrix products  3.82 us (2%)
    ppermute x6, waiting for transfers between devices, from_neighbour(): return lax.ppermute(value, 'zl', [(i, i ^ apart) for i in range(LEAVES)])  34.2 us
    all_to_all x1, waiting for transfers between devices, local(): lax.all_to_all(sent, hi, split_axis=0, concat_axis=0, tiled=True)  29.3 us
    all_to_all x1, blocking collectives, local(): sums = lax.all_to_all(sums, group, split_axis=0, concat_axis=0, tiled=True)  26.3 us
    ppermute x6, starting transfers between devices, from_neighbour(): return lax.ppermute(value, 'zl', [(i, i ^ apart) for i in range(LEAVES)])  20.9 us
    all_to_all x1, waiting for transfers between devices, local(): arrived = lax.all_to_all(parts, mp, split_axis=0, concat_axis=0, tiled=True)  14.6 us
    all_to_all x1, starting transfers between devices, local(): lax.all_to_all(sent, hi, split_axis=0, concat_axis=0, tiled=True)  12.3 us
    all_to_all x1, waiting for transfers between devices, local(): sums = lax.all_to_all(sums, dp, split_axis=0, concat_axis=0, tiled=True)  12.1 us
    pallas_call x4, Pallas kernels, local(): call(functools.partial(leaf_kernel, k), leaf_shape, [VMEM, VMEM], flops=2...  8.4 us
  transfers between devices with their start and end apart: 11, of which 8 were waited for; matrix products, arithmetic and copies ran while one was open for 3% of the time, Pallas kernels for 4%

profile of v1, /device:TPU:1, one launch (start us, length us, event | category | flops | bytes accessed | tf_op | source)
XLA Modules:
  0.0 207.0 jit_solution(17137988558009554920)
XLA Ops:
  0.6 0.0 copy-start
  0.6 4.5 %collective-permute-start = (bf16[64,512]{1,0:T(8,128)(2,1)}, bf16[64,512]{1,0:T(8,128)(2,1)S(1)}, u32[]{:S(2)}, u32[]{:S(2)}) collective-permute-start(bf16[64,512]{1,0:T(8,128)(2,1)} %param.5), channel_id=1, source_target_pairs={{0,8},{8,0},{16,24},{24,16},{1,9},{9,1},{17,25},{25,17},{2,10},{10... | collective-permute-start | bytes 196616 | tf_op jit(solution)/shard_map/ppermute | solution.py:227
  5.2 4.9 %collective-permute-start.1 = (bf16[64,512]{1,0:T(8,128)(2,1)}, bf16[64,512]{1,0:T(8,128)(2,1)S(1)}, u32[]{:S(2)}, u32[]{:S(2)}) collective-permute-start(bf16[64,512]{1,0:T(8,128)(2,1)} %param.5), channel_id=1, source_target_pairs={{0,16},{8,24},{16,0},{24,8},{1,17},{9,25},{17,1},{25,9},{2,18},{10... | collective-permute-start | bytes 196616 | tf_op jit(solution)/shard_map/ppermute | solution.py:227
  10.1 1.9 collective-permute-start.2
  12.0 0.0 collective-permute-done
  12.0 0.3 collective-permute-done.1
  12.3 5.0 %collective-permute-done.2 = bf16[64,512]{1,0:T(8,128)(2,1)S(1)} collective-permute-done((bf16[64,512]{1,0:T(8,128)(2,1)}, bf16[64,512]{1,0:T(8,128)(2,1)S(1)}, u32[]{:S(2)}, u32[]{:S(2)}) %collective-permute-start.2) | collective-permute-done | bytes 65568 | tf_op jit(solution)/shard_map/ppermute | solution.py:227
  17.3 0.9 pad_maximum_fusion
  18.2 1.6 broadcast_in_dim.3
  19.8 7.1 %all-to-all-start.1 = ((bf16[8,4,64,512]{3,2,1,0:T(8,128)(2,1)}), bf16[8,4,64,512]{3,2,1,0:T(8,128)(2,1)}, u32[]{:S(2)}, u32[]{:S(2)}) async-start(bf16[8,4,64,512]{3,2,1,0:T(8,128)(2,1)} %broadcast_in_dim.3), calls=%async_computation.1 | async-start | bytes 4194304 | tf_op jit(solution)/shard_map/all_to_all | solution.py:39
  26.9 0.0 copy-start.3
  26.9 1.6 copy-done.3
  28.5 2.3 %shard_map.50 = (bf16[512,512]{1,0:T(8,128)(2,1)S(1)}, bf16[512,512]{1,0:T(8,128)(2,1)S(1)}, bf16[512,512]{1,0:T(8,128)(2,1)}, bf16[512,512]{1,0:T(8,128)(2,1)}) custom-call(s32[1]{0:T(128)} %bitcast.2.me_ref, bf16[512,2048]{1,0:T(8,128)(2,1)S(1)} %copy-done.3), custom_call_target="tpu_custom_call" | custom-call | flops 1073741824 | bytes 4194304 | tf_op jit(solution)/shard_map/pallas_call | solution.py:230
  30.8 1.9 collective-permute-start.3
  32.7 5.7 %collective-permute-start.4 = (bf16[512,512]{1,0:T(8,128)(2,1)}, bf16[512,512]{1,0:T(8,128)(2,1)}, u32[]{:S(2)}, u32[]{:S(2)}) collective-permute-start(bf16[512,512]{1,0:T(8,128)(2,1)} %get-tuple-element.10), channel_id=1, source_target_pairs={{0,16},{8,24},{16,0},{24,8},{1,17},{9,25},{17,1},{25,9},{2,18},{10... | collective-permute-start | bytes 1572872 | tf_op jit(solution)/shard_map/ppermute | solution.py:227
  38.4 1.9 collective-permute-start.5
  40.4 14.7 %collective-permute-done.3.act_ref = bf16[512,512]{1,0:T(8,128)(2,1)S(1)} collective-permute-done((bf16[512,512]{1,0:T(8,128)(2,1)S(1)}, bf16[512,512]{1,0:T(8,128)(2,1)S(1)}, u32[]{:S(2)}, u32[]{:S(2)}) %collective-permute-start.3) | collective-permute-done | bytes 524320 | tf_op jit(solution)/shard_map/ppermute | solution.py:227
  55.0 0.0 copy-start.1
  55.1 0.8 copy-done.1
  55.9 0.0 all-to-all-done.1.grads_ref
  55.9 0.0 copy-start.2
  55.9 1.0 copy-done.2
  56.9 2.1 shard_map.52.refs_1_
  59.0 14.2 %collective-permute-done.4.act_ref = bf16[512,512]{1,0:T(8,128)(2,1)} collective-permute-done((bf16[512,512]{1,0:T(8,128)(2,1)}, bf16[512,512]{1,0:T(8,128)(2,1)}, u32[]{:S(2)}, u32[]{:S(2)}) %collective-permute-start.4) | collective-permute-done | bytes 524320 | tf_op jit(solution)/shard_map/ppermute | solution.py:227
  73.2 2.2 %shard_map.53.refs_2_ = f32[512,512]{1,0:T(8,128)S(1)} custom-call(bf16[512,512]{1,0:T(8,128)(2,1)} %collective-permute-done.4.act_ref, bf16[8,4,64,512]{3,2,1,0:T(8,128)(2,1)} %all-to-all-done.1.grads_ref), custom_call_target="tpu_custom_call" | custom-call | flops 268435456 | bytes 1048576 | tf_op jit(solution)/shard_map/pallas_call | solution.py:248
  75.4 0.0 collective-permute-done.5.act_ref
  75.4 2.1 shard_map.54.refs_3_
  77.5 2.1 shard_map.51.refs_0_
  79.5 0.9 shard_map.55
  80.4 26.3 %all_to_all.30.sums_ref = f32[32,16,128]{2,1,0:T(8,128)S(1)} all-to-all(f32[32,16,128]{2,1,0:T(8,128)S(1)} %shard_map.55), channel_id=1, replica_groups=mesh['y'=4,'zh'=4,'zl'=4,'x'=4,'c'=2] {'zl','x','c'}, dimensions={0} | all-to-all | bytes 524288 | tf_op jit(solution)/shard_map/all_to_all | solution.py:266
  106.7 0.7 shard_map.56
  107.4 0.9 convert_element_type.10
  108.3 12.3 %all-to-all-start.3 = ((f16[16,32,512]{2,1,0:T(8,128)(2,1)}), f16[16,32,512]{2,1,0:T(8,128)(2,1)}, u32[]{:S(2)}, u32[]{:S(2)}) async-start(f16[16,32,512]{2,1,0:T(8,128)(2,1)} %bitcast.7), calls=%async_computation.3 | async-start | bytes 1048576 | tf_op jit(solution)/shard_map/all_to_all | solution.py:277
  120.6 29.3 %all-to-all-done.3 = f16[16,32,512]{2,1,0:T(8,128)(2,1)} async-done(((f16[16,32,512]{2,1,0:T(8,128)(2,1)}), f16[16,32,512]{2,1,0:T(8,128)(2,1)}, u32[]{:S(2)}, u32[]{:S(2)}) %all-to-all-start.3) | async-done | bytes 524320 | tf_op jit(solution)/shard_map/all_to_all | solution.py:277
  150.0 1.2 convert_element_type.11.nodes_ref
  151.1 2.2 %shard_map.57 = f32[8,4,128]{2,1,0:T(4,128)} custom-call(s32[1]{0:T(128)} %bitcast.1.node_ref, f32[512,512]{1,0:T(8,128)S(1)} %bitcast.10, f32[8,128]{1,0:T(8,128)S(1)} %get-tuple-element.13.inverse_ref), custom_call_target="tpu_custom_call" | custom-call | flops 1073741824 | bytes 1048576 | tf_op jit(solution)/shard_map/pallas_call | solution.py:279
  153.3 7.8 %all-to-all-start.4 = ((f32[8,4,128]{2,1,0:T(4,128)}), f32[8,4,128]{2,1,0:T(4,128)S(1)}, u32[]{:S(2)}, u32[]{:S(2)}) async-start(f32[8,4,128]{2,1,0:T(4,128)} %shard_map.57), calls=%async_computation.4 | async-start | bytes 32768 | tf_op jit(solution)/shard_map/all_to_all | solution.py:286
  161.1 0.0 copy-done
  161.1 3.8 %fusion = f32[512,512]{1,0:T(8,128)} fusion(bf16[2048,512]{1,0:T(8,128)(2,1)S(1)} %copy-done, bf16[512,2048]{1,0:T(8,128)(2,1)} %pre_ref.1), kind=kOutput, calls=%fused_computation | convolution fusion | flops 1074790400 | bytes 5242880 | tf_op jit(solution)/shard_map/dot_general | solution.py:241
  165.0 0.8 all-to-all-done.4.sums_ref
  165.8 4.8 %all-to-all-start = ((f32[8,64,512]{2,1,0:T(8,128)}), f32[8,64,512]{2,1,0:T(8,128)}, u32[]{:S(2)}, u32[]{:S(2)}) async-start(f32[8,64,512]{2,1,0:T(8,128)} %bitcast.11), calls=%async_computation | async-start | bytes 2097152 | tf_op jit(solution)/shard_map/all_to_all | solution.py:243
  170.6 0.7 shard_map.58
  171.3 14.6 %all-to-all-done = f32[8,64,512]{2,1,0:T(8,128)} async-done(((f32[8,64,512]{2,1,0:T(8,128)}), f32[8,64,512]{2,1,0:T(8,128)}, u32[]{:S(2)}, u32[]{:S(2)}) %all-to-all-start) | async-done | bytes 1048608 | tf_op jit(solution)/shard_map/all_to_all | solution.py:243
  185.8 5.6 %all-to-all-start.5 = ((f32[64,4,128]{2,1,0:T(4,128)}), f32[64,4,128]{2,1,0:T(4,128)S(1)}, u32[]{:S(2)}, u32[]{:S(2)}) async-start(f32[64,4,128]{2,1,0:T(4,128)} %shard_map.58), calls=%async_computation.5 | async-start | bytes 262144 | tf_op jit(solution)/shard_map/all_to_all | solution.py:289
  191.4 1.9 reduce_sum.9
  193.4 12.1 %all-to-all-done.5.sums_ref = f32[64,4,128]{2,1,0:T(4,128)S(1)} async-done(((f32[64,4,128]{2,1,0:T(4,128)}), f32[64,4,128]{2,1,0:T(4,128)S(1)}, u32[]{:S(2)}, u32[]{:S(2)}) %all-to-all-start.5) | async-done | bytes 131104 | tf_op jit(solution)/shard_map/all_to_all | solution.py:289
  205.5 1.5 shard_map.59
Async XLA Ops:
  0.6 160.5 %copy-start = (bf16[2048,512]{1,0:T(8,128)(2,1)S(1)}, bf16[2048,512]{1,0:T(8,128)(2,1)}, u32[]{:S(2)}) copy-start(bf16[2048,512]{1,0:T(8,128)(2,1)} %param.4) | copy-start | bytes 6291460
  0.6 11.4 %collective-permute-start = (bf16[64,512]{1,0:T(8,128)(2,1)}, bf16[64,512]{1,0:T(8,128)(2,1)S(1)}, u32[]{:S(2)}, u32[]{:S(2)}) collective-permute-start(bf16[64,512]{1,0:T(8,128)(2,1)} %param.5), channel_id=1, source_target_pairs={{0,8},{8,0},{16,24},{24,16},{1,9},{9,1},{17,25},{25,17},{2,10},{10... | collective-permute-start | bytes 196616 | tf_op jit(solution)/shard_map/ppermute | solution.py:227
  5.2 7.2 %collective-permute-start.1 = (bf16[64,512]{1,0:T(8,128)(2,1)}, bf16[64,512]{1,0:T(8,128)(2,1)S(1)}, u32[]{:S(2)}, u32[]{:S(2)}) collective-permute-start(bf16[64,512]{1,0:T(8,128)(2,1)} %param.5), channel_id=1, source_target_pairs={{0,16},{8,24},{16,0},{24,8},{1,17},{9,25},{17,1},{25,9},{2,18},{10... | collective-permute-start | bytes 196616 | tf_op jit(solution)/shard_map/ppermute | solution.py:227
  10.1 7.3 %collective-permute-start.2 = (bf16[64,512]{1,0:T(8,128)(2,1)}, bf16[64,512]{1,0:T(8,128)(2,1)S(1)}, u32[]{:S(2)}, u32[]{:S(2)}) collective-permute-start(bf16[64,512]{1,0:T(8,128)(2,1)} %param.5), channel_id=1, source_target_pairs={{0,24},{8,16},{16,8},{24,0},{1,25},{9,17},{17,9},{25,1},{2,26},{10... | collective-permute-start | bytes 196616 | tf_op jit(solution)/shard_map/ppermute | solution.py:227
  19.8 36.1 %all-to-all-start.1 = ((bf16[8,4,64,512]{3,2,1,0:T(8,128)(2,1)}), bf16[8,4,64,512]{3,2,1,0:T(8,128)(2,1)}, u32[]{:S(2)}, u32[]{:S(2)}) async-start(bf16[8,4,64,512]{3,2,1,0:T(8,128)(2,1)} %broadcast_in_dim.3), calls=%async_computation.1 | async-start | bytes 4194304 | tf_op jit(solution)/shard_map/all_to_all | solution.py:39
  26.9 1.6 copy-start.3
  30.8 24.3 %collective-permute-start.3 = (bf16[512,512]{1,0:T(8,128)(2,1)S(1)}, bf16[512,512]{1,0:T(8,128)(2,1)S(1)}, u32[]{:S(2)}, u32[]{:S(2)}) collective-permute-start(bf16[512,512]{1,0:T(8,128)(2,1)S(1)} %get-tuple-element.9), channel_id=1, source_target_pairs={{0,8},{8,0},{16,24},{24,16},{1,9},{9,1},{17,25},{25,17},{2,10},{10... | collective-permute-start | bytes 1572872 | tf_op jit(solution)/shard_map/ppermute | solution.py:227
  32.7 40.5 %collective-permute-start.4 = (bf16[512,512]{1,0:T(8,128)(2,1)}, bf16[512,512]{1,0:T(8,128)(2,1)}, u32[]{:S(2)}, u32[]{:S(2)}) collective-permute-start(bf16[512,512]{1,0:T(8,128)(2,1)} %get-tuple-element.10), channel_id=1, source_target_pairs={{0,16},{8,24},{16,0},{24,8},{1,17},{9,25},{17,1},{25,9},{2,18},{10... | collective-permute-start | bytes 1572872 | tf_op jit(solution)/shard_map/ppermute | solution.py:227
  38.4 37.0 %collective-permute-start.5 = (bf16[512,512]{1,0:T(8,128)(2,1)}, bf16[512,512]{1,0:T(8,128)(2,1)S(1)}, u32[]{:S(2)}, u32[]{:S(2)}) collective-permute-start(bf16[512,512]{1,0:T(8,128)(2,1)} %get-tuple-element.11), channel_id=1, source_target_pairs={{0,24},{8,16},{16,8},{24,0},{1,25},{9,17},{17,9},{25,1},{2,26},{10... | collective-permute-start | bytes 1572872 | tf_op jit(solution)/shard_map/ppermute | solution.py:227
  55.0 0.8 copy-start.1
  55.9 1.0 copy-start.2
  108.3 41.6 %all-to-all-start.3 = ((f16[16,32,512]{2,1,0:T(8,128)(2,1)}), f16[16,32,512]{2,1,0:T(8,128)(2,1)}, u32[]{:S(2)}, u32[]{:S(2)}) async-start(f16[16,32,512]{2,1,0:T(8,128)(2,1)} %bitcast.7), calls=%async_computation.3 | async-start | bytes 1048576 | tf_op jit(solution)/shard_map/all_to_all | solution.py:277
  153.3 12.5 %all-to-all-start.4 = ((f32[8,4,128]{2,1,0:T(4,128)}), f32[8,4,128]{2,1,0:T(4,128)S(1)}, u32[]{:S(2)}, u32[]{:S(2)}) async-start(f32[8,4,128]{2,1,0:T(4,128)} %shard_map.57), calls=%async_computation.4 | async-start | bytes 32768 | tf_op jit(solution)/shard_map/all_to_all | solution.py:286
  165.8 20.1 %all-to-all-start = ((f32[8,64,512]{2,1,0:T(8,128)}), f32[8,64,512]{2,1,0:T(8,128)}, u32[]{:S(2)}, u32[]{:S(2)}) async-start(f32[8,64,512]{2,1,0:T(8,128)} %bitcast.11), calls=%async_computation | async-start | bytes 2097152 | tf_op jit(solution)/shard_map/all_to_all | solution.py:243
  185.8 19.6 %all-to-all-start.5 = ((f32[64,4,128]{2,1,0:T(4,128)}), f32[64,4,128]{2,1,0:T(4,128)S(1)}, u32[]{:S(2)}, u32[]{:S(2)}) async-start(f32[64,4,128]{2,1,0:T(4,128)} %shard_map.58), calls=%async_computation.5 | async-start | bytes 262144 | tf_op jit(solution)/shard_map/all_to_all | solution.py:289

commit v2 on v1

--- a/solution.py
+++ b/solution.py
@@ -34,48 +34,110 @@
 
 
 def from_everyone(array, axes):
-    count = lax.axis_size(axes)
-    copies = jnp.broadcast_to(array, (count, *array.shape))
+    copies = jnp.broadcast_to(array, (lax.axis_size(axes), *array.shape))
     return lax.all_to_all(copies, axes, split_axis=0, concat_axis=0, tiled=True)
 
 
-def deal_kernel(me_ref, pre_ref, *out_refs):
-    me = me_ref[0]
-    width = 512
-    row = lax.broadcasted_iota(jnp.int32, (width, width), 0)
-    col = lax.broadcasted_iota(jnp.int32, (width, width), 1)
-    block = row >> 5
-    place = (((block & 3) ^ me) << 7) + ((block >> 2) << 5) + (row & 31)
-    deal = jnp.where(place == col, 1.0, 0.0).astype(bf16)
-    for group in range(pre_ref.shape[1] // width):
-        part = jnp.maximum(pre_ref[:, group * width : (group + 1) * width], jnp.zeros((), bf16))
-        dealt = jnp.dot(part, deal, preferred_element_type=f32).astype(bf16)
-        for k in range(LEAVES):
-            out_refs[k][:, group * 128 : (group + 1) * 128] = dealt[:, k * 128 : (k + 1) * 128]
-
-
-def leaf_kernel(which, act_ref, grads_ref, out_ref):
+def deal_kernel(me_ref, pre_ref, *refs):
+    out_refs, deal_ref = refs[:LEAVES], refs[LEAVES]
+    width = pre_ref.shape[1]
+
+    @pl.when(pl.program_id(0) == 0)
+    def _():
+        row = lax.broadcasted_iota(jnp.int32, (width, width), 0)
+        col = lax.broadcasted_iota(jnp.int32, (width, width), 1)
+        block = row >> 5
+        place = (((block & 3) ^ me_ref[0]) << 7) + ((block >> 2) << 5) + (row & 31)
+        deal_ref[...] = jnp.where(place == col, 1.0, 0.0).astype(bf16)
+
+    part = jnp.maximum(pre_ref[...], jnp.zeros((), bf16))
+    dealt = jnp.dot(part, deal_ref[...], preferred_element_type=f32).astype(bf16)
+    for k in range(LEAVES):
+        out_refs[k][...] = dealt[:, k * 128 : (k + 1) * 128]
+
+
+def deal(me, pre_act):
+    tokens, hidden = pre_act.shape
+    group = 512
+    return pl.pallas_call(
+        deal_kernel,
+        grid_spec=pltpu.PrefetchScalarGridSpec(
+            num_scalar_prefetch=1,
+            grid=(hidden // group,),
+            in_specs=[pl.BlockSpec((tokens, group), lambda g, me: (0, g))],
+            out_specs=[pl.BlockSpec((tokens, group // LEAVES), lambda g, me: (0, g))] * LEAVES,
+            scratch_shapes=[pltpu.VMEM((group, group), bf16)],
+        ),
+        out_shape=[jax.ShapeDtypeStruct((tokens, hidden // LEAVES), bf16)] * LEAVES,
+        compiler_params=pltpu.CompilerParams(vmem_limit_bytes=LIMIT),
+        cost_estimate=pl.CostEstimate(
+            flops=2 * tokens * hidden * group, bytes_accessed=4 * tokens * hidden, transcendentals=0
+        ),
+    )(me, pre_act)
+
+
+def leaf_of(act_ref, grads_ref):
     peers, _, rows, width = grads_ref.shape
-    out_grad = grads_ref[:, which].reshape(peers * rows, width)
-    out_ref[...] = lax.dot_general(
-        act_ref[...], out_grad, (((0,), (0,)), ((), ())), preferred_element_type=f32
-    )
+    out_grad = grads_ref[:, 0].reshape(peers * rows, width)
+    return lax.dot_general(act_ref[...], out_grad, (((0,), (0,)), ((), ())), preferred_element_type=f32)
+
+
+def leaf_kernel(me_ref, act_ref, grads_ref, out_ref):
+    out_ref[...] = leaf_of(act_ref, grads_ref)
+
+
+def with_leaf(kernel, k, me, act, grads, others, outs):
+    peers, _, shard, width = grads.shape
+    tokens, quarter = act.shape
+
+    def whole(shape):
+        return pl.BlockSpec(shape, lambda g, me: (0,) * len(shape))
+
+    return pl.pallas_call(
+        kernel,
+        grid_spec=pltpu.PrefetchScalarGridSpec(
+            num_scalar_prefetch=1,
+            grid=(1,),
+            in_specs=[
+                whole(act.shape),
+                pl.BlockSpec((peers, 1, shard, width), lambda g, me: (0, me[0] ^ k, 0, 0)),
+            ]
+            + [whole(other.shape) for other in others],
+            out_specs=[whole(out.shape) for out in outs],
+        ),
+        out_shape=outs,
+        compiler_params=pltpu.CompilerParams(vmem_limit_bytes=LIMIT),
+        cost_estimate=pl.CostEstimate(
+            flops=2 * tokens * quarter * width, bytes_accessed=4 * quarter * width, transcendentals=0
+        ),
+    )(me, act, grads, *others)
+
+
+def project_kernel(pre_ref, weight_ref, late_ref, out_ref):
+    act = jnp.maximum(pre_ref[...], jnp.zeros((), bf16))
+    out_ref[...] = jnp.dot(act, weight_ref[...], preferred_element_type=f32)
 
 
 def lanes_of(total):
     return total[:, :128] + total[:, 128:256] + total[:, 256:384] + total[:, 384:512]
 
 
-def first_gram_kernel(me_ref, *refs):
-    leaf_refs, out_ref, held = refs[:LEAVES], refs[LEAVES], refs[LEAVES + 1]
+def first_gram_kernel(order, me_ref, act_ref, grads_ref, *refs):
+    count = LEAVES - 1
+    other_refs, (leaf_ref, out_ref) = refs[:count], refs[count:]
+    leaf_ref[...] = leaf_of(act_ref, grads_ref)
+    held = dict(zip(order, (*other_refs, leaf_ref)))
     me = me_ref[0]
+    lane = lax.broadcasted_iota(jnp.int32, (1, 128), 1)
+    whole = jnp.zeros((1, 128), f32)
     for a in range(LEAVES):
         for b in range(a, LEAVES):
-            partial_sum = lanes_of(jnp.sum(leaf_refs[a][...] * leaf_refs[b][...], axis=0, keepdims=True))
-            held[pl.ds(LEAVES * (a ^ me) + (b ^ me), 1), :] = partial_sum
+            lanes = lanes_of(jnp.sum(held[a][...] * held[b][...], axis=0, keepdims=True))
+            value = jnp.sum(lanes, axis=1, keepdims=True)
+            here = lane == LEAVES * (a ^ me) + (b ^ me)
             if a != b:
-                held[pl.ds(LEAVES * (b ^ me) + (a ^ me), 1), :] = partial_sum
-    whole = held[...]
+                here = here | (lane == LEAVES * (b ^ me) + (a ^ me))
+            whole = jnp.where(here, value, whole)
     for copy in range(out_ref.shape[0]):
         out_ref[copy] = whole
 
@@ -108,9 +170,14 @@
 def first_merge_kernel(me_ref, sums_ref, *refs):
     leaf_refs, node_ref, inverse_ref = refs[:LEAVES], refs[LEAVES], refs[LEAVES + 1]
     me = me_ref[0]
-    total = jnp.sum(jnp.sum(sums_ref[...], axis=0), axis=1, keepdims=True)
+    total = jnp.sum(sums_ref[...], axis=0)
+    lane = lax.broadcasted_iota(jnp.int32, total.shape, 1)
     gram = [
-        [total[LEAVES * i + j : LEAVES * i + j + 1, :] for j in range(LEAVES)] for i in range(LEAVES)
+        [
+            jnp.sum(jnp.where(lane == LEAVES * i + j, total, 0.0), axis=1, keepdims=True)
+            for j in range(LEAVES)
+        ]
+        for i in range(LEAVES)
     ]
     coef = tree(gram, LEAVES)
     bound = sum(jnp.abs(coef[i]) * jnp.sqrt(gram[i][i]) for i in range(LEAVES))
@@ -127,7 +194,7 @@
     node_ref[...] = merged
 
 
-def second_gram_kernel(copies, share, node_ref, nodes_ref, inverse_ref, out_ref):
+def second_gram_kernel(copies, share, node_ref, nodes_ref, inverse_ref, late_ref, out_ref):
     node = node_ref[0]
     total, width = nodes_ref.shape
     rows = total // NODES
@@ -226,43 +293,27 @@
     def from_neighbour(value, apart):
         return lax.ppermute(value, "zl", [(i, i ^ apart) for i in range(LEAVES)])
 
-    grad_shards = [out_grad] + [from_neighbour(out_grad, k) for k in range(1, LEAVES)]
-    dealt = call(
-        deal_kernel,
-        [jax.ShapeDtypeStruct((tokens, quarter), bf16)] * LEAVES,
-        [SMEM, VMEM],
-        flops=2 * tokens * hidden * 512,
-        size=4 * tokens * hidden,
-    )(me, pre_act)
+    shards = from_everyone(out_grad, "zl")
+    grads = from_everyone(shards, mp)
+    dealt = deal(me, pre_act)
     acts = [dealt[0]] + [from_neighbour(dealt[k], k) for k in range(1, LEAVES)]
-    grads = from_everyone(jnp.stack(grad_shards), mp)
-
-    act = jnp.maximum(pre_act, jnp.zeros((), bf16))
-    partial_out = jnp.dot(act, out_weight, preferred_element_type=f32)
-    parts = partial_out.reshape(peers, tokens // peers, width)
-    arrived = lax.all_to_all(parts, mp, split_axis=0, concat_axis=0, tiled=True)
-    projected = arrived.sum(axis=0).astype(bf16)
 
     leaf_shape = jax.ShapeDtypeStruct((quarter, width), f32)
-    leaves = [
-        call(
-            functools.partial(leaf_kernel, k),
-            leaf_shape,
-            [VMEM, VMEM],
-            flops=2 * tokens * quarter * width,
-            size=4 * quarter * width,
-        )(acts[k], grads)
-        for k in range(LEAVES)
-    ]
+    order = (0, 1, 3, 2)
+    leaves = {}
+    for k in order[:-1]:
+        (leaves[k],) = with_leaf(leaf_kernel, k, me, acts[k], grads, [], [leaf_shape])
+    k = order[-1]
     group = ("zl", *mp)
-    sums = call(
-        first_gram_kernel,
-        jax.ShapeDtypeStruct((LEAVES * peers, 16, 128), f32),
-        [SMEM] + [VMEM] * LEAVES,
-        flops=20 * quarter * width,
-        size=16 * quarter * width,
-        scratch=[pltpu.VMEM((16, 128), f32)],
-    )(me, *leaves)
+    leaves[k], sums = with_leaf(
+        functools.partial(first_gram_kernel, order),
+        k,
+        me,
+        acts[k],
+        grads,
+        [leaves[other] for other in order[:-1]],
+        [leaf_shape, jax.ShapeDtypeStruct((LEAVES * peers, 1, 128), f32)],
+    )
     sums = lax.all_to_all(sums, group, split_axis=0, concat_axis=0, tiled=True)
     scaled, inverse = call(
         first_merge_kernel,
@@ -270,23 +321,31 @@
         [SMEM] + [VMEM] * (LEAVES + 1),
         flops=8 * quarter * width,
         size=20 * quarter * width,
-    )(me, sums, *leaves)
+    )(me, sums, *[leaves[k] for k in range(LEAVES)])
+
+    partial_out = call(
+        project_kernel,
+        jax.ShapeDtypeStruct((tokens, width), f32),
+        [VMEM, VMEM, pl.BlockSpec(memory_space=pl.ANY)],
+        flops=2 * tokens * hidden * width,
+        size=4 * tokens * hidden,
+    )(pre_act, out_weight, inverse)
+    projected = lax.psum_scatter(partial_out, mp, scatter_dimension=0, tiled=True).astype(bf16)
 
     rows = quarter // NODES
     sent = scaled.astype(jnp.float16).reshape(NODES, rows, width)
     nodes = lax.all_to_all(sent, hi, split_axis=0, concat_axis=0, tiled=True).astype(f32)
     share = 1.0 / (LEAVES * peers)
     sums = call(
-        functools.partial(second_gram_kernel, peers, share),
-        jax.ShapeDtypeStruct((peers, 4, 128), f32),
-        [SMEM, VMEM, VMEM],
+        functools.partial(second_gram_kernel, LEAVES * peers, share),
+        jax.ShapeDtypeStruct((LEAVES * peers, 4, 128), f32),
+        [SMEM, VMEM, VMEM, pl.BlockSpec(memory_space=pl.ANY)],
         flops=8 * quarter * quarter * width,
         size=4 * quarter * width,
-    )(node, nodes.reshape(quarter, width), inverse)
-    sums = lax.all_to_all(sums, mp, split_axis=0, concat_axis=0, tiled=True)
-    dp = ("y", "zh", "zl")
-    sums = call(pass_on_kernel, jax.ShapeDtypeStruct((lax.axis_size(dp), 4, 128), f32), [VMEM])(sums)
-    sums = lax.all_to_all(sums, dp, split_axis=0, concat_axis=0, tiled=True)
+    )(node, nodes.reshape(quarter, width), inverse, partial_out)
+    sums = lax.all_to_all(sums, group, split_axis=0, concat_axis=0, tiled=True)
+    sums = call(pass_on_kernel, jax.ShapeDtypeStruct((NODES, 4, 128), f32), [VMEM])(sums)
+    sums = lax.all_to_all(sums, hi, split_axis=0, concat_axis=0, tiled=True)
     combined = call(
         second_merge_kernel,
         jax.ShapeDtypeStruct((rows, width), f32),

time: 209 us -> 194 us (0.928)
  starting transfers between devices: 58.5 us -> 34.9 us
  blocking collectives: 26.3 us -> 42.3 us
  waiting for transfers between devices: 91 us -> 77 us
  between operations: 0.78 us -> 14.2 us
  matrix products: 3.82 us -> 0 us
  local copies, waits for them, and re-layouts: 5 us -> 7.46 us
  other arithmetic: 4.87 us -> 2.58 us
  Pallas kernels: 16.7 us -> 14.5 us
    all_to_all x3 -> x1, waiting for transfers between devices: 27.5 us -> 12.1 us  [local(): sums = lax.all_to_all(sums, hi, split_axis=0, concat_axis=0, tiled=True)]
    all_to_all x3 -> x1, starting transfers between devices: 18.2 us -> 3.5 us  [local(): sums = lax.all_to_all(sums, hi, split_axis=0, concat_axis=0, tiled=True)]
    ppermute x6 -> x3, starting transfers between devices: 20.9 us -> 8.36 us  [from_neighbour(): return lax.ppermute(value, 'zl', [(i, i ^ apart) for i in range(LEAVES)])]
    all_to_all x0 -> x1, blocking collectives: none -> 12.2 us  [from_everyone(): return lax.all_to_all(copies, axes, split_axis=0, concat_axis=0, tiled=True)]
    all_to_all x1, waiting for transfers between devices: 0.01 us -> 4.95 us  [from_everyone(): return lax.all_to_all(copies, axes, split_axis=0, concat_axis=0, tiled=True)]
    all_to_all x1, waiting for transfers between devices: 29.3 us -> 25.5 us  [local(): lax.all_to_all(sent, hi, split_axis=0, concat_axis=0, tiled=True)]
    dot_general x1 -> x0, matrix products: 3.82 us -> none  [local(): partial_out = jnp.dot(act, out_weight, preferred_element_type=f32)]
    all_to_all x1 -> x2, blocking collectives: 26.3 us -> 30.1 us  [local(): sums = lax.all_to_all(sums, group, split_axis=0, concat_axis=0, tiled=True)]
  transfers between devices with their start and end apart: 11 -> 7, of which waited for: 8 -> 6; matrix products, arithmetic and copies ran while one was open for 3% -> 1% of each run, Pallas kernels for 4% -> 5%
where the time goes in v2:
time: 194 us; the launch traced here: 193 us
  waiting for transfers between devices  77 us (40%)
  blocking collectives  42.3 us (22%)
  starting transfers between devices  34.9 us (18%)
  Pallas kernels  14.5 us (7%)
  between operations  14.2 us (7%)
  local copies, waits for them, and re-layouts  7.46 us (4%)
  other arithmetic  2.58 us (1%)
    ppermute x3, waiting for transfers between devices, from_neighbour(): return lax.ppermute(value, 'zl', [(i, i ^ apart) for i in range(LEAVES)])  34.5 us
    all_to_all x2, blocking collectives, local(): sums = lax.all_to_all(sums, group, split_axis=0, concat_axis=0, tiled=True)  30.1 us
    all_to_all x1, waiting for transfers between devices, local(): lax.all_to_all(sent, hi, split_axis=0, concat_axis=0, tiled=True)  25.5 us
    all_to_all x1, starting transfers between devices, local(): lax.all_to_all(sent, hi, split_axis=0, concat_axis=0, tiled=True)  14.8 us
    all_to_all x1, blocking collectives, from_everyone(): return lax.all_to_all(copies, axes, split_axis=0, concat_axis=0, tiled=True)  12.2 us
    all_to_all x1, waiting for transfers between devices, local(): sums = lax.all_to_all(sums, hi, split_axis=0, concat_axis=0, tiled=True)  12.1 us
    ppermute x3, starting transfers between devices, from_neighbour(): return lax.ppermute(value, 'zl', [(i, i ^ apart) for i in range(LEAVES)])  8.36 us
    all_to_all x1, starting transfers between devices, from_everyone(): return lax.all_to_all(copies, axes, split_axis=0, concat_axis=0, tiled=True)  8.14 us
  transfers between devices with their start and end apart: 7, of which 6 were waited for; matrix products, arithmetic and copies ran while one was open for 1% of the time, Pallas kernels for 5%

profile of v2, /device:TPU:1, one launch (start us, length us, event | category | flops | bytes accessed | tf_op | source)
XLA Modules:
  0.0 192.9 jit_solution(502192338392013236)
XLA Ops:
  7.2 0.9 broadcast_in_dim.6
  8.0 12.2 %all_to_all.30 = bf16[4,64,512]{2,1,0:T(8,128)(2,1)S(1)} all-to-all(bf16[4,64,512]{2,1,0:T(8,128)(2,1)S(1)} %broadcast_in_dim.6), channel_id=1, replica_groups=mesh['y'=4,'zh'=4,'zl'=4,'x'=4,'c'=2] {'zl'}, dimensions={0} | all-to-all | bytes 524288 | tf_op jit(solution)/shard_map/all_to_all | solution.py:38
  20.2 1.6 broadcast_in_dim.7
  21.8 8.1 %all-to-all-start.1 = ((bf16[8,4,64,512]{3,2,1,0:T(8,128)(2,1)}), bf16[8,4,64,512]{3,2,1,0:T(8,128)(2,1)S(1)}, u32[]{:S(2)}, u32[]{:S(2)}) async-start(bf16[8,4,64,512]{3,2,1,0:T(8,128)(2,1)} %broadcast_in_dim.7), calls=%async_computation.1 | async-start | bytes 4194304 | tf_op jit(solution)/shard_map/all_to_all | solution.py:38
  30.0 0.0 copy-start.1
  30.0 1.6 copy-done.1
  31.6 3.2 %shard_map.50 = (bf16[512,512]{1,0:T(8,128)(2,1)S(1)}, bf16[512,512]{1,0:T(8,128)(2,1)S(1)}, bf16[512,512]{1,0:T(8,128)(2,1)}, bf16[512,512]{1,0:T(8,128)(2,1)}) custom-call(s32[1]{0:T(128)} %bitcast.me_ref, bf16[512,2048]{1,0:T(8,128)(2,1)S(1)} %copy-done.1), custom_call_target="tpu_custom_call" | custom-call | flops 1073741824 | bytes 4194304 | tf_op jit(solution)/shard_map/pallas_call | solution.py:62
  34.8 2.3 %collective-permute-start.1 = (bf16[512,512]{1,0:T(8,128)(2,1)S(1)}, bf16[512,512]{1,0:T(8,128)(2,1)S(1)}, u32[]{:S(2)}, u32[]{:S(2)}) collective-permute-start(bf16[512,512]{1,0:T(8,128)(2,1)S(1)} %get-tuple-element.12), channel_id=1, source_target_pairs={{0,8},{8,0},{16,24},{24,16},{1,9},{9,1},{17,25},{25,17},{2,10},{10... | collective-permute-start | bytes 1572872 | tf_op jit(solution)/shard_map/ppermute | solution.py:294
  37.1 2.7 %collective-permute-start.2 = (bf16[512,512]{1,0:T(8,128)(2,1)}, bf16[512,512]{1,0:T(8,128)(2,1)}, u32[]{:S(2)}, u32[]{:S(2)}) collective-permute-start(bf16[512,512]{1,0:T(8,128)(2,1)} %get-tuple-element.13), channel_id=1, source_target_pairs={{0,24},{8,16},{16,8},{24,0},{1,25},{9,17},{17,9},{25,1},{2,26},{10... | collective-permute-start | bytes 1572872 | tf_op jit(solution)/shard_map/ppermute | solution.py:294
  39.9 3.3 %collective-permute-start = (bf16[512,512]{1,0:T(8,128)(2,1)}, bf16[512,512]{1,0:T(8,128)(2,1)S(1)}, u32[]{:S(2)}, u32[]{:S(2)}) collective-permute-start(bf16[512,512]{1,0:T(8,128)(2,1)} %get-tuple-element.10), channel_id=1, source_target_pairs={{0,16},{8,24},{16,0},{24,8},{1,17},{9,25},{17,1},{25,9},{2,18},{10... | collective-permute-start | bytes 1572872 | tf_op jit(solution)/shard_map/ppermute | solution.py:294
  43.2 7.4 %collective-permute-done.1.act_ref = bf16[512,512]{1,0:T(8,128)(2,1)S(1)} collective-permute-done((bf16[512,512]{1,0:T(8,128)(2,1)S(1)}, bf16[512,512]{1,0:T(8,128)(2,1)S(1)}, u32[]{:S(2)}, u32[]{:S(2)}) %collective-permute-start.1) | collective-permute-done | bytes 524320 | tf_op jit(solution)/shard_map/ppermute | solution.py:294
  50.6 0.0 copy-start.4
  50.6 0.8 copy-done.4
  51.4 5.0 %all-to-all-done.1.grads_ref = bf16[8,4,64,512]{3,2,1,0:T(8,128)(2,1)S(1)} async-done(((bf16[8,4,64,512]{3,2,1,0:T(8,128)(2,1)}), bf16[8,4,64,512]{3,2,1,0:T(8,128)(2,1)S(1)}, u32[]{:S(2)}, u32[]{:S(2)}) %all-to-all-start.1) | async-done | bytes 2097184 | tf_op jit(solution)/shard_map/all_to_all | solution.py:38
  56.3 0.0 copy-start.5
  56.3 1.0 copy-done.5
  57.3 0.0 copy-start
  57.4 0.5 shard_map.52.refs_1_
  57.8 3.5 %collective-permute-done.2.act_ref = bf16[512,512]{1,0:T(8,128)(2,1)} collective-permute-done((bf16[512,512]{1,0:T(8,128)(2,1)}, bf16[512,512]{1,0:T(8,128)(2,1)}, u32[]{:S(2)}, u32[]{:S(2)}) %collective-permute-start.2) | collective-permute-done | bytes 524320 | tf_op jit(solution)/shard_map/ppermute | solution.py:294
  61.3 1.5 shard_map.53.refs_2_.refs_3_
  62.8 0.0 copy-done
  62.8 0.5 shard_map.51.refs_0_
  63.3 23.6 %collective-permute-done.act_ref = bf16[512,512]{1,0:T(8,128)(2,1)S(1)} collective-permute-done((bf16[512,512]{1,0:T(8,128)(2,1)}, bf16[512,512]{1,0:T(8,128)(2,1)S(1)}, u32[]{:S(2)}, u32[]{:S(2)}) %collective-permute-start) | collective-permute-done | bytes 524320 | tf_op jit(solution)/shard_map/ppermute | solution.py:294
  86.9 2.2 %shard_map.54 = (f32[512,512]{1,0:T(8,128)S(1)}, f32[32,1,128]{2,1,0:T(1,128)S(1)}) custom-call(s32[1]{0:T(128)} %bitcast.me_ref, bf16[512,512]{1,0:T(8,128)(2,1)S(1)} %collective-permute-done.act_ref, bf16[8,4,64,512]{3,2,1,0:T(8,128)(2,1)} %copy-done, f32[512,512]{1,0:T(8,128)S(1)} %shard_map.51.refs_0_, f32[512,512]{1,0:T(8,128)S(1)} %shard_map.52.refs_1_, ...), custom_call_target="tpu_custom_call" | custom-call | flops 268435456 | bytes 1048576 | tf_op jit(solution)/shard_map/pallas_call | solution.py:96
  89.2 13.7 %all_to_all.31.sums_ref = f32[32,1,128]{2,1,0:T(1,128)S(1)} all-to-all(f32[32,1,128]{2,1,0:T(1,128)S(1)} %get-tuple-element.14), channel_id=1, replica_groups=mesh['y'=4,'zh'=4,'zl'=4,'x'=4,'c'=2] {'zl','x','c'}, dimensions={0} | all-to-all | bytes 32768 | tf_op jit(solution)/shard_map/all_to_all | solution.py:317
  102.9 0.7 shard_map.55
  103.6 0.0 copy-start.2
  103.6 0.9 convert_element_type.10
  104.5 14.8 %all-to-all-start.3 = ((f16[16,32,512]{2,1,0:T(8,128)(2,1)}), f16[16,32,512]{2,1,0:T(8,128)(2,1)S(1)}, u32[]{:S(2)}, u32[]{:S(2)}) async-start(f16[16,32,512]{2,1,0:T(8,128)(2,1)} %bitcast.2), calls=%async_computation.4 | async-start | bytes 1048576 | tf_op jit(solution)/shard_map/all_to_all | solution.py:337
  119.4 0.0 reduce-scatter.2.cloned.1.call-start
  119.4 0.0 copy-done.2
  119.4 0.0 copy-start.3
  119.4 1.6 copy-done.3
  121.0 2.2 %shard_map.56.late_ref = f32[512,512]{1,0:T(8,128)} custom-call(bf16[512,2048]{1,0:T(8,128)(2,1)S(1)} %copy-done.2, bf16[2048,512]{1,0:T(8,128)(2,1)S(1)} %copy-done.3, f32[8,128]{1,0:T(8,128)S(1)} %get-tuple-element.16.late_ref.inverse_ref), custom_call_target="tpu_custom_call" | custom-call | flops 1073741824 | bytes 4194304 | tf_op jit(solution)/shard_map/pallas_call | solution.py:326
  123.3 0.0 reduce-scatter.2.cloned.1.call-update
  123.3 25.5 %all-to-all-done.3 = f16[16,32,512]{2,1,0:T(8,128)(2,1)S(1)} async-done(((f16[16,32,512]{2,1,0:T(8,128)(2,1)}), f16[16,32,512]{2,1,0:T(8,128)(2,1)S(1)}, u32[]{:S(2)}, u32[]{:S(2)}) %all-to-all-start.3) | async-done | bytes 524320 | tf_op jit(solution)/shard_map/all_to_all | solution.py:337
  148.8 0.1 convert_element_type.11.nodes_ref
  148.9 1.6 shard_map.57
  150.5 16.3 %all_to_all.32.sums_ref = f32[32,4,128]{2,1,0:T(4,128)S(1)} all-to-all(f32[32,4,128]{2,1,0:T(4,128)S(1)} %shard_map.57), channel_id=1, replica_groups=mesh['y'=4,'zh'=4,'zl'=4,'x'=4,'c'=2] {'zl','x','c'}, dimensions={0} | all-to-all | bytes 131072 | tf_op jit(solution)/shard_map/all_to_all | solution.py:346
  166.8 0.7 shard_map.58
  167.5 3.5 %all-to-all-start.5 = ((f32[16,4,128]{2,1,0:T(4,128)}), f32[16,4,128]{2,1,0:T(4,128)S(1)}, u32[]{:S(2)}, u32[]{:S(2)}) async-start(f32[16,4,128]{2,1,0:T(4,128)} %shard_map.58), calls=%async_computation.6 | async-start | bytes 65536 | tf_op jit(solution)/shard_map/all_to_all | solution.py:348
  171.0 0.0 reduce-scatter.2.cloned.1.call-done
  171.0 1.5 convert_element_type.9
  172.5 12.1 %all-to-all-done.5.sums_ref = f32[16,4,128]{2,1,0:T(4,128)S(1)} async-done(((f32[16,4,128]{2,1,0:T(4,128)}), f32[16,4,128]{2,1,0:T(4,128)S(1)}, u32[]{:S(2)}, u32[]{:S(2)}) %all-to-all-start.5) | async-done | bytes 32800 | tf_op jit(solution)/shard_map/all_to_all | solution.py:348
  184.6 1.4 shard_map.59
Async XLA Ops:
  21.8 34.5 %all-to-all-start.1 = ((bf16[8,4,64,512]{3,2,1,0:T(8,128)(2,1)}), bf16[8,4,64,512]{3,2,1,0:T(8,128)(2,1)S(1)}, u32[]{:S(2)}, u32[]{:S(2)}) async-start(bf16[8,4,64,512]{3,2,1,0:T(8,128)(2,1)} %broadcast_in_dim.7), calls=%async_computation.1 | async-start | bytes 4194304 | tf_op jit(solution)/shard_map/all_to_all | solution.py:38
  30.0 1.6 copy-start.1
  34.8 15.7 %collective-permute-start.1 = (bf16[512,512]{1,0:T(8,128)(2,1)S(1)}, bf16[512,512]{1,0:T(8,128)(2,1)S(1)}, u32[]{:S(2)}, u32[]{:S(2)}) collective-permute-start(bf16[512,512]{1,0:T(8,128)(2,1)S(1)} %get-tuple-element.12), channel_id=1, source_target_pairs={{0,8},{8,0},{16,24},{24,16},{1,9},{9,1},{17,25},{25,17},{2,10},{10... | collective-permute-start | bytes 1572872 | tf_op jit(solution)/shard_map/ppermute | solution.py:294
  37.1 24.2 %collective-permute-start.2 = (bf16[512,512]{1,0:T(8,128)(2,1)}, bf16[512,512]{1,0:T(8,128)(2,1)}, u32[]{:S(2)}, u32[]{:S(2)}) collective-permute-start(bf16[512,512]{1,0:T(8,128)(2,1)} %get-tuple-element.13), channel_id=1, source_target_pairs={{0,24},{8,16},{16,8},{24,0},{1,25},{9,17},{17,9},{25,1},{2,26},{10... | collective-permute-start | bytes 1572872 | tf_op jit(solution)/shard_map/ppermute | solution.py:294
  39.9 47.1 %collective-permute-start = (bf16[512,512]{1,0:T(8,128)(2,1)}, bf16[512,512]{1,0:T(8,128)(2,1)S(1)}, u32[]{:S(2)}, u32[]{:S(2)}) collective-permute-start(bf16[512,512]{1,0:T(8,128)(2,1)} %get-tuple-element.10), channel_id=1, source_target_pairs={{0,16},{8,24},{16,0},{24,8},{1,17},{9,25},{17,1},{25,9},{2,18},{10... | collective-permute-start | bytes 1572872 | tf_op jit(solution)/shard_map/ppermute | solution.py:294
  50.6 0.8 copy-start.4
  56.3 1.0 copy-start.5
  57.3 5.5 %copy-start = (bf16[8,4,64,512]{3,2,1,0:T(8,128)(2,1)}, bf16[8,4,64,512]{3,2,1,0:T(8,128)(2,1)S(1)}, u32[]{:S(2)}) copy-start(bf16[8,4,64,512]{3,2,1,0:T(8,128)(2,1)S(1)} %all-to-all-done.1.grads_ref) | copy-start | bytes 6291460
  103.6 15.8 %copy-start.2 = (bf16[512,2048]{1,0:T(8,128)(2,1)S(1)}, bf16[512,2048]{1,0:T(8,128)(2,1)}, u32[]{:S(2)}) copy-start(bf16[512,2048]{1,0:T(8,128)(2,1)} %pre_ref.3) | copy-start | bytes 6291460
  104.5 44.2 %all-to-all-start.3 = ((f16[16,32,512]{2,1,0:T(8,128)(2,1)}), f16[16,32,512]{2,1,0:T(8,128)(2,1)S(1)}, u32[]{:S(2)}, u32[]{:S(2)}) async-start(f16[16,32,512]{2,1,0:T(8,128)(2,1)} %bitcast.2), calls=%async_computation.4 | async-start | bytes 1048576 | tf_op jit(solution)/shard_map/all_to_all | solution.py:337
  119.4 51.6 %reduce-scatter.2.cloned.1.call-start = ((), (), s32[]{:S(2)}) async-start(), calls=%async_computation.7 | async-start | bytes 1179648 | tf_op jit(solution)/shard_map/reduce_scatter | solution.py:333
  119.4 1.6 copy-start.3
  167.5 17.2 %all-to-all-start.5 = ((f32[16,4,128]{2,1,0:T(4,128)}), f32[16,4,128]{2,1,0:T(4,128)S(1)}, u32[]{:S(2)}, u32[]{:S(2)}) async-start(f32[16,4,128]{2,1,0:T(4,128)} %shard_map.58), calls=%async_computation.6 | async-start | bytes 65536 | tf_op jit(solution)/shard_map/all_to_all | solution.py:348
Sparse Core Ops, SparseCore 0:
  123.4 37.6 reduce-scatter.1

commit v3 on v2

--- a/solution.py
+++ b/solution.py
@@ -10,7 +10,7 @@
 epsilon = 1e-06
 LEAVES = 4
 NODES = 16
-LIMIT = 64 * 1024 * 1024 * 3 // 4
+LIMIT = 24 * 1024 * 1024
 TOP = 16384.0
 FLOOR = 1e-15
 
@@ -18,6 +18,7 @@
 bf16 = jnp.bfloat16
 SMEM = pl.BlockSpec(memory_space=pltpu.SMEM)
 VMEM = pl.BlockSpec(memory_space=pltpu.VMEM)
+ANY = pl.BlockSpec(memory_space=pl.ANY)
 
 
 def call(kernel, out_shape, in_specs, flops=0, size=0, scratch=()):
@@ -76,58 +77,34 @@
     )(me, pre_act)
 
 
-def leaf_of(act_ref, grads_ref):
-    peers, _, rows, width = grads_ref.shape
-    out_grad = grads_ref[:, 0].reshape(peers * rows, width)
-    return lax.dot_general(act_ref[...], out_grad, (((0,), (0,)), ((), ())), preferred_element_type=f32)
-
-
-def leaf_kernel(me_ref, act_ref, grads_ref, out_ref):
-    out_ref[...] = leaf_of(act_ref, grads_ref)
-
-
-def with_leaf(kernel, k, me, act, grads, others, outs):
-    peers, _, shard, width = grads.shape
-    tokens, quarter = act.shape
-
-    def whole(shape):
-        return pl.BlockSpec(shape, lambda g, me: (0,) * len(shape))
-
-    return pl.pallas_call(
-        kernel,
-        grid_spec=pltpu.PrefetchScalarGridSpec(
-            num_scalar_prefetch=1,
-            grid=(1,),
-            in_specs=[
-                whole(act.shape),
-                pl.BlockSpec((peers, 1, shard, width), lambda g, me: (0, me[0] ^ k, 0, 0)),
-            ]
-            + [whole(other.shape) for other in others],
-            out_specs=[whole(out.shape) for out in outs],
-        ),
-        out_shape=outs,
-        compiler_params=pltpu.CompilerParams(vmem_limit_bytes=LIMIT),
-        cost_estimate=pl.CostEstimate(
-            flops=2 * tokens * quarter * width, bytes_accessed=4 * quarter * width, transcendentals=0
-        ),
-    )(me, act, grads, *others)
-
-
-def project_kernel(pre_ref, weight_ref, late_ref, out_ref):
+def arrived_kernel(*refs):
+    refs[-1][...] = jnp.zeros_like(refs[-1])
+
+
+def project_kernel(spot_ref, pre_ref, weight_ref, late_ref, mine_ref, theirs_ref, held_ref):
+    count = mine_ref.shape[0]
+    x, core = spot_ref[1], spot_ref[2]
     act = jnp.maximum(pre_ref[...], jnp.zeros((), bf16))
-    out_ref[...] = jnp.dot(act, weight_ref[...], preferred_element_type=f32)
+    total = jnp.dot(act, weight_ref[...], preferred_element_type=f32)
+    held_ref[...] = total.reshape(held_ref.shape)
+    for k in range(count):
+        mine_ref[k] = held_ref[x ^ k, core]
+        theirs_ref[k] = held_ref[x ^ k, 1 - core]
 
 
 def lanes_of(total):
     return total[:, :128] + total[:, 128:256] + total[:, 256:384] + total[:, 384:512]
 
 
-def first_gram_kernel(order, me_ref, act_ref, grads_ref, *refs):
-    count = LEAVES - 1
-    other_refs, (leaf_ref, out_ref) = refs[:count], refs[count:]
-    leaf_ref[...] = leaf_of(act_ref, grads_ref)
-    held = dict(zip(order, (*other_refs, leaf_ref)))
-    me = me_ref[0]
+def first_gram_kernel(spot_ref, grads_ref, late_ref, *refs):
+    act_refs, held, out_ref = refs[:LEAVES], refs[LEAVES:-1], refs[-1]
+    peers, _, rows, width = grads_ref.shape
+    me = spot_ref[0]
+    for k in range(LEAVES):
+        out_grad = grads_ref[:, me ^ k].reshape(peers * rows, width)
+        held[k][...] = lax.dot_general(
+            act_refs[k][...], out_grad, (((0,), (0,)), ((), ())), preferred_element_type=f32
+        )
     lane = lax.broadcasted_iota(jnp.int32, (1, 128), 1)
     whole = jnp.zeros((1, 128), f32)
     for a in range(LEAVES):
@@ -286,34 +263,36 @@
     mp = ("x", "c")
     hi = ("y", "zh")
     peers = lax.axis_size(mp)
-    me = lax.axis_index("zl").astype(jnp.int32).reshape(1)
+    spot = jnp.stack([lax.axis_index(axis) for axis in ("zl", "x", "c")]).astype(jnp.int32)
+    me = spot[:1]
     node = lax.axis_index(hi).astype(jnp.int32).reshape(1)
     quarter = hidden // LEAVES
-
-    def from_neighbour(value, apart):
-        return lax.ppermute(value, "zl", [(i, i ^ apart) for i in range(LEAVES)])
+    along = lax.axis_size("x")
+
+    def swapped(value, axis, apart):
+        return lax.ppermute(value, axis, [(i, i ^ apart) for i in range(lax.axis_size(axis))])
 
     shards = from_everyone(out_grad, "zl")
     grads = from_everyone(shards, mp)
     dealt = deal(me, pre_act)
-    acts = [dealt[0]] + [from_neighbour(dealt[k], k) for k in range(1, LEAVES)]
+    acts = [dealt[0]] + [swapped(dealt[k], "zl", k) for k in range(1, LEAVES)]
+    arrived = pl.pallas_call(
+        arrived_kernel,
+        out_shape=jax.ShapeDtypeStruct((8, 128), f32),
+        in_specs=[ANY] * (LEAVES - 1),
+        compiler_params=pltpu.CompilerParams(vmem_limit_bytes=1024 * 1024),
+        cost_estimate=pl.CostEstimate(flops=10**11, bytes_accessed=0, transcendentals=0),
+    )(*acts[1:])
 
     leaf_shape = jax.ShapeDtypeStruct((quarter, width), f32)
-    order = (0, 1, 3, 2)
-    leaves = {}
-    for k in order[:-1]:
-        (leaves[k],) = with_leaf(leaf_kernel, k, me, acts[k], grads, [], [leaf_shape])
-    k = order[-1]
     group = ("zl", *mp)
-    leaves[k], sums = with_leaf(
-        functools.partial(first_gram_kernel, order),
-        k,
-        me,
-        acts[k],
-        grads,
-        [leaves[other] for other in order[:-1]],
-        [leaf_shape, jax.ShapeDtypeStruct((LEAVES * peers, 1, 128), f32)],
-    )
+    *leaves, sums = call(
+        first_gram_kernel,
+        [leaf_shape] * LEAVES + [jax.ShapeDtypeStruct((LEAVES * peers, 1, 128), f32)],
+        [SMEM, VMEM, VMEM] + [VMEM] * LEAVES,
+        flops=2 * tokens * hidden * width,
+        size=16 * quarter * width,
+    )(spot, grads, arrived, *acts)
     sums = lax.all_to_all(sums, group, split_axis=0, concat_axis=0, tiled=True)
     scaled, inverse = call(
         first_merge_kernel,
@@ -321,16 +300,22 @@
         [SMEM] + [VMEM] * (LEAVES + 1),
         flops=8 * quarter * width,
         size=20 * quarter * width,
-    )(me, sums, *[leaves[k] for k in range(LEAVES)])
-
-    partial_out = call(
+    )(me, sums, *leaves)
+
+    half = jax.ShapeDtypeStruct((along, tokens // peers, width), f32)
+    mine, theirs = call(
         project_kernel,
-        jax.ShapeDtypeStruct((tokens, width), f32),
-        [VMEM, VMEM, pl.BlockSpec(memory_space=pl.ANY)],
+        [half, half],
+        [SMEM, VMEM, VMEM, VMEM],
         flops=2 * tokens * hidden * width,
         size=4 * tokens * hidden,
-    )(pre_act, out_weight, inverse)
-    projected = lax.psum_scatter(partial_out, mp, scatter_dimension=0, tiled=True).astype(bf16)
+        scratch=[pltpu.VMEM((along, 2, tokens // peers, width), f32)],
+    )(spot, pre_act, out_weight, inverse)
+    both = mine + swapped(theirs, "c", 1)
+    projected = both[0]
+    for k in range(1, along):
+        projected = projected + swapped(both[k], "x", k)
+    projected = projected.astype(bf16)
 
     rows = quarter // NODES
     sent = scaled.astype(jnp.float16).reshape(NODES, rows, width)
@@ -339,10 +324,10 @@
     sums = call(
         functools.partial(second_gram_kernel, LEAVES * peers, share),
         jax.ShapeDtypeStruct((LEAVES * peers, 4, 128), f32),
-        [SMEM, VMEM, VMEM, pl.BlockSpec(memory_space=pl.ANY)],
+        [SMEM, VMEM, VMEM, VMEM],
         flops=8 * quarter * quarter * width,
         size=4 * quarter * width,
-    )(node, nodes.reshape(quarter, width), inverse, partial_out)
+    )(node, nodes.reshape(quarter, width), inverse, projected)
     sums = lax.all_to_all(sums, group, split_axis=0, concat_axis=0, tiled=True)
     sums = call(pass_on_kernel, jax.ShapeDtypeStruct((NODES, 4, 128), f32), [VMEM])(sums)
     sums = lax.all_to_all(sums, hi, split_axis=0, concat_axis=0, tiled=True)

time: 194 us -> 166 us (0.86)
  waiting for transfers between devices: 77 us -> 40.3 us
  starting transfers between devices: 34.9 us -> 51 us
  between operations: 14.2 us -> 0.82 us
  blocking collectives: 42.3 us -> 54.3 us
  Pallas kernels: 14.5 us -> 11.7 us
    all_to_all x1, waiting for transfers between devices: 25.5 us -> 8.9 us  [local(): lax.all_to_all(sent, hi, split_axis=0, concat_axis=0, tiled=True)]
    ppermute x3 -> x7, starting transfers between devices: 8.36 us -> 21.1 us  [swapped(): lax.ppermute(value, axis, [(i, i ^ apart) for i in range(lax.axis_size(ax...]
    ppermute x3 -> x7, waiting for transfers between devices: 34.5 us -> 22 us  [swapped(): lax.ppermute(value, axis, [(i, i ^ apart) for i in range(lax.axis_size(ax...]
    all_to_all x1 -> x0, waiting for transfers between devices: 12.1 us -> none  [local(): sums = lax.all_to_all(sums, hi, split_axis=0, concat_axis=0, tiled=True)]
    all_to_all x2, blocking collectives: 30.1 us -> 37.9 us  [local(): sums = lax.all_to_all(sums, group, split_axis=0, concat_axis=0, tiled=True)]
    all_to_all x1 -> x2, starting transfers between devices: 8.14 us -> 14.6 us  [from_everyone(): return lax.all_to_all(copies, axes, split_axis=0, concat_axis=0, tiled=True)]
    all_to_all x1 -> x2, waiting for transfers between devices: 4.95 us -> 9.38 us  [from_everyone(): return lax.all_to_all(copies, axes, split_axis=0, concat_axis=0, tiled=True)]
    all_to_all x1, blocking collectives: 12.2 us -> 16.4 us  [local(): sums = lax.all_to_all(sums, hi, split_axis=0, concat_axis=0, tiled=True)]
  transfers between devices with their start and end apart: 7 -> 10, of which waited for: 6 -> 8; matrix products, arithmetic and copies ran while one was open for 1% -> 1% of each run, Pallas kernels for 5% -> 3%
where the time goes in v3:
time: 166 us
  blocking collectives  54.3 us (33%)
  starting transfers between devices  51 us (31%)
  waiting for transfers between devices  40.3 us (24%)
  Pallas kernels  11.7 us (7%)
  local copies, waits for them, and re-layouts  6.35 us (4%)
    all_to_all x2, blocking collectives, local(): sums = lax.all_to_all(sums, group, split_axis=0, concat_axis=0, tiled=True)  37.9 us
    ppermute x7, waiting for transfers between devices, swapped(): lax.ppermute(value, axis, [(i, i ^ apart) for i in range(lax.axis_size(ax...  22 us
    ppermute x7, starting transfers between devices, swapped(): lax.ppermute(value, axis, [(i, i ^ apart) for i in range(lax.axis_size(ax...  21.1 us
    all_to_all x1, blocking collectives, local(): sums = lax.all_to_all(sums, hi, split_axis=0, concat_axis=0, tiled=True)  16.4 us
    all_to_all x1, starting transfers between devices, local(): lax.all_to_all(sent, hi, split_axis=0, concat_axis=0, tiled=True)  15.3 us
    all_to_all x2, starting transfers between devices, from_everyone(): return lax.all_to_all(copies, axes, split_axis=0, concat_axis=0, tiled=True)  14.6 us
    all_to_all x2, waiting for transfers between devices, from_everyone(): return lax.all_to_all(copies, axes, split_axis=0, concat_axis=0, tiled=True)  9.38 us
    all_to_all x1, waiting for transfers between devices, local(): lax.all_to_all(sent, hi, split_axis=0, concat_axis=0, tiled=True)  8.9 us
  transfers between devices with their start and end apart: 10, of which 8 were waited for; matrix products, arithmetic and copies ran while one was open for 1% of the time, Pallas kernels for 3%

profile of v3, /device:TPU:1, one launch (start us, length us, event | category | flops | bytes accessed | tf_op | source)
XLA Modules:
  0.0 165.6 jit_solution(11480646750260184335)
XLA Ops:
  0.6 1.6 broadcast_in_dim.6
  2.2 6.4 %all-to-all-start = ((bf16[4,64,512]{2,1,0:T(8,128)(2,1)}), bf16[4,64,512]{2,1,0:T(8,128)(2,1)S(1)}, u32[]{:S(2)}, u32[]{:S(2)}) async-start(bf16[4,64,512]{2,1,0:T(8,128)(2,1)} %broadcast_in_dim.6), calls=%async_computation | async-start | bytes 524288 | tf_op jit(solution)/shard_map/all_to_all | solution.py:39
  8.6 0.0 copy-start
  8.6 1.6 copy-done
  10.2 3.3 %shard_map.50 = (bf16[512,512]{1,0:T(8,128)(2,1)S(1)}, bf16[512,512]{1,0:T(8,128)(2,1)}, bf16[512,512]{1,0:T(8,128)(2,1)}, bf16[512,512]{1,0:T(8,128)(2,1)}) custom-call(s32[1]{0:T(128)} %bitcast.me_ref, bf16[512,2048]{1,0:T(8,128)(2,1)S(1)} %copy-done), custom_call_target="tpu_custom_call" | custom-call | flops 1073741824 | bytes 4194304 | tf_op jit(solution)/shard_map/pallas_call | solution.py:63
  13.5 3.4 %collective-permute-start = (bf16[512,512]{1,0:T(8,128)(2,1)}, bf16[512,512]{1,0:T(8,128)(2,1)S(1)}, u32[]{:S(2)}, u32[]{:S(2)}) collective-permute-start(bf16[512,512]{1,0:T(8,128)(2,1)} %get-tuple-element.15), channel_id=1, source_target_pairs={{0,8},{8,0},{16,24},{24,16},{1,9},{9,1},{17,25},{25,17},{2,10},{10... | collective-permute-start | bytes 1572872 | tf_op jit(solution)/shard_map/ppermute | solution.py:273
  16.9 4.0 %collective-permute-start.1 = (bf16[512,512]{1,0:T(8,128)(2,1)}, bf16[512,512]{1,0:T(8,128)(2,1)}, u32[]{:S(2)}, u32[]{:S(2)}) collective-permute-start(bf16[512,512]{1,0:T(8,128)(2,1)} %get-tuple-element.16), channel_id=1, source_target_pairs={{0,16},{8,24},{16,0},{24,8},{1,17},{9,25},{17,1},{25,9},{2,18},{10... | collective-permute-start | bytes 1572872 | tf_op jit(solution)/shard_map/ppermute | solution.py:273
  20.9 1.9 %collective-permute-start.2 = (bf16[512,512]{1,0:T(8,128)(2,1)}, bf16[512,512]{1,0:T(8,128)(2,1)}, u32[]{:S(2)}, u32[]{:S(2)}) collective-permute-start(bf16[512,512]{1,0:T(8,128)(2,1)} %get-tuple-element.17), channel_id=1, source_target_pairs={{0,24},{8,16},{16,8},{24,0},{1,25},{9,17},{17,9},{25,1},{2,26},{10... | collective-permute-start | bytes 1572872 | tf_op jit(solution)/shard_map/ppermute | solution.py:273
  22.8 0.1 pad_add_fusion.spot_ref
  22.9 0.0 all-to-all-done
  22.9 1.6 broadcast_in_dim.7
  24.5 8.2 %all-to-all-start.1 = ((bf16[8,4,64,512]{3,2,1,0:T(8,128)(2,1)}), bf16[8,4,64,512]{3,2,1,0:T(8,128)(2,1)S(1)}, u32[]{:S(2)}, u32[]{:S(2)}) async-start(bf16[8,4,64,512]{3,2,1,0:T(8,128)(2,1)} %broadcast_in_dim.7), calls=%async_computation.1 | async-start | bytes 4194304 | tf_op jit(solution)/shard_map/all_to_all | solution.py:39
  32.6 0.7 collective-permute-done.refs_0_.refs_1_
  33.4 2.2 %collective-permute-done.1.refs_1_.refs_2_ = bf16[512,512]{1,0:T(8,128)(2,1)} collective-permute-done((bf16[512,512]{1,0:T(8,128)(2,1)}, bf16[512,512]{1,0:T(8,128)(2,1)}, u32[]{:S(2)}, u32[]{:S(2)}) %collective-permute-start.1) | collective-permute-done | bytes 524320 | tf_op jit(solution)/shard_map/ppermute | solution.py:273
  35.6 14.1 %collective-permute-done.2.refs_2_.refs_3_ = bf16[512,512]{1,0:T(8,128)(2,1)} collective-permute-done((bf16[512,512]{1,0:T(8,128)(2,1)}, bf16[512,512]{1,0:T(8,128)(2,1)}, u32[]{:S(2)}, u32[]{:S(2)}) %collective-permute-start.2) | collective-permute-done | bytes 524320 | tf_op jit(solution)/shard_map/ppermute | solution.py:273
  49.6 9.4 %all-to-all-done.1.grads_ref = bf16[8,4,64,512]{3,2,1,0:T(8,128)(2,1)S(1)} async-done(((bf16[8,4,64,512]{3,2,1,0:T(8,128)(2,1)}), bf16[8,4,64,512]{3,2,1,0:T(8,128)(2,1)S(1)}, u32[]{:S(2)}, u32[]{:S(2)}) %all-to-all-start.1) | async-done | bytes 2097184 | tf_op jit(solution)/shard_map/all_to_all | solution.py:39
  59.0 2.8 %shard_map.52 = (f32[512,512]{1,0:T(8,128)S(1)}, f32[512,512]{1,0:T(8,128)S(1)}, f32[512,512]{1,0:T(8,128)S(1)}, f32[512,512]{1,0:T(8,128)S(1)}, f32[32,1,128]{2,1,0:T(1,128)S(1)}) custom-call(s32[3]{0:T(128)S(1)} %pad_add_fusion.spot_ref, bf16[8,4,64,512]{3,2,1,0:T(8,128)(2,1)S(1)} %all-to-all-done.1.grads_ref, f32[8,128]{1,0:T(8,128)S(1)} %shard_map.51.late_ref, ...), custom_call_target="tpu_custom_call" | custom-call | flops 1073741824 | bytes 4194304 | tf_op jit(solution)/shard_map/pallas_call | solution.py:289
  61.8 21.5 %all_to_all.30.sums_ref = f32[32,1,128]{2,1,0:T(1,128)S(1)} all-to-all(f32[32,1,128]{2,1,0:T(1,128)S(1)} %get-tuple-element.19), channel_id=1, replica_groups=mesh['y'=4,'zh'=4,'zl'=4,'x'=4,'c'=2] {'zl','x','c'}, dimensions={0} | all-to-all | bytes 32768 | tf_op jit(solution)/shard_map/all_to_all | solution.py:296
  83.3 0.7 shard_map.53
  84.0 0.0 copy-start.1
  84.0 0.9 convert_element_type.10
  85.0 15.3 %all-to-all-start.3 = ((f16[16,32,512]{2,1,0:T(8,128)(2,1)}), f16[16,32,512]{2,1,0:T(8,128)(2,1)S(1)}, u32[]{:S(2)}, u32[]{:S(2)}) async-start(f16[16,32,512]{2,1,0:T(8,128)(2,1)} %bitcast.8), calls=%async_computation.3 | async-start | bytes 1048576 | tf_op jit(solution)/shard_map/all_to_all | solution.py:322
  100.3 0.0 copy-done.1
  100.3 0.0 copy-start.2
  100.3 1.6 copy-done.2
  101.9 1.9 %shard_map.54 = (f32[4,64,512]{2,1,0:T(8,128)S(1)}, f32[4,64,512]{2,1,0:T(8,128)S(1)}) custom-call(s32[3]{0:T(128)S(1)} %pad_add_fusion.spot_ref, bf16[512,2048]{1,0:T(8,128)(2,1)S(1)} %copy-done.1, bf16[2048,512]{1,0:T(8,128)(2,1)S(1)} %copy-done.2, f32[8,128]{1,0:T(8,128)S(1)} %get-tuple-element.24.late_ref.inverse_ref), custom_call_target="tpu_custom_call" | custom-call | flops 1073741824 | bytes 4194304 | tf_op jit(solution)/shard_map/pallas_call | solution.py:306
  103.7 2.8 %collective-permute-start.3 = (f32[4,64,512]{2,1,0:T(8,128)S(1)}, f32[4,64,512]{2,1,0:T(8,128)S(1)}, u32[]{:S(2)}, u32[]{:S(2)}) collective-permute-start(f32[4,64,512]{2,1,0:T(8,128)S(1)} %get-tuple-element.26), channel_id=1, source_target_pairs={{0,1},{1,0},{2,3},{3,2},{4,5},{5,4},{6,7},{7,6},{8,9},{9,8},{10,11... | collective-permute-start | bytes 1572872 | tf_op jit(solution)/shard_map/ppermute | solution.py:273
  106.6 1.5 collective-permute-done.3
  108.1 0.1 add.15
  108.2 2.2 %collective-permute-start.4 = (f32[64,512]{1,0:T(8,128)S(1)}, f32[64,512]{1,0:T(8,128)S(1)}, u32[]{:S(2)}, u32[]{:S(2)}) collective-permute-start(f32[64,512]{1,0:T(8,128)S(1)} %get-tuple-element.28), channel_id=1, source_target_pairs={{0,2},{2,0},{4,6},{6,4},{1,3},{3,1},{5,7},{7,5},{8,10},{10,8},{12,... | collective-permute-start | bytes 393224 | tf_op jit(solution)/shard_map/ppermute | solution.py:273
  110.4 2.8 %collective-permute-start.6 = (f32[64,512]{1,0:T(8,128)S(1)}, f32[64,512]{1,0:T(8,128)S(1)}, u32[]{:S(2)}, u32[]{:S(2)}) collective-permute-start(f32[64,512]{1,0:T(8,128)S(1)} %get-tuple-element.29), channel_id=1, source_target_pairs={{0,6},{2,4},{4,2},{6,0},{1,7},{3,5},{5,3},{7,1},{8,14},{10,12},{12... | collective-permute-start | bytes 393224 | tf_op jit(solution)/shard_map/ppermute | solution.py:273
  113.2 4.0 %collective-permute-start.5 = (f32[64,512]{1,0:T(8,128)S(1)}, f32[64,512]{1,0:T(8,128)S(1)}, u32[]{:S(2)}, u32[]{:S(2)}) collective-permute-start(f32[64,512]{1,0:T(8,128)S(1)} %get-tuple-element.30), channel_id=1, source_target_pairs={{0,4},{2,6},{4,0},{6,2},{1,5},{3,7},{5,1},{7,3},{8,12},{10,14},{12... | collective-permute-start | bytes 393224 | tf_op jit(solution)/shard_map/ppermute | solution.py:273
  117.2 0.0 collective-permute-done.4
  117.2 0.7 collective-permute-done.6
  117.9 2.8 %collective-permute-done.5 = f32[64,512]{1,0:T(8,128)S(1)} collective-permute-done((f32[64,512]{1,0:T(8,128)S(1)}, f32[64,512]{1,0:T(8,128)S(1)}, u32[]{:S(2)}, u32[]{:S(2)}) %collective-permute-start.5) | collective-permute-done | bytes 131104 | tf_op jit(solution)/shard_map/ppermute | solution.py:273
  120.7 0.0 copy-start.3
  120.8 8.9 %all-to-all-done.3 = f16[16,32,512]{2,1,0:T(8,128)(2,1)S(1)} async-done(((f16[16,32,512]{2,1,0:T(8,128)(2,1)}), f16[16,32,512]{2,1,0:T(8,128)(2,1)S(1)}, u32[]{:S(2)}, u32[]{:S(2)}) %all-to-all-start.3) | async-done | bytes 524320 | tf_op jit(solution)/shard_map/all_to_all | solution.py:322
  129.7 0.1 convert_element_type.11.nodes_ref
  129.8 1.6 shard_map.55
  131.4 0.0 copy-done.3
  131.4 16.3 %all_to_all.31.sums_ref = f32[32,4,128]{2,1,0:T(4,128)S(1)} all-to-all(f32[32,4,128]{2,1,0:T(4,128)S(1)} %shard_map.55), channel_id=1, replica_groups=mesh['y'=4,'zh'=4,'zl'=4,'x'=4,'c'=2] {'zl','x','c'}, dimensions={0} | all-to-all | bytes 131072 | tf_op jit(solution)/shard_map/all_to_all | solution.py:331
  147.8 16.4 %all_to_all.32.sums_ref = f32[16,4,128]{2,1,0:T(4,128)S(1)} all-to-all(f32[16,4,128]{2,1,0:T(4,128)S(1)} %shard_map.56), channel_id=1, replica_groups=mesh['y'=4,'zh'=4,'zl'=4,'x'=4,'c'=2] {'y','zh'}, dimensions={0} | all-to-all | bytes 65536 | tf_op jit(solution)/shard_map/all_to_all | solution.py:333
  164.2 1.4 shard_map.57
  (4 shorter events, 0.1 us)
Async XLA Ops:
  2.2 20.7 %all-to-all-start = ((bf16[4,64,512]{2,1,0:T(8,128)(2,1)}), bf16[4,64,512]{2,1,0:T(8,128)(2,1)S(1)}, u32[]{:S(2)}, u32[]{:S(2)}) async-start(bf16[4,64,512]{2,1,0:T(8,128)(2,1)} %broadcast_in_dim.6), calls=%async_computation | async-start | bytes 524288 | tf_op jit(solution)/shard_map/all_to_all | solution.py:39
  8.6 1.6 copy-start
  13.5 19.9 %collective-permute-start = (bf16[512,512]{1,0:T(8,128)(2,1)}, bf16[512,512]{1,0:T(8,128)(2,1)S(1)}, u32[]{:S(2)}, u32[]{:S(2)}) collective-permute-start(bf16[512,512]{1,0:T(8,128)(2,1)} %get-tuple-element.15), channel_id=1, source_target_pairs={{0,8},{8,0},{16,24},{24,16},{1,9},{9,1},{17,25},{25,17},{2,10},{10... | collective-permute-start | bytes 1572872 | tf_op jit(solution)/shard_map/ppermute | solution.py:273
  16.9 18.7 %collective-permute-start.1 = (bf16[512,512]{1,0:T(8,128)(2,1)}, bf16[512,512]{1,0:T(8,128)(2,1)}, u32[]{:S(2)}, u32[]{:S(2)}) collective-permute-start(bf16[512,512]{1,0:T(8,128)(2,1)} %get-tuple-element.16), channel_id=1, source_target_pairs={{0,16},{8,24},{16,0},{24,8},{1,17},{9,25},{17,1},{25,9},{2,18},{10... | collective-permute-start | bytes 1572872 | tf_op jit(solution)/shard_map/ppermute | solution.py:273
  20.9 28.8 %collective-permute-start.2 = (bf16[512,512]{1,0:T(8,128)(2,1)}, bf16[512,512]{1,0:T(8,128)(2,1)}, u32[]{:S(2)}, u32[]{:S(2)}) collective-permute-start(bf16[512,512]{1,0:T(8,128)(2,1)} %get-tuple-element.17), channel_id=1, source_target_pairs={{0,24},{8,16},{16,8},{24,0},{1,25},{9,17},{17,9},{25,1},{2,26},{10... | collective-permute-start | bytes 1572872 | tf_op jit(solution)/shard_map/ppermute | solution.py:273
  24.5 34.5 %all-to-all-start.1 = ((bf16[8,4,64,512]{3,2,1,0:T(8,128)(2,1)}), bf16[8,4,64,512]{3,2,1,0:T(8,128)(2,1)S(1)}, u32[]{:S(2)}, u32[]{:S(2)}) async-start(bf16[8,4,64,512]{3,2,1,0:T(8,128)(2,1)} %broadcast_in_dim.7), calls=%async_computation.1 | async-start | bytes 4194304 | tf_op jit(solution)/shard_map/all_to_all | solution.py:39
  84.0 16.2 %copy-start.1 = (bf16[512,2048]{1,0:T(8,128)(2,1)S(1)}, bf16[512,2048]{1,0:T(8,128)(2,1)}, u32[]{:S(2)}) copy-start(bf16[512,2048]{1,0:T(8,128)(2,1)} %pre_ref.3) | copy-start | bytes 6291460
  85.0 44.7 %all-to-all-start.3 = ((f16[16,32,512]{2,1,0:T(8,128)(2,1)}), f16[16,32,512]{2,1,0:T(8,128)(2,1)S(1)}, u32[]{:S(2)}, u32[]{:S(2)}) async-start(f16[16,32,512]{2,1,0:T(8,128)(2,1)} %bitcast.8), calls=%async_computation.3 | async-start | bytes 1048576 | tf_op jit(solution)/shard_map/all_to_all | solution.py:322
  100.3 1.6 copy-start.2
  103.7 4.4 %collective-permute-start.3 = (f32[4,64,512]{2,1,0:T(8,128)S(1)}, f32[4,64,512]{2,1,0:T(8,128)S(1)}, u32[]{:S(2)}, u32[]{:S(2)}) collective-permute-start(f32[4,64,512]{2,1,0:T(8,128)S(1)} %get-tuple-element.26), channel_id=1, source_target_pairs={{0,1},{1,0},{2,3},{3,2},{4,5},{5,4},{6,7},{7,6},{8,9},{9,8},{10,11... | collective-permute-start | bytes 1572872 | tf_op jit(solution)/shard_map/ppermute | solution.py:273
  108.2 9.0 %collective-permute-start.4 = (f32[64,512]{1,0:T(8,128)S(1)}, f32[64,512]{1,0:T(8,128)S(1)}, u32[]{:S(2)}, u32[]{:S(2)}) collective-permute-start(f32[64,512]{1,0:T(8,128)S(1)} %get-tuple-element.28), channel_id=1, source_target_pairs={{0,2},{2,0},{4,6},{6,4},{1,3},{3,1},{5,7},{7,5},{8,10},{10,8},{12,... | collective-permute-start | bytes 393224 | tf_op jit(solution)/shard_map/ppermute | solution.py:273
  110.4 7.5 %collective-permute-start.6 = (f32[64,512]{1,0:T(8,128)S(1)}, f32[64,512]{1,0:T(8,128)S(1)}, u32[]{:S(2)}, u32[]{:S(2)}) collective-permute-start(f32[64,512]{1,0:T(8,128)S(1)} %get-tuple-element.29), channel_id=1, source_target_pairs={{0,6},{2,4},{4,2},{6,0},{1,7},{3,5},{5,3},{7,1},{8,14},{10,12},{12... | collective-permute-start | bytes 393224 | tf_op jit(solution)/shard_map/ppermute | solution.py:273
  113.2 7.5 %collective-permute-start.5 = (f32[64,512]{1,0:T(8,128)S(1)}, f32[64,512]{1,0:T(8,128)S(1)}, u32[]{:S(2)}, u32[]{:S(2)}) collective-permute-start(f32[64,512]{1,0:T(8,128)S(1)} %get-tuple-element.30), channel_id=1, source_target_pairs={{0,4},{2,6},{4,0},{6,2},{1,5},{3,7},{5,1},{7,3},{8,12},{10,14},{12... | collective-permute-start | bytes 393224 | tf_op jit(solution)/shard_map/ppermute | solution.py:273
  120.7 10.6 %copy-start.3 = (bf16[64,512]{1,0:T(8,128)(2,1)}, bf16[64,512]{1,0:T(8,128)(2,1)S(1)}, u32[]{:S(2)}) copy-start(bf16[64,512]{1,0:T(8,128)(2,1)S(1)} %fusion.3.late_ref) | copy-start | bytes 196612

commit v4 on v3

--- a/solution.py
+++ b/solution.py
@@ -39,7 +39,7 @@
     return lax.all_to_all(copies, axes, split_axis=0, concat_axis=0, tiled=True)
 
 
-def deal_kernel(me_ref, pre_ref, *refs):
+def deal_kernel(me_ref, pre_ref, grad_ref, copies_ref, *refs):
     out_refs, deal_ref = refs[:LEAVES], refs[LEAVES]
     width = pre_ref.shape[1]
 
@@ -50,6 +50,8 @@
         block = row >> 5
         place = (((block & 3) ^ me_ref[0]) << 7) + ((block >> 2) << 5) + (row & 31)
         deal_ref[...] = jnp.where(place == col, 1.0, 0.0).astype(bf16)
+        for copy in range(LEAVES):
+            copies_ref[copy] = grad_ref[...]
 
     part = jnp.maximum(pre_ref[...], jnp.zeros((), bf16))
     dealt = jnp.dot(part, deal_ref[...], preferred_element_type=f32).astype(bf16)
@@ -57,24 +59,30 @@
         out_refs[k][...] = dealt[:, k * 128 : (k + 1) * 128]
 
 
-def deal(me, pre_act):
+def deal(me, pre_act, out_grad):
     tokens, hidden = pre_act.shape
+    shard, width = out_grad.shape
     group = 512
     return pl.pallas_call(
         deal_kernel,
         grid_spec=pltpu.PrefetchScalarGridSpec(
             num_scalar_prefetch=1,
             grid=(hidden // group,),
-            in_specs=[pl.BlockSpec((tokens, group), lambda g, me: (0, g))],
-            out_specs=[pl.BlockSpec((tokens, group // LEAVES), lambda g, me: (0, g))] * LEAVES,
+            in_specs=[
+                pl.BlockSpec((tokens, group), lambda g, me: (0, g)),
+                pl.BlockSpec((shard, width), lambda g, me: (0, 0)),
+            ],
+            out_specs=[pl.BlockSpec((LEAVES, shard, width), lambda g, me: (0, 0, 0))]
+            + [pl.BlockSpec((tokens, group // LEAVES), lambda g, me: (0, g))] * LEAVES,
             scratch_shapes=[pltpu.VMEM((group, group), bf16)],
         ),
-        out_shape=[jax.ShapeDtypeStruct((tokens, hidden // LEAVES), bf16)] * LEAVES,
-        compiler_params=pltpu.CompilerParams(vmem_limit_bytes=LIMIT),
+        out_shape=[jax.ShapeDtypeStruct((LEAVES, shard, width), bf16)]
+        + [jax.ShapeDtypeStruct((tokens, hidden // LEAVES), bf16)] * LEAVES,
+        compiler_params=pltpu.CompilerParams(vmem_limit_bytes=63 * 1024 * 1024),
         cost_estimate=pl.CostEstimate(
             flops=2 * tokens * hidden * group, bytes_accessed=4 * tokens * hidden, transcendentals=0
         ),
-    )(me, pre_act)
+    )(me, pre_act, out_grad)
 
 
 def arrived_kernel(*refs):
@@ -197,16 +205,11 @@
     lane = lax.broadcasted_iota(jnp.int32, (NODES, 128), 1)
     packed = jnp.where(lane // NODES == (place & 7), gram, 0.0)
     lane = lane[:1]
-    inverse = jnp.where(lane == node, inverse_ref[:1] * share, 0.0)
-    whole = jnp.concatenate(
-        [
-            jnp.sum(packed[:8], axis=0, keepdims=True),
-            jnp.sum(packed[8:], axis=0, keepdims=True),
-            inverse,
-            jnp.zeros_like(inverse),
-        ],
-        axis=0,
-    )
+    upper = jnp.sum(packed[:8], axis=0, keepdims=True)
+    lower = jnp.sum(packed[8:], axis=0, keepdims=True)
+    inverse = jnp.where(lane == (node & 7) + 2 * (node & 8), inverse_ref[:1] * share, 0.0)
+    lower = jnp.where((lane & (NODES - 1)) < 8, inverse, lower)
+    whole = jnp.concatenate([upper, lower], axis=0)
     for copy in range(copies):
         out_ref[copy] = whole
 
@@ -223,12 +226,26 @@
     lane = lax.broadcasted_iota(jnp.int32, (NODES, 128), 1)
     gram = jnp.where(place < 8, total[0:1], total[1:2])
     gram = jnp.where(lane // NODES == (place & 7), gram, 0.0)
-    inverse_row = jnp.where(lane[:1] < NODES, total[2:3], 0.0)
+    free = (lane & 8) == 0
+    gram = jnp.where((place >= 8) & free, 0.0, gram)
+    inverse_row = jnp.where((lane[:1] < NODES) & free[:1], total[1:2], 0.0)
+    second = jnp.where((lane[:1] >= NODES) & (lane[:1] < NODES + 8), total[1:2], 0.0)
+    inverse_row = inverse_row + pltpu.roll(second, 128 - 8, 1)
     for turn in (16, 32, 64):
         gram = gram + pltpu.roll(gram, turn, 1)
         inverse_row = inverse_row + pltpu.roll(inverse_row, turn, 1)
     other = lane & (NODES - 1)
     first = lane < NODES
+    corner = jnp.where((place < 8) & (other >= 8), gram, 0.0)
+    unit = jnp.where(place == other, 1.0, 0.0)
+    mirrored = lax.dot_general(
+        corner,
+        unit,
+        (((0,), (0,)), ((), ())),
+        preferred_element_type=f32,
+        precision=lax.Precision.HIGHEST,
+    )
+    gram = gram + mirrored[:NODES]
 
     def column(row):
         return jnp.sum(jnp.where(lane == place, row, 0.0), axis=1, keepdims=True)
@@ -272,17 +289,19 @@
     def swapped(value, axis, apart):
         return lax.ppermute(value, axis, [(i, i ^ apart) for i in range(lax.axis_size(axis))])
 
-    shards = from_everyone(out_grad, "zl")
+    copies, *dealt = deal(me, pre_act, out_grad)
+    acts = {0: dealt[0]}
+    for k in (3, 2, 1):
+        acts[k] = swapped(dealt[k], "zl", k)
+    shards = lax.all_to_all(copies, "zl", split_axis=0, concat_axis=0, tiled=True)
     grads = from_everyone(shards, mp)
-    dealt = deal(me, pre_act)
-    acts = [dealt[0]] + [swapped(dealt[k], "zl", k) for k in range(1, LEAVES)]
     arrived = pl.pallas_call(
         arrived_kernel,
         out_shape=jax.ShapeDtypeStruct((8, 128), f32),
         in_specs=[ANY] * (LEAVES - 1),
         compiler_params=pltpu.CompilerParams(vmem_limit_bytes=1024 * 1024),
         cost_estimate=pl.CostEstimate(flops=10**11, bytes_accessed=0, transcendentals=0),
-    )(*acts[1:])
+    )(acts[3], acts[2], acts[1])
 
     leaf_shape = jax.ShapeDtypeStruct((quarter, width), f32)
     group = ("zl", *mp)
@@ -292,7 +311,7 @@
         [SMEM, VMEM, VMEM] + [VMEM] * LEAVES,
         flops=2 * tokens * hidden * width,
         size=16 * quarter * width,
-    )(spot, grads, arrived, *acts)
+    )(spot, grads, arrived, *[acts[k] for k in range(LEAVES)])
     sums = lax.all_to_all(sums, group, split_axis=0, concat_axis=0, tiled=True)
     scaled, inverse = call(
         first_merge_kernel,
@@ -322,15 +341,16 @@
     nodes = lax.all_to_all(sent, hi, split_axis=0, concat_axis=0, tiled=True).astype(f32)
     share = 1.0 / (LEAVES * peers)
     sums = call(
-        functools.partial(second_gram_kernel, LEAVES * peers, share),
-        jax.ShapeDtypeStruct((LEAVES * peers, 4, 128), f32),
+        functools.partial(second_gram_kernel, peers, share),
+        jax.ShapeDtypeStruct((peers, 2, 128), f32),
         [SMEM, VMEM, VMEM, VMEM],
         flops=8 * quarter * quarter * width,
         size=4 * quarter * width,
     )(node, nodes.reshape(quarter, width), inverse, projected)
-    sums = lax.all_to_all(sums, group, split_axis=0, concat_axis=0, tiled=True)
-    sums = call(pass_on_kernel, jax.ShapeDtypeStruct((NODES, 4, 128), f32), [VMEM])(sums)
-    sums = lax.all_to_all(sums, hi, split_axis=0, concat_axis=0, tiled=True)
+    sums = lax.all_to_all(sums, mp, split_axis=0, concat_axis=0, tiled=True)
+    dp = ("y", "zh", "zl")
+    sums = call(pass_on_kernel, jax.ShapeDtypeStruct((LEAVES * NODES, 2, 128), f32), [VMEM])(sums)
+    sums = lax.all_to_all(sums, dp, split_axis=0, concat_axis=0, tiled=True)
     combined = call(
         second_merge_kernel,
         jax.ShapeDtypeStruct((rows, width), f32),

time: 166 us -> 172 us (1.036)
  starting transfers between devices: 51 us -> 70.8 us
  blocking collectives: 54.3 us -> 41.8 us
  local copies, waits for them, and re-layouts: 6.35 us -> 3.2 us
  Pallas kernels: 11.7 us -> 13.5 us
    all_to_all x2 -> x1, blocking collectives: 37.9 us -> 11.5 us  [local(): sums = lax.all_to_all(sums, group, split_axis=0, concat_axis=0, tiled=True)]
    all_to_all x1 -> x2, blocking collectives: 16.4 us -> 30.3 us  [the longest x1 21.7 us: local(): sums = lax.all_to_all(sums, dp, split_axis=0, concat_axis=0, tiled=True)]
    all_to_all x2 -> x1, starting transfers between devices: 14.6 us -> 28.3 us  [from_everyone(): return lax.all_to_all(copies, axes, split_axis=0, concat_axis=0, tiled=True)]
    all_to_all x0 -> x1, starting transfers between devices: none -> 6.44 us  [local(): lax.all_to_all(copies, 'zl', split_axis=0, concat_axis=0, tiled=True)]
    ppermute x7, waiting for transfers between devices: 22 us -> 18.6 us  [swapped(): lax.ppermute(value, axis, [(i, i ^ apart) for i in range(lax.axis_size(ax...]
    all_to_all x2 -> x1, waiting for transfers between devices: 9.38 us -> 12.7 us  [from_everyone(): return lax.all_to_all(copies, axes, split_axis=0, concat_axis=0, tiled=True)]
  transfers between devices with their start and end apart: 10 -> 10, of which waited for: 8 -> 6; matrix products, arithmetic and copies ran while one was open for 1% -> 1% of each run, Pallas kernels for 3% -> 1%
where the time goes in v4:
time: 172 us
  starting transfers between devices  70.8 us (41%)
  blocking collectives  41.8 us (24%)
  waiting for transfers between devices  40.2 us (23%)
  Pallas kernels  13.5 us (8%)
  local copies, waits for them, and re-layouts  3.2 us (2%)
    all_to_all x1, starting transfers between devices, from_everyone(): return lax.all_to_all(copies, axes, split_axis=0, concat_axis=0, tiled=True)  28.3 us
    all_to_all x1, blocking collectives, local(): sums = lax.all_to_all(sums, dp, split_axis=0, concat_axis=0, tiled=True)  21.7 us
    ppermute x7, starting transfers between devices, swapped(): lax.ppermute(value, axis, [(i, i ^ apart) for i in range(lax.axis_size(ax...  21.1 us
    ppermute x7, waiting for transfers between devices, swapped(): lax.ppermute(value, axis, [(i, i ^ apart) for i in range(lax.axis_size(ax...  18.6 us
    all_to_all x1, starting transfers between devices, local(): lax.all_to_all(sent, hi, split_axis=0, concat_axis=0, tiled=True)  15 us
    all_to_all x1, waiting for transfers between devices, from_everyone(): return lax.all_to_all(copies, axes, split_axis=0, concat_axis=0, tiled=True)  12.7 us
    all_to_all x1, blocking collectives, local(): sums = lax.all_to_all(sums, group, split_axis=0, concat_axis=0, tiled=True)  11.5 us
    all_to_all x1, waiting for transfers between devices, local(): lax.all_to_all(sent, hi, split_axis=0, concat_axis=0, tiled=True)  8.9 us
  transfers between devices with their start and end apart: 10, of which 6 were waited for; matrix products, arithmetic and copies ran while one was open for 1% of the time, Pallas kernels for 1%

profile of v4, /device:TPU:1, one launch (start us, length us, event | category | flops | bytes accessed | tf_op | source)
XLA Modules:
  0.0 171.6 jit_solution(6304219216715763010)
XLA Ops:
  0.6 4.9 %shard_map.50 = (bf16[4,64,512]{2,1,0:T(8,128)(2,1)}, bf16[512,512]{1,0:T(8,128)(2,1)}, bf16[512,512]{1,0:T(8,128)(2,1)}, bf16[512,512]{1,0:T(8,128)(2,1)}, bf16[512,512]{1,0:T(8,128)(2,1)}) custom-call(s32[1]{0:T(128)} %bitcast.me_ref, bf16[512,2048]{1,0:T(8,128)(2,1)} %pre_ref.3, bf16[64,512]{1,0:T(8,128)(2,1)} %grad_ref.1), custom_call_target="tpu_custom_call" | custom-call | flops 1073741824 | bytes 4194304 | tf_op jit(solution)/shard_map/pallas_call | solution.py:66
  5.5 6.4 %all-to-all-start = ((bf16[4,64,512]{2,1,0:T(8,128)(2,1)}), bf16[4,64,512]{2,1,0:T(8,128)(2,1)S(1)}, u32[]{:S(2)}, u32[]{:S(2)}) async-start(bf16[4,64,512]{2,1,0:T(8,128)(2,1)} %get-tuple-element.16), calls=%async_computation | async-start | bytes 524288 | tf_op jit(solution)/shard_map/all_to_all | solution.py:296
  12.0 5.2 %collective-permute-start = (bf16[512,512]{1,0:T(8,128)(2,1)}, bf16[512,512]{1,0:T(8,128)(2,1)S(1)}, u32[]{:S(2)}, u32[]{:S(2)}) collective-permute-start(bf16[512,512]{1,0:T(8,128)(2,1)} %get-tuple-element.17), channel_id=1, source_target_pairs={{0,24},{8,16},{16,8},{24,0},{1,25},{9,17},{17,9},{25,1},{2,26},{10... | collective-permute-start | bytes 1572872 | tf_op jit(solution)/shard_map/ppermute | solution.py:290
  17.1 1.9 %collective-permute-start.1 = (bf16[512,512]{1,0:T(8,128)(2,1)}, bf16[512,512]{1,0:T(8,128)(2,1)}, u32[]{:S(2)}, u32[]{:S(2)}) collective-permute-start(bf16[512,512]{1,0:T(8,128)(2,1)} %get-tuple-element.18), channel_id=1, source_target_pairs={{0,16},{8,24},{16,0},{24,8},{1,17},{9,25},{17,1},{25,9},{2,18},{10... | collective-permute-start | bytes 1572872 | tf_op jit(solution)/shard_map/ppermute | solution.py:290
  19.1 2.2 %collective-permute-start.2 = (bf16[512,512]{1,0:T(8,128)(2,1)}, bf16[512,512]{1,0:T(8,128)(2,1)}, u32[]{:S(2)}, u32[]{:S(2)}) collective-permute-start(bf16[512,512]{1,0:T(8,128)(2,1)} %get-tuple-element.19), channel_id=1, source_target_pairs={{0,8},{8,0},{16,24},{24,16},{1,9},{9,1},{17,25},{25,17},{2,10},{10... | collective-permute-start | bytes 1572872 | tf_op jit(solution)/shard_map/ppermute | solution.py:290
  21.3 0.1 pad_add_fusion.spot_ref
  21.3 0.0 all-to-all-done
  21.4 1.6 broadcast_in_dim.3
  22.9 28.3 %all-to-all-start.1 = ((bf16[8,4,64,512]{3,2,1,0:T(8,128)(2,1)}), bf16[8,4,64,512]{3,2,1,0:T(8,128)(2,1)S(1)}, u32[]{:S(2)}, u32[]{:S(2)}) async-start(bf16[8,4,64,512]{3,2,1,0:T(8,128)(2,1)} %broadcast_in_dim.3), calls=%async_computation.1 | async-start | bytes 4194304 | tf_op jit(solution)/shard_map/all_to_all | solution.py:39
  51.2 0.0 copy-start.2
  51.2 0.0 collective-permute-done.refs_0_.refs_3_
  51.2 13.6 %collective-permute-done.1.refs_1_.refs_2_ = bf16[512,512]{1,0:T(8,128)(2,1)} collective-permute-done((bf16[512,512]{1,0:T(8,128)(2,1)}, bf16[512,512]{1,0:T(8,128)(2,1)}, u32[]{:S(2)}, u32[]{:S(2)}) %collective-permute-start.1) | collective-permute-done | bytes 524320 | tf_op jit(solution)/shard_map/ppermute | solution.py:290
  64.9 0.0 collective-permute-done.2.refs_2_.refs_1_
  64.9 12.7 %all-to-all-done.1.grads_ref = bf16[8,4,64,512]{3,2,1,0:T(8,128)(2,1)S(1)} async-done(((bf16[8,4,64,512]{3,2,1,0:T(8,128)(2,1)}), bf16[8,4,64,512]{3,2,1,0:T(8,128)(2,1)S(1)}, u32[]{:S(2)}, u32[]{:S(2)}) %all-to-all-start.1) | async-done | bytes 2097184 | tf_op jit(solution)/shard_map/all_to_all | solution.py:39
  77.6 0.0 copy-done.2
  77.6 2.8 %shard_map.52 = (f32[512,512]{1,0:T(8,128)S(1)}, f32[512,512]{1,0:T(8,128)S(1)}, f32[512,512]{1,0:T(8,128)S(1)}, f32[512,512]{1,0:T(8,128)S(1)}, f32[32,1,128]{2,1,0:T(1,128)S(1)}) custom-call(s32[3]{0:T(128)S(1)} %pad_add_fusion.spot_ref, bf16[8,4,64,512]{3,2,1,0:T(8,128)(2,1)S(1)} %all-to-all-done.1.grads_ref, f32[8,128]{1,0:T(8,128)S(1)} %shard_map.51.late_ref, ...), custom_call_target="tpu_custom_call" | custom-call | flops 1073741824 | bytes 4194304 | tf_op jit(solution)/shard_map/pallas_call | solution.py:308
  80.4 11.5 %all_to_all.30.sums_ref = f32[32,1,128]{2,1,0:T(1,128)S(1)} all-to-all(f32[32,1,128]{2,1,0:T(1,128)S(1)} %get-tuple-element.21), channel_id=1, replica_groups=mesh['y'=4,'zh'=4,'zl'=4,'x'=4,'c'=2] {'zl','x','c'}, dimensions={0} | all-to-all | bytes 32768 | tf_op jit(solution)/shard_map/all_to_all | solution.py:315
  91.9 0.7 shard_map.53
  92.6 0.0 copy-start
  92.6 0.9 convert_element_type.10
  93.5 15.0 %all-to-all-start.3 = ((f16[16,32,512]{2,1,0:T(8,128)(2,1)}), f16[16,32,512]{2,1,0:T(8,128)(2,1)S(1)}, u32[]{:S(2)}, u32[]{:S(2)}) async-start(f16[16,32,512]{2,1,0:T(8,128)(2,1)} %bitcast.8), calls=%async_computation.3 | async-start | bytes 1048576 | tf_op jit(solution)/shard_map/all_to_all | solution.py:341
  108.5 0.0 copy-done
  108.5 0.0 copy-start.1
  108.5 1.6 copy-done.1
  110.1 1.9 %shard_map.54 = (f32[4,64,512]{2,1,0:T(8,128)S(1)}, f32[4,64,512]{2,1,0:T(8,128)S(1)}) custom-call(s32[3]{0:T(128)S(1)} %pad_add_fusion.spot_ref, bf16[512,2048]{1,0:T(8,128)(2,1)S(1)} %copy-done, bf16[2048,512]{1,0:T(8,128)(2,1)S(1)} %copy-done.1, f32[8,128]{1,0:T(8,128)S(1)} %get-tuple-element.26.late_ref.inverse_ref), custom_call_target="tpu_custom_call" | custom-call | flops 1073741824 | bytes 4194304 | tf_op jit(solution)/shard_map/pallas_call | solution.py:325
  111.9 2.8 %collective-permute-start.3 = (f32[4,64,512]{2,1,0:T(8,128)S(1)}, f32[4,64,512]{2,1,0:T(8,128)S(1)}, u32[]{:S(2)}, u32[]{:S(2)}) collective-permute-start(f32[4,64,512]{2,1,0:T(8,128)S(1)} %get-tuple-element.28), channel_id=1, source_target_pairs={{0,1},{1,0},{2,3},{3,2},{4,5},{5,4},{6,7},{7,6},{8,9},{9,8},{10,11... | collective-permute-start | bytes 1572872 | tf_op jit(solution)/shard_map/ppermute | solution.py:290
  114.8 1.5 collective-permute-done.3
  116.3 0.1 add.15
  116.4 2.2 %collective-permute-start.4 = (f32[64,512]{1,0:T(8,128)S(1)}, f32[64,512]{1,0:T(8,128)S(1)}, u32[]{:S(2)}, u32[]{:S(2)}) collective-permute-start(f32[64,512]{1,0:T(8,128)S(1)} %get-tuple-element.30), channel_id=1, source_target_pairs={{0,2},{2,0},{4,6},{6,4},{1,3},{3,1},{5,7},{7,5},{8,10},{10,8},{12,... | collective-permute-start | bytes 393224 | tf_op jit(solution)/shard_map/ppermute | solution.py:290
  118.6 2.8 %collective-permute-start.6 = (f32[64,512]{1,0:T(8,128)S(1)}, f32[64,512]{1,0:T(8,128)S(1)}, u32[]{:S(2)}, u32[]{:S(2)}) collective-permute-start(f32[64,512]{1,0:T(8,128)S(1)} %get-tuple-element.31), channel_id=1, source_target_pairs={{0,6},{2,4},{4,2},{6,0},{1,7},{3,5},{5,3},{7,1},{8,14},{10,12},{12... | collective-permute-start | bytes 393224 | tf_op jit(solution)/shard_map/ppermute | solution.py:290
  121.4 4.0 %collective-permute-start.5 = (f32[64,512]{1,0:T(8,128)S(1)}, f32[64,512]{1,0:T(8,128)S(1)}, u32[]{:S(2)}, u32[]{:S(2)}) collective-permute-start(f32[64,512]{1,0:T(8,128)S(1)} %get-tuple-element.32), channel_id=1, source_target_pairs={{0,4},{2,6},{4,0},{6,2},{1,5},{3,7},{5,1},{7,3},{8,12},{10,14},{12... | collective-permute-start | bytes 393224 | tf_op jit(solution)/shard_map/ppermute | solution.py:290
  125.4 0.0 collective-permute-done.4
  125.4 0.7 collective-permute-done.6
  126.1 2.8 %collective-permute-done.5 = f32[64,512]{1,0:T(8,128)S(1)} collective-permute-done((f32[64,512]{1,0:T(8,128)S(1)}, f32[64,512]{1,0:T(8,128)S(1)}, u32[]{:S(2)}, u32[]{:S(2)}) %collective-permute-start.5) | collective-permute-done | bytes 131104 | tf_op jit(solution)/shard_map/ppermute | solution.py:290
  128.9 0.0 copy-start.3
  128.9 8.9 %all-to-all-done.3 = f16[16,32,512]{2,1,0:T(8,128)(2,1)S(1)} async-done(((f16[16,32,512]{2,1,0:T(8,128)(2,1)}), f16[16,32,512]{2,1,0:T(8,128)(2,1)S(1)}, u32[]{:S(2)}, u32[]{:S(2)}) %all-to-all-start.3) | async-done | bytes 524320 | tf_op jit(solution)/shard_map/all_to_all | solution.py:341
  137.8 0.1 convert_element_type.11.nodes_ref
  138.0 1.6 shard_map.55
  139.6 0.0 copy-done.3
  139.6 8.6 %all_to_all.31.sums_ref = f32[8,2,128]{2,1,0:T(2,128)S(1)} all-to-all(f32[8,2,128]{2,1,0:T(2,128)S(1)} %shard_map.55), channel_id=1, replica_groups=mesh['y'=4,'zh'=4,'zl'=4,'x'=4,'c'=2] {'x','c'}, dimensions={0} | all-to-all | bytes 16384 | tf_op jit(solution)/shard_map/all_to_all | solution.py:350
  148.2 21.7 %all_to_all.32.sums_ref = f32[64,2,128]{2,1,0:T(2,128)S(1)} all-to-all(f32[64,2,128]{2,1,0:T(2,128)S(1)} %shard_map.56), channel_id=1, replica_groups=mesh['y'=4,'zh'=4,'zl'=4,'x'=4,'c'=2] {'y','zh','zl'}, dimensions={0} | all-to-all | bytes 131072 | tf_op jit(solution)/shard_map/all_to_all | solution.py:353
  169.9 1.7 shard_map.57
  (4 shorter events, 0.1 us)
Async XLA Ops:
  5.5 15.8 %all-to-all-start = ((bf16[4,64,512]{2,1,0:T(8,128)(2,1)}), bf16[4,64,512]{2,1,0:T(8,128)(2,1)S(1)}, u32[]{:S(2)}, u32[]{:S(2)}) async-start(bf16[4,64,512]{2,1,0:T(8,128)(2,1)} %get-tuple-element.16), calls=%async_computation | async-start | bytes 524288 | tf_op jit(solution)/shard_map/all_to_all | solution.py:296
  12.0 39.3 %collective-permute-start = (bf16[512,512]{1,0:T(8,128)(2,1)}, bf16[512,512]{1,0:T(8,128)(2,1)S(1)}, u32[]{:S(2)}, u32[]{:S(2)}) collective-permute-start(bf16[512,512]{1,0:T(8,128)(2,1)} %get-tuple-element.17), channel_id=1, source_target_pairs={{0,24},{8,16},{16,8},{24,0},{1,25},{9,17},{17,9},{25,1},{2,26},{10... | collective-permute-start | bytes 1572872 | tf_op jit(solution)/shard_map/ppermute | solution.py:290
  17.1 47.7 %collective-permute-start.1 = (bf16[512,512]{1,0:T(8,128)(2,1)}, bf16[512,512]{1,0:T(8,128)(2,1)}, u32[]{:S(2)}, u32[]{:S(2)}) collective-permute-start(bf16[512,512]{1,0:T(8,128)(2,1)} %get-tuple-element.18), channel_id=1, source_target_pairs={{0,16},{8,24},{16,0},{24,8},{1,17},{9,25},{17,1},{25,9},{2,18},{10... | collective-permute-start | bytes 1572872 | tf_op jit(solution)/shard_map/ppermute | solution.py:290
  19.1 45.8 %collective-permute-start.2 = (bf16[512,512]{1,0:T(8,128)(2,1)}, bf16[512,512]{1,0:T(8,128)(2,1)}, u32[]{:S(2)}, u32[]{:S(2)}) collective-permute-start(bf16[512,512]{1,0:T(8,128)(2,1)} %get-tuple-element.19), channel_id=1, source_target_pairs={{0,8},{8,0},{16,24},{24,16},{1,9},{9,1},{17,25},{25,17},{2,10},{10... | collective-permute-start | bytes 1572872 | tf_op jit(solution)/shard_map/ppermute | solution.py:290
  22.9 54.6 %all-to-all-start.1 = ((bf16[8,4,64,512]{3,2,1,0:T(8,128)(2,1)}), bf16[8,4,64,512]{3,2,1,0:T(8,128)(2,1)S(1)}, u32[]{:S(2)}, u32[]{:S(2)}) async-start(bf16[8,4,64,512]{3,2,1,0:T(8,128)(2,1)} %broadcast_in_dim.3), calls=%async_computation.1 | async-start | bytes 4194304 | tf_op jit(solution)/shard_map/all_to_all | solution.py:39
  51.2 26.3 %copy-start.2 = (bf16[512,512]{1,0:T(8,128)(2,1)S(1)}, bf16[512,512]{1,0:T(8,128)(2,1)}, u32[]{:S(2)}) copy-start(bf16[512,512]{1,0:T(8,128)(2,1)} %get-tuple-element.20.refs_0_) | copy-start | bytes 1572868
  92.6 15.9 %copy-start = (bf16[512,2048]{1,0:T(8,128)(2,1)S(1)}, bf16[512,2048]{1,0:T(8,128)(2,1)}, u32[]{:S(2)}) copy-start(bf16[512,2048]{1,0:T(8,128)(2,1)} %pre_ref.3) | copy-start | bytes 6291460
  93.5 44.4 %all-to-all-start.3 = ((f16[16,32,512]{2,1,0:T(8,128)(2,1)}), f16[16,32,512]{2,1,0:T(8,128)(2,1)S(1)}, u32[]{:S(2)}, u32[]{:S(2)}) async-start(f16[16,32,512]{2,1,0:T(8,128)(2,1)} %bitcast.8), calls=%async_computation.3 | async-start | bytes 1048576 | tf_op jit(solution)/shard_map/all_to_all | solution.py:341
  108.5 1.6 copy-start.1
  111.9 4.4 %collective-permute-start.3 = (f32[4,64,512]{2,1,0:T(8,128)S(1)}, f32[4,64,512]{2,1,0:T(8,128)S(1)}, u32[]{:S(2)}, u32[]{:S(2)}) collective-permute-start(f32[4,64,512]{2,1,0:T(8,128)S(1)} %get-tuple-element.28), channel_id=1, source_target_pairs={{0,1},{1,0},{2,3},{3,2},{4,5},{5,4},{6,7},{7,6},{8,9},{9,8},{10,11... | collective-permute-start | bytes 1572872 | tf_op jit(solution)/shard_map/ppermute | solution.py:290
  116.4 9.0 %collective-permute-start.4 = (f32[64,512]{1,0:T(8,128)S(1)}, f32[64,512]{1,0:T(8,128)S(1)}, u32[]{:S(2)}, u32[]{:S(2)}) collective-permute-start(f32[64,512]{1,0:T(8,128)S(1)} %get-tuple-element.30), channel_id=1, source_target_pairs={{0,2},{2,0},{4,6},{6,4},{1,3},{3,1},{5,7},{7,5},{8,10},{10,8},{12,... | collective-permute-start | bytes 393224 | tf_op jit(solution)/shard_map/ppermute | solution.py:290
  118.6 7.5 %collective-permute-start.6 = (f32[64,512]{1,0:T(8,128)S(1)}, f32[64,512]{1,0:T(8,128)S(1)}, u32[]{:S(2)}, u32[]{:S(2)}) collective-permute-start(f32[64,512]{1,0:T(8,128)S(1)} %get-tuple-element.31), channel_id=1, source_target_pairs={{0,6},{2,4},{4,2},{6,0},{1,7},{3,5},{5,3},{7,1},{8,14},{10,12},{12... | collective-permute-start | bytes 393224 | tf_op jit(solution)/shard_map/ppermute | solution.py:290
  121.4 7.5 %collective-permute-start.5 = (f32[64,512]{1,0:T(8,128)S(1)}, f32[64,512]{1,0:T(8,128)S(1)}, u32[]{:S(2)}, u32[]{:S(2)}) collective-permute-start(f32[64,512]{1,0:T(8,128)S(1)} %get-tuple-element.32), channel_id=1, source_target_pairs={{0,4},{2,6},{4,0},{6,2},{1,5},{3,7},{5,1},{7,3},{8,12},{10,14},{12... | collective-permute-start | bytes 393224 | tf_op jit(solution)/shard_map/ppermute | solution.py:290
  128.9 10.6 %copy-start.3 = (bf16[64,512]{1,0:T(8,128)(2,1)}, bf16[64,512]{1,0:T(8,128)(2,1)S(1)}, u32[]{:S(2)}) copy-start(bf16[64,512]{1,0:T(8,128)(2,1)S(1)} %fusion.3.late_ref) | copy-start | bytes 196612

commit v5 on v4

--- a/solution.py
+++ b/solution.py
@@ -39,7 +39,7 @@
     return lax.all_to_all(copies, axes, split_axis=0, concat_axis=0, tiled=True)
 
 
-def deal_kernel(me_ref, pre_ref, grad_ref, copies_ref, *refs):
+def deal_kernel(me_ref, pre_ref, *refs):
     out_refs, deal_ref = refs[:LEAVES], refs[LEAVES]
     width = pre_ref.shape[1]
 
@@ -50,8 +50,6 @@
         block = row >> 5
         place = (((block & 3) ^ me_ref[0]) << 7) + ((block >> 2) << 5) + (row & 31)
         deal_ref[...] = jnp.where(place == col, 1.0, 0.0).astype(bf16)
-        for copy in range(LEAVES):
-            copies_ref[copy] = grad_ref[...]
 
     part = jnp.maximum(pre_ref[...], jnp.zeros((), bf16))
     dealt = jnp.dot(part, deal_ref[...], preferred_element_type=f32).astype(bf16)
@@ -59,30 +57,24 @@
         out_refs[k][...] = dealt[:, k * 128 : (k + 1) * 128]
 
 
-def deal(me, pre_act, out_grad):
+def deal(me, pre_act):
     tokens, hidden = pre_act.shape
-    shard, width = out_grad.shape
     group = 512
     return pl.pallas_call(
         deal_kernel,
         grid_spec=pltpu.PrefetchScalarGridSpec(
             num_scalar_prefetch=1,
             grid=(hidden // group,),
-            in_specs=[
-                pl.BlockSpec((tokens, group), lambda g, me: (0, g)),
-                pl.BlockSpec((shard, width), lambda g, me: (0, 0)),
-            ],
-            out_specs=[pl.BlockSpec((LEAVES, shard, width), lambda g, me: (0, 0, 0))]
-            + [pl.BlockSpec((tokens, group // LEAVES), lambda g, me: (0, g))] * LEAVES,
+            in_specs=[pl.BlockSpec((tokens, group), lambda g, me: (0, g))],
+            out_specs=[pl.BlockSpec((tokens, group // LEAVES), lambda g, me: (0, g))] * LEAVES,
             scratch_shapes=[pltpu.VMEM((group, group), bf16)],
         ),
-        out_shape=[jax.ShapeDtypeStruct((LEAVES, shard, width), bf16)]
-        + [jax.ShapeDtypeStruct((tokens, hidden // LEAVES), bf16)] * LEAVES,
-        compiler_params=pltpu.CompilerParams(vmem_limit_bytes=63 * 1024 * 1024),
+        out_shape=[jax.ShapeDtypeStruct((tokens, hidden // LEAVES), bf16)] * LEAVES,
+        compiler_params=pltpu.CompilerParams(vmem_limit_bytes=LIMIT),
         cost_estimate=pl.CostEstimate(
             flops=2 * tokens * hidden * group, bytes_accessed=4 * tokens * hidden, transcendentals=0
         ),
-    )(me, pre_act, out_grad)
+    )(me, pre_act)
 
 
 def arrived_kernel(*refs):
@@ -289,12 +281,12 @@
     def swapped(value, axis, apart):
         return lax.ppermute(value, axis, [(i, i ^ apart) for i in range(lax.axis_size(axis))])
 
-    copies, *dealt = deal(me, pre_act, out_grad)
+    shards = from_everyone(out_grad, "zl")
+    grads = from_everyone(shards, mp)
+    dealt = deal(me, pre_act)
     acts = {0: dealt[0]}
     for k in (3, 2, 1):
         acts[k] = swapped(dealt[k], "zl", k)
-    shards = lax.all_to_all(copies, "zl", split_axis=0, concat_axis=0, tiled=True)
-    grads = from_everyone(shards, mp)
     arrived = pl.pallas_call(
         arrived_kernel,
         out_shape=jax.ShapeDtypeStruct((8, 128), f32),

time: 172 us -> 162 us (0.942)
  starting transfers between devices: 70.8 us -> 51 us
  waiting for transfers between devices: 40.2 us -> 45.5 us
  local copies, waits for them, and re-layouts: 3.2 us -> 6.35 us
  blocking collectives: 41.8 us -> 44.3 us
    ppermute x7, waiting for transfers between devices: 18.6 us -> 36.6 us  [swapped(): lax.ppermute(value, axis, [(i, i ^ apart) for i in range(lax.axis_size(ax...]
    all_to_all x1 -> x2, starting transfers between devices: 28.3 us -> 14.6 us  [from_everyone(): return lax.all_to_all(copies, axes, split_axis=0, concat_axis=0, tiled=True)]
    all_to_all x1 -> x2, waiting for transfers between devices: 12.7 us -> 0.01 us  [from_everyone(): return lax.all_to_all(copies, axes, split_axis=0, concat_axis=0, tiled=True)]
    all_to_all x1 -> x0, starting transfers between devices: 6.44 us -> none  [local(): lax.all_to_all(copies, 'zl', split_axis=0, concat_axis=0, tiled=True)]
    all_to_all x1, blocking collectives: 11.5 us -> 14 us  [local(): sums = lax.all_to_all(sums, group, split_axis=0, concat_axis=0, tiled=True)]
  transfers between devices with their start and end apart: 10 -> 10, of which waited for: 6 -> 5; matrix products, arithmetic and copies ran while one was open for 1% -> 1% of each run, Pallas kernels for 1% -> 3%
where the time goes in v5:
time: 162 us; the launch traced here: 161 us
  starting transfers between devices  51 us (31%)
  waiting for transfers between devices  45.5 us (28%)
  blocking collectives  44.3 us (27%)
  Pallas kernels  11.9 us (7%)
  local copies, waits for them, and re-layouts  6.35 us (4%)
    ppermute x7, waiting for transfers between devices, swapped(): lax.ppermute(value, axis, [(i, i ^ apart) for i in range(lax.axis_size(ax...  36.6 us
    all_to_all x1, blocking collectives, local(): sums = lax.all_to_all(sums, dp, split_axis=0, concat_axis=0, tiled=True)  21.7 us
    ppermute x7, starting transfers between devices, swapped(): lax.ppermute(value, axis, [(i, i ^ apart) for i in range(lax.axis_size(ax...  21.1 us
    all_to_all x1, starting transfers between devices, local(): lax.all_to_all(sent, hi, split_axis=0, concat_axis=0, tiled=True)  15.3 us
    all_to_all x2, starting transfers between devices, from_everyone(): return lax.all_to_all(copies, axes, split_axis=0, concat_axis=0, tiled=True)  14.6 us
    all_to_all x1, blocking collectives, local(): sums = lax.all_to_all(sums, group, split_axis=0, concat_axis=0, tiled=True)  14 us
    all_to_all x1, waiting for transfers between devices, local(): lax.all_to_all(sent, hi, split_axis=0, concat_axis=0, tiled=True)  8.9 us
    all_to_all x1, blocking collectives, local(): sums = lax.all_to_all(sums, mp, split_axis=0, concat_axis=0, tiled=True)  8.61 us
  transfers between devices with their start and end apart: 10, of which 5 were waited for; matrix products, arithmetic and copies ran while one was open for 1% of the time, Pallas kernels for 3%

profile of v5, /device:TPU:1, one launch (start us, length us, event | category | flops | bytes accessed | tf_op | source)
XLA Modules:
  0.0 161.2 jit_solution(6366767406147284140)
XLA Ops:
  0.6 1.6 broadcast_in_dim.6
  2.2 6.4 %all-to-all-start = ((bf16[4,64,512]{2,1,0:T(8,128)(2,1)}), bf16[4,64,512]{2,1,0:T(8,128)(2,1)S(1)}, u32[]{:S(2)}, u32[]{:S(2)}) async-start(bf16[4,64,512]{2,1,0:T(8,128)(2,1)} %broadcast_in_dim.6), calls=%async_computation | async-start | bytes 524288 | tf_op jit(solution)/shard_map/all_to_all | solution.py:39
  8.6 0.0 copy-start
  8.6 1.6 copy-done
  10.2 3.3 %shard_map.50 = (bf16[512,512]{1,0:T(8,128)(2,1)S(1)}, bf16[512,512]{1,0:T(8,128)(2,1)}, bf16[512,512]{1,0:T(8,128)(2,1)}, bf16[512,512]{1,0:T(8,128)(2,1)}) custom-call(s32[1]{0:T(128)} %bitcast.me_ref, bf16[512,2048]{1,0:T(8,128)(2,1)S(1)} %copy-done), custom_call_target="tpu_custom_call" | custom-call | flops 1073741824 | bytes 4194304 | tf_op jit(solution)/shard_map/pallas_call | solution.py:63
  13.5 5.2 %collective-permute-start = (bf16[512,512]{1,0:T(8,128)(2,1)}, bf16[512,512]{1,0:T(8,128)(2,1)S(1)}, u32[]{:S(2)}, u32[]{:S(2)}) collective-permute-start(bf16[512,512]{1,0:T(8,128)(2,1)} %get-tuple-element.15), channel_id=1, source_target_pairs={{0,24},{8,16},{16,8},{24,0},{1,25},{9,17},{17,9},{25,1},{2,26},{10... | collective-permute-start | bytes 1572872 | tf_op jit(solution)/shard_map/ppermute | solution.py:282
  18.7 1.9 %collective-permute-start.1 = (bf16[512,512]{1,0:T(8,128)(2,1)}, bf16[512,512]{1,0:T(8,128)(2,1)}, u32[]{:S(2)}, u32[]{:S(2)}) collective-permute-start(bf16[512,512]{1,0:T(8,128)(2,1)} %get-tuple-element.16), channel_id=1, source_target_pairs={{0,16},{8,24},{16,0},{24,8},{1,17},{9,25},{17,1},{25,9},{2,18},{10... | collective-permute-start | bytes 1572872 | tf_op jit(solution)/shard_map/ppermute | solution.py:282
  20.6 2.2 %collective-permute-start.2 = (bf16[512,512]{1,0:T(8,128)(2,1)}, bf16[512,512]{1,0:T(8,128)(2,1)}, u32[]{:S(2)}, u32[]{:S(2)}) collective-permute-start(bf16[512,512]{1,0:T(8,128)(2,1)} %get-tuple-element.17), channel_id=1, source_target_pairs={{0,8},{8,0},{16,24},{24,16},{1,9},{9,1},{17,25},{25,17},{2,10},{10... | collective-permute-start | bytes 1572872 | tf_op jit(solution)/shard_map/ppermute | solution.py:282
  22.8 0.1 pad_add_fusion.spot_ref
  22.9 0.0 all-to-all-done
  22.9 1.6 broadcast_in_dim.7
  24.5 8.2 %all-to-all-start.1 = ((bf16[8,4,64,512]{3,2,1,0:T(8,128)(2,1)}), bf16[8,4,64,512]{3,2,1,0:T(8,128)(2,1)S(1)}, u32[]{:S(2)}, u32[]{:S(2)}) async-start(bf16[8,4,64,512]{3,2,1,0:T(8,128)(2,1)} %broadcast_in_dim.7), calls=%async_computation.1 | async-start | bytes 4194304 | tf_op jit(solution)/shard_map/all_to_all | solution.py:39
  32.6 0.0 collective-permute-done.refs_0_.refs_3_
  32.6 31.6 %collective-permute-done.1.refs_1_.refs_2_ = bf16[512,512]{1,0:T(8,128)(2,1)} collective-permute-done((bf16[512,512]{1,0:T(8,128)(2,1)}, bf16[512,512]{1,0:T(8,128)(2,1)}, u32[]{:S(2)}, u32[]{:S(2)}) %collective-permute-start.1) | collective-permute-done | bytes 524320 | tf_op jit(solution)/shard_map/ppermute | solution.py:282
  64.3 0.0 collective-permute-done.2.refs_2_.refs_1_
  64.3 0.0 all-to-all-done.1.grads_ref
  64.3 2.8 %shard_map.52 = (f32[512,512]{1,0:T(8,128)S(1)}, f32[512,512]{1,0:T(8,128)S(1)}, f32[512,512]{1,0:T(8,128)S(1)}, f32[512,512]{1,0:T(8,128)S(1)}, f32[32,1,128]{2,1,0:T(1,128)S(1)}) custom-call(s32[3]{0:T(128)S(1)} %pad_add_fusion.spot_ref, bf16[8,4,64,512]{3,2,1,0:T(8,128)(2,1)S(1)} %all-to-all-done.1.grads_ref, f32[8,128]{1,0:T(8,128)S(1)} %shard_map.51.late_ref, ...), custom_call_target="tpu_custom_call" | custom-call | flops 1073741824 | bytes 4194304 | tf_op jit(solution)/shard_map/pallas_call | solution.py:300
  67.1 14.0 %all_to_all.30.sums_ref = f32[32,1,128]{2,1,0:T(1,128)S(1)} all-to-all(f32[32,1,128]{2,1,0:T(1,128)S(1)} %get-tuple-element.19), channel_id=1, replica_groups=mesh['y'=4,'zh'=4,'zl'=4,'x'=4,'c'=2] {'zl','x','c'}, dimensions={0} | all-to-all | bytes 32768 | tf_op jit(solution)/shard_map/all_to_all | solution.py:307
  81.1 0.7 shard_map.53
  81.8 0.0 copy-start.1
  81.8 0.9 convert_element_type.10
  82.7 15.3 %all-to-all-start.3 = ((f16[16,32,512]{2,1,0:T(8,128)(2,1)}), f16[16,32,512]{2,1,0:T(8,128)(2,1)S(1)}, u32[]{:S(2)}, u32[]{:S(2)}) async-start(f16[16,32,512]{2,1,0:T(8,128)(2,1)} %bitcast.8), calls=%async_computation.3 | async-start | bytes 1048576 | tf_op jit(solution)/shard_map/all_to_all | solution.py:333
  98.0 0.0 copy-done.1
  98.0 0.0 copy-start.2
  98.1 1.6 copy-done.2
  99.6 1.9 %shard_map.54 = (f32[4,64,512]{2,1,0:T(8,128)S(1)}, f32[4,64,512]{2,1,0:T(8,128)S(1)}) custom-call(s32[3]{0:T(128)S(1)} %pad_add_fusion.spot_ref, bf16[512,2048]{1,0:T(8,128)(2,1)S(1)} %copy-done.1, bf16[2048,512]{1,0:T(8,128)(2,1)S(1)} %copy-done.2, f32[8,128]{1,0:T(8,128)S(1)} %get-tuple-element.24.late_ref.inverse_ref), custom_call_target="tpu_custom_call" | custom-call | flops 1073741824 | bytes 4194304 | tf_op jit(solution)/shard_map/pallas_call | solution.py:317
  101.5 2.8 %collective-permute-start.3 = (f32[4,64,512]{2,1,0:T(8,128)S(1)}, f32[4,64,512]{2,1,0:T(8,128)S(1)}, u32[]{:S(2)}, u32[]{:S(2)}) collective-permute-start(f32[4,64,512]{2,1,0:T(8,128)S(1)} %get-tuple-element.26), channel_id=1, source_target_pairs={{0,1},{1,0},{2,3},{3,2},{4,5},{5,4},{6,7},{7,6},{8,9},{9,8},{10,11... | collective-permute-start | bytes 1572872 | tf_op jit(solution)/shard_map/ppermute | solution.py:282
  104.3 1.5 collective-permute-done.3
  105.8 0.1 add.15
  106.0 2.2 %collective-permute-start.4 = (f32[64,512]{1,0:T(8,128)S(1)}, f32[64,512]{1,0:T(8,128)S(1)}, u32[]{:S(2)}, u32[]{:S(2)}) collective-permute-start(f32[64,512]{1,0:T(8,128)S(1)} %get-tuple-element.28), channel_id=1, source_target_pairs={{0,2},{2,0},{4,6},{6,4},{1,3},{3,1},{5,7},{7,5},{8,10},{10,8},{12,... | collective-permute-start | bytes 393224 | tf_op jit(solution)/shard_map/ppermute | solution.py:282
  108.2 2.8 %collective-permute-start.6 = (f32[64,512]{1,0:T(8,128)S(1)}, f32[64,512]{1,0:T(8,128)S(1)}, u32[]{:S(2)}, u32[]{:S(2)}) collective-permute-start(f32[64,512]{1,0:T(8,128)S(1)} %get-tuple-element.29), channel_id=1, source_target_pairs={{0,6},{2,4},{4,2},{6,0},{1,7},{3,5},{5,3},{7,1},{8,14},{10,12},{12... | collective-permute-start | bytes 393224 | tf_op jit(solution)/shard_map/ppermute | solution.py:282
  111.0 4.0 %collective-permute-start.5 = (f32[64,512]{1,0:T(8,128)S(1)}, f32[64,512]{1,0:T(8,128)S(1)}, u32[]{:S(2)}, u32[]{:S(2)}) collective-permute-start(f32[64,512]{1,0:T(8,128)S(1)} %get-tuple-element.30), channel_id=1, source_target_pairs={{0,4},{2,6},{4,0},{6,2},{1,5},{3,7},{5,1},{7,3},{8,12},{10,14},{12... | collective-permute-start | bytes 393224 | tf_op jit(solution)/shard_map/ppermute | solution.py:282
  115.0 0.0 collective-permute-done.4
  115.0 0.7 collective-permute-done.6
  115.7 2.8 %collective-permute-done.5 = f32[64,512]{1,0:T(8,128)S(1)} collective-permute-done((f32[64,512]{1,0:T(8,128)S(1)}, f32[64,512]{1,0:T(8,128)S(1)}, u32[]{:S(2)}, u32[]{:S(2)}) %collective-permute-start.5) | collective-permute-done | bytes 131104 | tf_op jit(solution)/shard_map/ppermute | solution.py:282
  118.5 0.0 copy-start.3
  118.5 8.9 %all-to-all-done.3 = f16[16,32,512]{2,1,0:T(8,128)(2,1)S(1)} async-done(((f16[16,32,512]{2,1,0:T(8,128)(2,1)}), f16[16,32,512]{2,1,0:T(8,128)(2,1)S(1)}, u32[]{:S(2)}, u32[]{:S(2)}) %all-to-all-start.3) | async-done | bytes 524320 | tf_op jit(solution)/shard_map/all_to_all | solution.py:333
  127.4 0.1 convert_element_type.11.nodes_ref
  127.6 1.6 shard_map.55
  129.1 0.0 copy-done.3
  129.1 8.6 %all_to_all.31.sums_ref = f32[8,2,128]{2,1,0:T(2,128)S(1)} all-to-all(f32[8,2,128]{2,1,0:T(2,128)S(1)} %shard_map.55), channel_id=1, replica_groups=mesh['y'=4,'zh'=4,'zl'=4,'x'=4,'c'=2] {'x','c'}, dimensions={0} | all-to-all | bytes 16384 | tf_op jit(solution)/shard_map/all_to_all | solution.py:342
  137.8 21.7 %all_to_all.32.sums_ref = f32[64,2,128]{2,1,0:T(2,128)S(1)} all-to-all(f32[64,2,128]{2,1,0:T(2,128)S(1)} %shard_map.56), channel_id=1, replica_groups=mesh['y'=4,'zh'=4,'zl'=4,'x'=4,'c'=2] {'y','zh','zl'}, dimensions={0} | all-to-all | bytes 131072 | tf_op jit(solution)/shard_map/all_to_all | solution.py:345
  159.5 1.7 %shard_map.57 = f32[32,512]{1,0:T(8,128)} custom-call(f32[64,2,128]{2,1,0:T(2,128)S(1)} %all_to_all.32.sums_ref, f32[16,32,512]{2,1,0:T(8,128)S(1)} %convert_element_type.11.nodes_ref), custom_call_target="tpu_custom_call" | custom-call | flops 524288 | bytes 1048576 | tf_op jit(solution)/shard_map/pallas_call | solution.py:346
  (4 shorter events, 0.1 us)
Async XLA Ops:
  2.2 20.7 %all-to-all-start = ((bf16[4,64,512]{2,1,0:T(8,128)(2,1)}), bf16[4,64,512]{2,1,0:T(8,128)(2,1)S(1)}, u32[]{:S(2)}, u32[]{:S(2)}) async-start(bf16[4,64,512]{2,1,0:T(8,128)(2,1)} %broadcast_in_dim.6), calls=%async_computation | async-start | bytes 524288 | tf_op jit(solution)/shard_map/all_to_all | solution.py:39
  8.6 1.6 copy-start
  13.5 19.1 %collective-permute-start = (bf16[512,512]{1,0:T(8,128)(2,1)}, bf16[512,512]{1,0:T(8,128)(2,1)S(1)}, u32[]{:S(2)}, u32[]{:S(2)}) collective-permute-start(bf16[512,512]{1,0:T(8,128)(2,1)} %get-tuple-element.15), channel_id=1, source_target_pairs={{0,24},{8,16},{16,8},{24,0},{1,25},{9,17},{17,9},{25,1},{2,26},{10... | collective-permute-start | bytes 1572872 | tf_op jit(solution)/shard_map/ppermute | solution.py:282
  18.7 45.6 %collective-permute-start.1 = (bf16[512,512]{1,0:T(8,128)(2,1)}, bf16[512,512]{1,0:T(8,128)(2,1)}, u32[]{:S(2)}, u32[]{:S(2)}) collective-permute-start(bf16[512,512]{1,0:T(8,128)(2,1)} %get-tuple-element.16), channel_id=1, source_target_pairs={{0,16},{8,24},{16,0},{24,8},{1,17},{9,25},{17,1},{25,9},{2,18},{10... | collective-permute-start | bytes 1572872 | tf_op jit(solution)/shard_map/ppermute | solution.py:282
  20.6 43.7 %collective-permute-start.2 = (bf16[512,512]{1,0:T(8,128)(2,1)}, bf16[512,512]{1,0:T(8,128)(2,1)}, u32[]{:S(2)}, u32[]{:S(2)}) collective-permute-start(bf16[512,512]{1,0:T(8,128)(2,1)} %get-tuple-element.17), channel_id=1, source_target_pairs={{0,8},{8,0},{16,24},{24,16},{1,9},{9,1},{17,25},{25,17},{2,10},{10... | collective-permute-start | bytes 1572872 | tf_op jit(solution)/shard_map/ppermute | solution.py:282
  24.5 39.8 %all-to-all-start.1 = ((bf16[8,4,64,512]{3,2,1,0:T(8,128)(2,1)}), bf16[8,4,64,512]{3,2,1,0:T(8,128)(2,1)S(1)}, u32[]{:S(2)}, u32[]{:S(2)}) async-start(bf16[8,4,64,512]{3,2,1,0:T(8,128)(2,1)} %broadcast_in_dim.7), calls=%async_computation.1 | async-start | bytes 4194304 | tf_op jit(solution)/shard_map/all_to_all | solution.py:39
  81.8 16.2 %copy-start.1 = (bf16[512,2048]{1,0:T(8,128)(2,1)S(1)}, bf16[512,2048]{1,0:T(8,128)(2,1)}, u32[]{:S(2)}) copy-start(bf16[512,2048]{1,0:T(8,128)(2,1)} %pre_ref.3) | copy-start | bytes 6291460
  82.7 44.7 %all-to-all-start.3 = ((f16[16,32,512]{2,1,0:T(8,128)(2,1)}), f16[16,32,512]{2,1,0:T(8,128)(2,1)S(1)}, u32[]{:S(2)}, u32[]{:S(2)}) async-start(f16[16,32,512]{2,1,0:T(8,128)(2,1)} %bitcast.8), calls=%async_computation.3 | async-start | bytes 1048576 | tf_op jit(solution)/shard_map/all_to_all | solution.py:333
  98.0 1.6 copy-start.2
  101.5 4.4 %collective-permute-start.3 = (f32[4,64,512]{2,1,0:T(8,128)S(1)}, f32[4,64,512]{2,1,0:T(8,128)S(1)}, u32[]{:S(2)}, u32[]{:S(2)}) collective-permute-start(f32[4,64,512]{2,1,0:T(8,128)S(1)} %get-tuple-element.26), channel_id=1, source_target_pairs={{0,1},{1,0},{2,3},{3,2},{4,5},{5,4},{6,7},{7,6},{8,9},{9,8},{10,11... | collective-permute-start | bytes 1572872 | tf_op jit(solution)/shard_map/ppermute | solution.py:282
  106.0 9.0 %collective-permute-start.4 = (f32[64,512]{1,0:T(8,128)S(1)}, f32[64,512]{1,0:T(8,128)S(1)}, u32[]{:S(2)}, u32[]{:S(2)}) collective-permute-start(f32[64,512]{1,0:T(8,128)S(1)} %get-tuple-element.28), channel_id=1, source_target_pairs={{0,2},{2,0},{4,6},{6,4},{1,3},{3,1},{5,7},{7,5},{8,10},{10,8},{12,... | collective-permute-start | bytes 393224 | tf_op jit(solution)/shard_map/ppermute | solution.py:282
  108.2 7.5 %collective-permute-start.6 = (f32[64,512]{1,0:T(8,128)S(1)}, f32[64,512]{1,0:T(8,128)S(1)}, u32[]{:S(2)}, u32[]{:S(2)}) collective-permute-start(f32[64,512]{1,0:T(8,128)S(1)} %get-tuple-element.29), channel_id=1, source_target_pairs={{0,6},{2,4},{4,2},{6,0},{1,7},{3,5},{5,3},{7,1},{8,14},{10,12},{12... | collective-permute-start | bytes 393224 | tf_op jit(solution)/shard_map/ppermute | solution.py:282
  111.0 7.5 %collective-permute-start.5 = (f32[64,512]{1,0:T(8,128)S(1)}, f32[64,512]{1,0:T(8,128)S(1)}, u32[]{:S(2)}, u32[]{:S(2)}) collective-permute-start(f32[64,512]{1,0:T(8,128)S(1)} %get-tuple-element.30), channel_id=1, source_target_pairs={{0,4},{2,6},{4,0},{6,2},{1,5},{3,7},{5,1},{7,3},{8,12},{10,14},{12... | collective-permute-start | bytes 393224 | tf_op jit(solution)/shard_map/ppermute | solution.py:282
  118.5 10.6 %copy-start.3 = (bf16[64,512]{1,0:T(8,128)(2,1)}, bf16[64,512]{1,0:T(8,128)(2,1)S(1)}, u32[]{:S(2)}) copy-start(bf16[64,512]{1,0:T(8,128)(2,1)S(1)} %fusion.3.late_ref) | copy-start | bytes 196612

commit v6 on v5

--- a/solution.py
+++ b/solution.py
@@ -84,9 +84,16 @@
 def project_kernel(spot_ref, pre_ref, weight_ref, late_ref, mine_ref, theirs_ref, held_ref):
     count = mine_ref.shape[0]
     x, core = spot_ref[1], spot_ref[2]
-    act = jnp.maximum(pre_ref[...], jnp.zeros((), bf16))
-    total = jnp.dot(act, weight_ref[...], preferred_element_type=f32)
-    held_ref[...] = total.reshape(held_ref.shape)
+    rows, width = mine_ref.shape[1:]
+
+    def step(at, carry):
+        here = pl.ds(pl.multiple_of(at * 2 * rows, 2 * rows), 2 * rows)
+        act = jnp.maximum(pre_ref[here, :], jnp.zeros((), bf16))
+        total = jnp.dot(act, weight_ref[...], preferred_element_type=f32)
+        held_ref[at] = total.reshape(2, rows, width)
+        return carry
+
+    lax.fori_loop(0, count, step, 0)
     for k in range(count):
         mine_ref[k] = held_ref[x ^ k, core]
         theirs_ref[k] = held_ref[x ^ k, 1 - core]
@@ -97,24 +104,39 @@
 
 
 def first_gram_kernel(spot_ref, grads_ref, late_ref, *refs):
-    act_refs, held, out_ref = refs[:LEAVES], refs[LEAVES:-1], refs[-1]
+    act_refs, leaf_refs, out_ref = refs[:LEAVES], refs[LEAVES:-1], refs[-1]
     peers, _, rows, width = grads_ref.shape
     me = spot_ref[0]
-    for k in range(LEAVES):
-        out_grad = grads_ref[:, me ^ k].reshape(peers * rows, width)
-        held[k][...] = lax.dot_general(
-            act_refs[k][...], out_grad, (((0,), (0,)), ((), ())), preferred_element_type=f32
-        )
+    block = 128
+    pairs = [(a, b) for a in range(LEAVES) for b in range(a, LEAVES)]
+
+    def step(at, totals):
+        here = pl.ds(pl.multiple_of(at * block, block), block)
+        leaves = []
+        for k in range(LEAVES):
+            out_grad = grads_ref[:, me ^ k].reshape(peers * rows, width)
+            leaf = lax.dot_general(
+                act_refs[k][:, here], out_grad, (((0,), (0,)), ((), ())), preferred_element_type=f32
+            )
+            leaf_refs[k][here, :] = leaf
+            leaves.append(leaf)
+        added = []
+        for total, (a, b) in zip(totals, pairs):
+            product = jnp.sum((leaves[a] * leaves[b]).reshape(-1, 8, width), axis=0)
+            added.append(total + lanes_of(product))
+        return tuple(added)
+
+    totals = lax.fori_loop(
+        0, leaf_refs[0].shape[0] // block, step, tuple(jnp.zeros((8, 128), f32) for _ in pairs)
+    )
     lane = lax.broadcasted_iota(jnp.int32, (1, 128), 1)
     whole = jnp.zeros((1, 128), f32)
-    for a in range(LEAVES):
-        for b in range(a, LEAVES):
-            lanes = lanes_of(jnp.sum(held[a][...] * held[b][...], axis=0, keepdims=True))
-            value = jnp.sum(lanes, axis=1, keepdims=True)
-            here = lane == LEAVES * (a ^ me) + (b ^ me)
-            if a != b:
-                here = here | (lane == LEAVES * (b ^ me) + (a ^ me))
-            whole = jnp.where(here, value, whole)
+    for total, (a, b) in zip(totals, pairs):
+        value = jnp.sum(jnp.sum(total, axis=0, keepdims=True), axis=1, keepdims=True)
+        here = lane == LEAVES * (a ^ me) + (b ^ me)
+        if a != b:
+            here = here | (lane == LEAVES * (b ^ me) + (a ^ me))
+        whole = jnp.where(here, value, whole)
     for copy in range(out_ref.shape[0]):
         out_ref[copy] = whole
 
@@ -171,7 +193,7 @@
     node_ref[...] = merged
 
 
-def second_gram_kernel(copies, share, node_ref, nodes_ref, inverse_ref, late_ref, out_ref):
+def second_gram_kernel(copies, share, node_ref, nodes_ref, inverse_ref, late_ref, out_ref, by_node_ref):
     node = node_ref[0]
     total, width = nodes_ref.shape
     rows = total // NODES
@@ -179,16 +201,28 @@
     high = held.astype(bf16)
     low = (held - high.astype(f32)).astype(bf16)
     last = (((1,), (1,)), ((), ()))
-    products = (
-        lax.dot_general(high, high, last, preferred_element_type=f32)
-        + lax.dot_general(high, low, last, preferred_element_type=f32)
-        + lax.dot_general(low, high, last, preferred_element_type=f32)
-        + lax.dot_general(low, low, last, preferred_element_type=f32)
-    )
-    row = lax.broadcasted_iota(jnp.int32, (total, total), 0)
-    col = lax.broadcasted_iota(jnp.int32, (total, total), 1)
-    products = jnp.where((row & (rows - 1)) == (col & (rows - 1)), products, 0.0)
-    by_node = jnp.sum(products.reshape(NODES, rows, total), axis=1)
+    some = 8 * rows
+
+    def step(at, carry):
+        here = pl.ds(pl.multiple_of(at * some, some), some)
+        part = nodes_ref[here, :]
+        part_high = part.astype(bf16)
+        part_low = (part - part_high.astype(f32)).astype(bf16)
+        products = (
+            lax.dot_general(part_high, high, last, preferred_element_type=f32)
+            + lax.dot_general(part_high, low, last, preferred_element_type=f32)
+            + lax.dot_general(part_low, high, last, preferred_element_type=f32)
+            + lax.dot_general(part_low, low, last, preferred_element_type=f32)
+        )
+        row = lax.broadcasted_iota(jnp.int32, (some, total), 0)
+        col = lax.broadcasted_iota(jnp.int32, (some, total), 1)
+        products = jnp.where((row & (rows - 1)) == (col & (rows - 1)), products, 0.0)
+        found = jnp.sum(products.reshape(8, rows, total), axis=1)
+        by_node_ref[pl.ds(pl.multiple_of(at * 8, 8), 8), :] = found
+        return carry
+
+    lax.fori_loop(0, total // some, step, 0)
+    by_node = by_node_ref[...]
     source = lax.broadcasted_iota(jnp.int32, (total, 128), 0)
     lane = lax.broadcasted_iota(jnp.int32, (total, 128), 1)
     spread = jnp.where(source // rows == (lane & (NODES - 1)), 1.0, 0.0)
@@ -285,7 +319,7 @@
     grads = from_everyone(shards, mp)
     dealt = deal(me, pre_act)
     acts = {0: dealt[0]}
-    for k in (3, 2, 1):
+    for k in (2, 3, 1):
         acts[k] = swapped(dealt[k], "zl", k)
     arrived = pl.pallas_call(
         arrived_kernel,
@@ -293,7 +327,7 @@
         in_specs=[ANY] * (LEAVES - 1),
         compiler_params=pltpu.CompilerParams(vmem_limit_bytes=1024 * 1024),
         cost_estimate=pl.CostEstimate(flops=10**11, bytes_accessed=0, transcendentals=0),
-    )(acts[3], acts[2], acts[1])
+    )(acts[2], acts[3], acts[1])
 
     leaf_shape = jax.ShapeDtypeStruct((quarter, width), f32)
     group = ("zl", *mp)
@@ -333,16 +367,16 @@
     nodes = lax.all_to_all(sent, hi, split_axis=0, concat_axis=0, tiled=True).astype(f32)
     share = 1.0 / (LEAVES * peers)
     sums = call(
-        functools.partial(second_gram_kernel, peers, share),
-        jax.ShapeDtypeStruct((peers, 2, 128), f32),
+        functools.partial(second_gram_kernel, peers * along, share),
+        jax.ShapeDtypeStruct((peers * along, 2, 128), f32),
         [SMEM, VMEM, VMEM, VMEM],
         flops=8 * quarter * quarter * width,
         size=4 * quarter * width,
+        scratch=[pltpu.VMEM((NODES, quarter), f32)],
     )(node, nodes.reshape(quarter, width), inverse, projected)
-    sums = lax.all_to_all(sums, mp, split_axis=0, concat_axis=0, tiled=True)
-    dp = ("y", "zh", "zl")
-    sums = call(pass_on_kernel, jax.ShapeDtypeStruct((LEAVES * NODES, 2, 128), f32), [VMEM])(sums)
-    sums = lax.all_to_all(sums, dp, split_axis=0, concat_axis=0, tiled=True)
+    sums = lax.all_to_all(sums, ("y", *mp), split_axis=0, concat_axis=0, tiled=True)
+    sums = call(pass_on_kernel, jax.ShapeDtypeStruct((NODES, 2, 128), f32), [VMEM])(sums)
+    sums = lax.all_to_all(sums, ("zh", "zl"), split_axis=0, concat_axis=0, tiled=True)
     combined = call(
         second_merge_kernel,
         jax.ShapeDtypeStruct((rows, width), f32),

time: 162 us -> 163 us (level)
  waiting for transfers between devices: 45.5 us -> 39.7 us
  blocking collectives: 44.3 us -> 49.4 us
    ppermute x7, waiting for transfers between devices: 36.6 us -> 27.8 us  [swapped(): lax.ppermute(value, axis, [(i, i ^ apart) for i in range(lax.axis_size(ax...]
    all_to_all x1, blocking collectives: 14 us -> 19.4 us  [local(): sums = lax.all_to_all(sums, group, split_axis=0, concat_axis=0, tiled=True)]
    all_to_all x2, waiting for transfers between devices: 0.01 us -> 3.59 us  [from_everyone(): return lax.all_to_all(copies, axes, split_axis=0, concat_axis=0, tiled=True)]
  transfers between devices with their start and end apart: 10 -> 10, of which waited for: 5 -> 7; matrix products, arithmetic and copies ran while one was open for 1% -> 1% of each run, Pallas kernels for 3% -> 4%
where the time goes in v6:
time: 163 us; the launch traced here: 162 us
  starting transfers between devices  51 us (31%)
  blocking collectives  49.4 us (30%)
  waiting for transfers between devices  39.7 us (24%)
  Pallas kernels  13.4 us (8%)
  local copies, waits for them, and re-layouts  6.35 us (4%)
    ppermute x7, waiting for transfers between devices, swapped(): lax.ppermute(value, axis, [(i, i ^ apart) for i in range(lax.axis_size(ax...  27.8 us
    ppermute x7, starting transfers between devices, swapped(): lax.ppermute(value, axis, [(i, i ^ apart) for i in range(lax.axis_size(ax...  21.1 us
    all_to_all x1, blocking collectives, local(): sums = lax.all_to_all(sums, group, split_axis=0, concat_axis=0, tiled=True)  19.4 us
    all_to_all x1, blocking collectives, local(): lax.all_to_all(sums, ('zh', 'zl'), split_axis=0, concat_axis=0, tiled=True)  17.1 us
    all_to_all x1, starting transfers between devices, local(): lax.all_to_all(sent, hi, split_axis=0, concat_axis=0, tiled=True)  15.3 us
    all_to_all x2, starting transfers between devices, from_everyone(): return lax.all_to_all(copies, axes, split_axis=0, concat_axis=0, tiled=True)  14.6 us
    all_to_all x1, blocking collectives, local(): lax.all_to_all(sums, ('y', *mp), split_axis=0, concat_axis=0, tiled=True)  12.9 us
    all_to_all x1, waiting for transfers between devices, local(): lax.all_to_all(sent, hi, split_axis=0, concat_axis=0, tiled=True)  8.35 us
  transfers between devices with their start and end apart: 10, of which 7 were waited for; matrix products, arithmetic and copies ran while one was open for 1% of the time, Pallas kernels for 4%

profile of v6, /device:TPU:1, one launch (start us, length us, event | category | flops | bytes accessed | tf_op | source)
XLA Modules:
  0.0 161.9 jit_solution(7561728186317735561)
XLA Ops:
  0.6 1.6 broadcast_in_dim.6
  2.2 6.4 %all-to-all-start = ((bf16[4,64,512]{2,1,0:T(8,128)(2,1)}), bf16[4,64,512]{2,1,0:T(8,128)(2,1)S(1)}, u32[]{:S(2)}, u32[]{:S(2)}) async-start(bf16[4,64,512]{2,1,0:T(8,128)(2,1)} %broadcast_in_dim.6), calls=%async_computation | async-start | bytes 524288 | tf_op jit(solution)/shard_map/all_to_all | solution.py:39
  8.6 0.0 copy-start
  8.6 1.6 copy-done
  10.2 3.3 %shard_map.50 = (bf16[512,512]{1,0:T(8,128)(2,1)S(1)}, bf16[512,512]{1,0:T(8,128)(2,1)}, bf16[512,512]{1,0:T(8,128)(2,1)}, bf16[512,512]{1,0:T(8,128)(2,1)}) custom-call(s32[1]{0:T(128)} %bitcast.me_ref, bf16[512,2048]{1,0:T(8,128)(2,1)S(1)} %copy-done), custom_call_target="tpu_custom_call" | custom-call | flops 1073741824 | bytes 4194304 | tf_op jit(solution)/shard_map/pallas_call | solution.py:63
  13.5 4.3 %collective-permute-start = (bf16[512,512]{1,0:T(8,128)(2,1)}, bf16[512,512]{1,0:T(8,128)(2,1)S(1)}, u32[]{:S(2)}, u32[]{:S(2)}) collective-permute-start(bf16[512,512]{1,0:T(8,128)(2,1)} %get-tuple-element.15), channel_id=1, source_target_pairs={{0,16},{8,24},{16,0},{24,8},{1,17},{9,25},{17,1},{25,9},{2,18},{10... | collective-permute-start | bytes 1572872 | tf_op jit(solution)/shard_map/ppermute | solution.py:316
  17.8 3.1 %collective-permute-start.1 = (bf16[512,512]{1,0:T(8,128)(2,1)}, bf16[512,512]{1,0:T(8,128)(2,1)}, u32[]{:S(2)}, u32[]{:S(2)}) collective-permute-start(bf16[512,512]{1,0:T(8,128)(2,1)} %get-tuple-element.16), channel_id=1, source_target_pairs={{0,24},{8,16},{16,8},{24,0},{1,25},{9,17},{17,9},{25,1},{2,26},{10... | collective-permute-start | bytes 1572872 | tf_op jit(solution)/shard_map/ppermute | solution.py:316
  20.9 1.9 %collective-permute-start.2 = (bf16[512,512]{1,0:T(8,128)(2,1)}, bf16[512,512]{1,0:T(8,128)(2,1)}, u32[]{:S(2)}, u32[]{:S(2)}) collective-permute-start(bf16[512,512]{1,0:T(8,128)(2,1)} %get-tuple-element.17), channel_id=1, source_target_pairs={{0,8},{8,0},{16,24},{24,16},{1,9},{9,1},{17,25},{25,17},{2,10},{10... | collective-permute-start | bytes 1572872 | tf_op jit(solution)/shard_map/ppermute | solution.py:316
  22.8 0.1 pad_add_fusion.spot_ref
  22.9 0.0 all-to-all-done
  22.9 1.6 broadcast_in_dim.7
  24.5 8.2 %all-to-all-start.1 = ((bf16[8,4,64,512]{3,2,1,0:T(8,128)(2,1)}), bf16[8,4,64,512]{3,2,1,0:T(8,128)(2,1)S(1)}, u32[]{:S(2)}, u32[]{:S(2)}) async-start(bf16[8,4,64,512]{3,2,1,0:T(8,128)(2,1)} %broadcast_in_dim.7), calls=%async_computation.1 | async-start | bytes 4194304 | tf_op jit(solution)/shard_map/all_to_all | solution.py:39
  32.6 20.0 %collective-permute-done.refs_0_.refs_2_ = bf16[512,512]{1,0:T(8,128)(2,1)S(1)} collective-permute-done((bf16[512,512]{1,0:T(8,128)(2,1)}, bf16[512,512]{1,0:T(8,128)(2,1)S(1)}, u32[]{:S(2)}, u32[]{:S(2)}) %collective-permute-start) | collective-permute-done | bytes 524320 | tf_op jit(solution)/shard_map/ppermute | solution.py:316
  52.6 0.0 collective-permute-done.1.refs_1_.refs_3_
  52.7 2.7 %collective-permute-done.2.refs_2_.refs_1_ = bf16[512,512]{1,0:T(8,128)(2,1)} collective-permute-done((bf16[512,512]{1,0:T(8,128)(2,1)}, bf16[512,512]{1,0:T(8,128)(2,1)}, u32[]{:S(2)}, u32[]{:S(2)}) %collective-permute-start.2) | collective-permute-done | bytes 524320 | tf_op jit(solution)/shard_map/ppermute | solution.py:316
  55.4 3.6 %all-to-all-done.1.grads_ref = bf16[8,4,64,512]{3,2,1,0:T(8,128)(2,1)S(1)} async-done(((bf16[8,4,64,512]{3,2,1,0:T(8,128)(2,1)}), bf16[8,4,64,512]{3,2,1,0:T(8,128)(2,1)S(1)}, u32[]{:S(2)}, u32[]{:S(2)}) %all-to-all-start.1) | async-done | bytes 2097184 | tf_op jit(solution)/shard_map/all_to_all | solution.py:39
  59.0 3.4 %shard_map.52 = (f32[512,512]{1,0:T(8,128)S(1)}, f32[512,512]{1,0:T(8,128)S(1)}, f32[512,512]{1,0:T(8,128)S(1)}, f32[512,512]{1,0:T(8,128)S(1)}, f32[32,1,128]{2,1,0:T(1,128)S(1)}) custom-call(s32[3]{0:T(128)S(1)} %pad_add_fusion.spot_ref, bf16[8,4,64,512]{3,2,1,0:T(8,128)(2,1)S(1)} %all-to-all-done.1.grads_ref, f32[8,128]{1,0:T(8,128)S(1)} %shard_map.51.late_ref, ...), custom_call_target="tpu_custom_call" | custom-call | flops 1073741824 | bytes 4194304 | tf_op jit(solution)/shard_map/pallas_call | solution.py:334
  62.4 19.4 %all_to_all.30.sums_ref = f32[32,1,128]{2,1,0:T(1,128)S(1)} all-to-all(f32[32,1,128]{2,1,0:T(1,128)S(1)} %get-tuple-element.19), channel_id=1, replica_groups=mesh['y'=4,'zh'=4,'zl'=4,'x'=4,'c'=2] {'zl','x','c'}, dimensions={0} | all-to-all | bytes 32768 | tf_op jit(solution)/shard_map/all_to_all | solution.py:341
  81.7 0.7 shard_map.53
  82.4 0.0 copy-start.1
  82.5 0.9 convert_element_type.10
  83.4 15.3 %all-to-all-start.3 = ((f16[16,32,512]{2,1,0:T(8,128)(2,1)}), f16[16,32,512]{2,1,0:T(8,128)(2,1)S(1)}, u32[]{:S(2)}, u32[]{:S(2)}) async-start(f16[16,32,512]{2,1,0:T(8,128)(2,1)} %bitcast.8), calls=%async_computation.3 | async-start | bytes 1048576 | tf_op jit(solution)/shard_map/all_to_all | solution.py:367
  98.7 0.0 copy-done.1
  98.7 0.0 copy-start.2
  98.7 1.6 copy-done.2
  100.3 2.4 %shard_map.54 = (f32[4,64,512]{2,1,0:T(8,128)S(1)}, f32[4,64,512]{2,1,0:T(8,128)S(1)}) custom-call(s32[3]{0:T(128)S(1)} %pad_add_fusion.spot_ref, bf16[512,2048]{1,0:T(8,128)(2,1)S(1)} %copy-done.1, bf16[2048,512]{1,0:T(8,128)(2,1)S(1)} %copy-done.2, f32[8,128]{1,0:T(8,128)S(1)} %get-tuple-element.24.late_ref.inverse_ref), custom_call_target="tpu_custom_call" | custom-call | flops 1073741824 | bytes 4194304 | tf_op jit(solution)/shard_map/pallas_call | solution.py:351
  102.7 2.8 %collective-permute-start.3 = (f32[4,64,512]{2,1,0:T(8,128)S(1)}, f32[4,64,512]{2,1,0:T(8,128)S(1)}, u32[]{:S(2)}, u32[]{:S(2)}) collective-permute-start(f32[4,64,512]{2,1,0:T(8,128)S(1)} %get-tuple-element.26), channel_id=1, source_target_pairs={{0,1},{1,0},{2,3},{3,2},{4,5},{5,4},{6,7},{7,6},{8,9},{9,8},{10,11... | collective-permute-start | bytes 1572872 | tf_op jit(solution)/shard_map/ppermute | solution.py:316
  105.5 1.5 collective-permute-done.3
  107.0 0.1 add.15
  107.2 2.2 %collective-permute-start.4 = (f32[64,512]{1,0:T(8,128)S(1)}, f32[64,512]{1,0:T(8,128)S(1)}, u32[]{:S(2)}, u32[]{:S(2)}) collective-permute-start(f32[64,512]{1,0:T(8,128)S(1)} %get-tuple-element.28), channel_id=1, source_target_pairs={{0,2},{2,0},{4,6},{6,4},{1,3},{3,1},{5,7},{7,5},{8,10},{10,8},{12,... | collective-permute-start | bytes 393224 | tf_op jit(solution)/shard_map/ppermute | solution.py:316
  109.4 2.8 %collective-permute-start.6 = (f32[64,512]{1,0:T(8,128)S(1)}, f32[64,512]{1,0:T(8,128)S(1)}, u32[]{:S(2)}, u32[]{:S(2)}) collective-permute-start(f32[64,512]{1,0:T(8,128)S(1)} %get-tuple-element.29), channel_id=1, source_target_pairs={{0,6},{2,4},{4,2},{6,0},{1,7},{3,5},{5,3},{7,1},{8,14},{10,12},{12... | collective-permute-start | bytes 393224 | tf_op jit(solution)/shard_map/ppermute | solution.py:316
  112.2 4.0 %collective-permute-start.5 = (f32[64,512]{1,0:T(8,128)S(1)}, f32[64,512]{1,0:T(8,128)S(1)}, u32[]{:S(2)}, u32[]{:S(2)}) collective-permute-start(f32[64,512]{1,0:T(8,128)S(1)} %get-tuple-element.30), channel_id=1, source_target_pairs={{0,4},{2,6},{4,0},{6,2},{1,5},{3,7},{5,1},{7,3},{8,12},{10,14},{12... | collective-permute-start | bytes 393224 | tf_op jit(solution)/shard_map/ppermute | solution.py:316
  116.2 0.0 collective-permute-done.4
  116.2 0.7 collective-permute-done.6
  116.9 2.8 %collective-permute-done.5 = f32[64,512]{1,0:T(8,128)S(1)} collective-permute-done((f32[64,512]{1,0:T(8,128)S(1)}, f32[64,512]{1,0:T(8,128)S(1)}, u32[]{:S(2)}, u32[]{:S(2)}) %collective-permute-start.5) | collective-permute-done | bytes 131104 | tf_op jit(solution)/shard_map/ppermute | solution.py:316
  119.7 0.0 copy-start.3
  119.7 8.3 %all-to-all-done.3 = f16[16,32,512]{2,1,0:T(8,128)(2,1)S(1)} async-done(((f16[16,32,512]{2,1,0:T(8,128)(2,1)}), f16[16,32,512]{2,1,0:T(8,128)(2,1)S(1)}, u32[]{:S(2)}, u32[]{:S(2)}) %all-to-all-start.3) | async-done | bytes 524320 | tf_op jit(solution)/shard_map/all_to_all | solution.py:367
  128.1 0.1 convert_element_type.11.nodes_ref
  128.2 2.0 %shard_map.55 = f32[32,2,128]{2,1,0:T(2,128)S(1)} custom-call(s32[1]{0:T(128)} %bitcast.7.node_ref, f32[512,512]{1,0:T(8,128)S(1)} %bitcast.22, f32[8,128]{1,0:T(8,128)S(1)} %get-tuple-element.24.late_ref.inverse_ref, bf16[64,512]{1,0:T(8,128)(2,1)S(1)} %fusion.3.late_ref), custom_call_target="tpu_custom_call" | custom-call | flops 1073741824 | bytes 1048576 | tf_op jit(solution)/shard_map/pallas_call | solution.py:369
  130.2 0.0 copy-done.3
  130.2 12.9 %all_to_all.31.sums_ref = f32[32,2,128]{2,1,0:T(2,128)S(1)} all-to-all(f32[32,2,128]{2,1,0:T(2,128)S(1)} %shard_map.55), channel_id=1, replica_groups=mesh['y'=4,'zh'=4,'zl'=4,'x'=4,'c'=2] {'y','x','c'}, dimensions={0} | all-to-all | bytes 65536 | tf_op jit(solution)/shard_map/all_to_all | solution.py:377
  143.1 17.1 %all_to_all.32.sums_ref = f32[16,2,128]{2,1,0:T(2,128)S(1)} all-to-all(f32[16,2,128]{2,1,0:T(2,128)S(1)} %shard_map.56), channel_id=1, replica_groups=mesh['y'=4,'zh'=4,'zl'=4,'x'=4,'c'=2] {'zh','zl'}, dimensions={0} | all-to-all | bytes 32768 | tf_op jit(solution)/shard_map/all_to_all | solution.py:379
  160.2 1.6 %shard_map.57 = f32[32,512]{1,0:T(8,128)} custom-call(f32[16,2,128]{2,1,0:T(2,128)S(1)} %all_to_all.32.sums_ref, f32[16,32,512]{2,1,0:T(8,128)S(1)} %convert_element_type.11.nodes_ref), custom_call_target="tpu_custom_call" | custom-call | flops 524288 | bytes 1048576 | tf_op jit(solution)/shard_map/pallas_call | solution.py:380
  (4 shorter events, 0.1 us)
Async XLA Ops:
  2.2 20.7 %all-to-all-start = ((bf16[4,64,512]{2,1,0:T(8,128)(2,1)}), bf16[4,64,512]{2,1,0:T(8,128)(2,1)S(1)}, u32[]{:S(2)}, u32[]{:S(2)}) async-start(bf16[4,64,512]{2,1,0:T(8,128)(2,1)} %broadcast_in_dim.6), calls=%async_computation | async-start | bytes 524288 | tf_op jit(solution)/shard_map/all_to_all | solution.py:39
  8.6 1.6 copy-start
  13.5 39.2 %collective-permute-start = (bf16[512,512]{1,0:T(8,128)(2,1)}, bf16[512,512]{1,0:T(8,128)(2,1)S(1)}, u32[]{:S(2)}, u32[]{:S(2)}) collective-permute-start(bf16[512,512]{1,0:T(8,128)(2,1)} %get-tuple-element.15), channel_id=1, source_target_pairs={{0,16},{8,24},{16,0},{24,8},{1,17},{9,25},{17,1},{25,9},{2,18},{10... | collective-permute-start | bytes 1572872 | tf_op jit(solution)/shard_map/ppermute | solution.py:316
  17.8 34.9 %collective-permute-start.1 = (bf16[512,512]{1,0:T(8,128)(2,1)}, bf16[512,512]{1,0:T(8,128)(2,1)}, u32[]{:S(2)}, u32[]{:S(2)}) collective-permute-start(bf16[512,512]{1,0:T(8,128)(2,1)} %get-tuple-element.16), channel_id=1, source_target_pairs={{0,24},{8,16},{16,8},{24,0},{1,25},{9,17},{17,9},{25,1},{2,26},{10... | collective-permute-start | bytes 1572872 | tf_op jit(solution)/shard_map/ppermute | solution.py:316
  20.9 34.5 %collective-permute-start.2 = (bf16[512,512]{1,0:T(8,128)(2,1)}, bf16[512,512]{1,0:T(8,128)(2,1)}, u32[]{:S(2)}, u32[]{:S(2)}) collective-permute-start(bf16[512,512]{1,0:T(8,128)(2,1)} %get-tuple-element.17), channel_id=1, source_target_pairs={{0,8},{8,0},{16,24},{24,16},{1,9},{9,1},{17,25},{25,17},{2,10},{10... | collective-permute-start | bytes 1572872 | tf_op jit(solution)/shard_map/ppermute | solution.py:316
  24.5 34.5 %all-to-all-start.1 = ((bf16[8,4,64,512]{3,2,1,0:T(8,128)(2,1)}), bf16[8,4,64,512]{3,2,1,0:T(8,128)(2,1)S(1)}, u32[]{:S(2)}, u32[]{:S(2)}) async-start(bf16[8,4,64,512]{3,2,1,0:T(8,128)(2,1)} %broadcast_in_dim.7), calls=%async_computation.1 | async-start | bytes 4194304 | tf_op jit(solution)/shard_map/all_to_all | solution.py:39
  82.4 16.2 %copy-start.1 = (bf16[512,2048]{1,0:T(8,128)(2,1)S(1)}, bf16[512,2048]{1,0:T(8,128)(2,1)}, u32[]{:S(2)}) copy-start(bf16[512,2048]{1,0:T(8,128)(2,1)} %pre_ref.3) | copy-start | bytes 6291460
  83.4 44.7 %all-to-all-start.3 = ((f16[16,32,512]{2,1,0:T(8,128)(2,1)}), f16[16,32,512]{2,1,0:T(8,128)(2,1)S(1)}, u32[]{:S(2)}, u32[]{:S(2)}) async-start(f16[16,32,512]{2,1,0:T(8,128)(2,1)} %bitcast.8), calls=%async_computation.3 | async-start | bytes 1048576 | tf_op jit(solution)/shard_map/all_to_all | solution.py:367
  98.7 1.6 copy-start.2
  102.7 4.4 %collective-permute-start.3 = (f32[4,64,512]{2,1,0:T(8,128)S(1)}, f32[4,64,512]{2,1,0:T(8,128)S(1)}, u32[]{:S(2)}, u32[]{:S(2)}) collective-permute-start(f32[4,64,512]{2,1,0:T(8,128)S(1)} %get-tuple-element.26), channel_id=1, source_target_pairs={{0,1},{1,0},{2,3},{3,2},{4,5},{5,4},{6,7},{7,6},{8,9},{9,8},{10,11... | collective-permute-start | bytes 1572872 | tf_op jit(solution)/shard_map/ppermute | solution.py:316
  107.2 9.0 %collective-permute-start.4 = (f32[64,512]{1,0:T(8,128)S(1)}, f32[64,512]{1,0:T(8,128)S(1)}, u32[]{:S(2)}, u32[]{:S(2)}) collective-permute-start(f32[64,512]{1,0:T(8,128)S(1)} %get-tuple-element.28), channel_id=1, source_target_pairs={{0,2},{2,0},{4,6},{6,4},{1,3},{3,1},{5,7},{7,5},{8,10},{10,8},{12,... | collective-permute-start | bytes 393224 | tf_op jit(solution)/shard_map/ppermute | solution.py:316
  109.4 7.5 %collective-permute-start.6 = (f32[64,512]{1,0:T(8,128)S(1)}, f32[64,512]{1,0:T(8,128)S(1)}, u32[]{:S(2)}, u32[]{:S(2)}) collective-permute-start(f32[64,512]{1,0:T(8,128)S(1)} %get-tuple-element.29), channel_id=1, source_target_pairs={{0,6},{2,4},{4,2},{6,0},{1,7},{3,5},{5,3},{7,1},{8,14},{10,12},{12... | collective-permute-start | bytes 393224 | tf_op jit(solution)/shard_map/ppermute | solution.py:316
  112.2 7.5 %collective-permute-start.5 = (f32[64,512]{1,0:T(8,128)S(1)}, f32[64,512]{1,0:T(8,128)S(1)}, u32[]{:S(2)}, u32[]{:S(2)}) collective-permute-start(f32[64,512]{1,0:T(8,128)S(1)} %get-tuple-element.30), channel_id=1, source_target_pairs={{0,4},{2,6},{4,0},{6,2},{1,5},{3,7},{5,1},{7,3},{8,12},{10,14},{12... | collective-permute-start | bytes 393224 | tf_op jit(solution)/shard_map/ppermute | solution.py:316
  119.7 10.5 %copy-start.3 = (bf16[64,512]{1,0:T(8,128)(2,1)}, bf16[64,512]{1,0:T(8,128)(2,1)S(1)}, u32[]{:S(2)}) copy-start(bf16[64,512]{1,0:T(8,128)(2,1)S(1)} %fusion.3.late_ref) | copy-start | bytes 196612

commit v7 on v5

--- a/solution.py
+++ b/solution.py
@@ -81,11 +81,15 @@
     refs[-1][...] = jnp.zeros_like(refs[-1])
 
 
-def project_kernel(spot_ref, pre_ref, weight_ref, late_ref, mine_ref, theirs_ref, held_ref):
+def project_kernel(spot_ref, weight_ref, late_ref, *refs):
+    act_refs, (mine_ref, theirs_ref, held_ref) = refs[:LEAVES], refs[LEAVES:]
     count = mine_ref.shape[0]
-    x, core = spot_ref[1], spot_ref[2]
-    act = jnp.maximum(pre_ref[...], jnp.zeros((), bf16))
-    total = jnp.dot(act, weight_ref[...], preferred_element_type=f32)
+    me, x, core = spot_ref[0], spot_ref[1], spot_ref[2]
+    total = None
+    for k in range(LEAVES):
+        weight = weight_ref[:, me ^ k].reshape(act_refs[k].shape[1], -1)
+        part = jnp.dot(act_refs[k][...], weight, preferred_element_type=f32)
+        total = part if total is None else total + part
     held_ref[...] = total.reshape(held_ref.shape)
     for k in range(count):
         mine_ref[k] = held_ref[x ^ k, core]
@@ -285,7 +289,7 @@
     grads = from_everyone(shards, mp)
     dealt = deal(me, pre_act)
     acts = {0: dealt[0]}
-    for k in (3, 2, 1):
+    for k in (2, 3, 1):
         acts[k] = swapped(dealt[k], "zl", k)
     arrived = pl.pallas_call(
         arrived_kernel,
@@ -293,7 +297,7 @@
         in_specs=[ANY] * (LEAVES - 1),
         compiler_params=pltpu.CompilerParams(vmem_limit_bytes=1024 * 1024),
         cost_estimate=pl.CostEstimate(flops=10**11, bytes_accessed=0, transcendentals=0),
-    )(acts[3], acts[2], acts[1])
+    )(acts[2], acts[3], acts[1])
 
     leaf_shape = jax.ShapeDtypeStruct((quarter, width), f32)
     group = ("zl", *mp)
@@ -317,11 +321,11 @@
     mine, theirs = call(
         project_kernel,
         [half, half],
-        [SMEM, VMEM, VMEM, VMEM],
+        [SMEM] + [VMEM] * (LEAVES + 2),
         flops=2 * tokens * hidden * width,
         size=4 * tokens * hidden,
         scratch=[pltpu.VMEM((along, 2, tokens // peers, width), f32)],
-    )(spot, pre_act, out_weight, inverse)
+    )(spot, out_weight.reshape(NODES, LEAVES, -1, width), inverse, *dealt)
     both = mine + swapped(theirs, "c", 1)
     projected = both[0]
     for k in range(1, along):
@@ -333,16 +337,15 @@
     nodes = lax.all_to_all(sent, hi, split_axis=0, concat_axis=0, tiled=True).astype(f32)
     share = 1.0 / (LEAVES * peers)
     sums = call(
-        functools.partial(second_gram_kernel, peers, share),
-        jax.ShapeDtypeStruct((peers, 2, 128), f32),
+        functools.partial(second_gram_kernel, peers * along, share),
+        jax.ShapeDtypeStruct((peers * along, 2, 128), f32),
         [SMEM, VMEM, VMEM, VMEM],
         flops=8 * quarter * quarter * width,
         size=4 * quarter * width,
     )(node, nodes.reshape(quarter, width), inverse, projected)
-    sums = lax.all_to_all(sums, mp, split_axis=0, concat_axis=0, tiled=True)
-    dp = ("y", "zh", "zl")
-    sums = call(pass_on_kernel, jax.ShapeDtypeStruct((LEAVES * NODES, 2, 128), f32), [VMEM])(sums)
-    sums = lax.all_to_all(sums, dp, split_axis=0, concat_axis=0, tiled=True)
+    sums = lax.all_to_all(sums, ("y", *mp), split_axis=0, concat_axis=0, tiled=True)
+    sums = call(pass_on_kernel, jax.ShapeDtypeStruct((NODES, 2, 128), f32), [VMEM])(sums)
+    sums = lax.all_to_all(sums, ("zh", "zl"), split_axis=0, concat_axis=0, tiled=True)
     combined = call(
         second_merge_kernel,
         jax.ShapeDtypeStruct((rows, width), f32),

time: 162 us -> 163 us (level)
  blocking collectives: 44.3 us -> 49.4 us
  waiting for transfers between devices: 45.5 us -> 41.2 us
    ppermute x7, waiting for transfers between devices: 36.6 us -> 27.6 us  [swapped(): lax.ppermute(value, axis, [(i, i ^ apart) for i in range(lax.axis_size(ax...]
    all_to_all x1, blocking collectives: 14 us -> 19.4 us  [local(): sums = lax.all_to_all(sums, group, split_axis=0, concat_axis=0, tiled=True)]
    all_to_all x2, waiting for transfers between devices: 0.01 us -> 3.88 us  [from_everyone(): return lax.all_to_all(copies, axes, split_axis=0, concat_axis=0, tiled=True)]
  transfers between devices with their start and end apart: 10 -> 10, of which waited for: 5 -> 7; matrix products, arithmetic and copies ran while one was open for 1% -> 1% of each run, Pallas kernels for 3% -> 4%
where the time goes in v7:
time: 163 us; the launch traced here: 162 us
  starting transfers between devices  51 us (31%)
  blocking collectives  49.4 us (30%)
  waiting for transfers between devices  41.2 us (25%)
  Pallas kernels  12.7 us (8%)
  local copies, waits for them, and re-layouts  4.77 us (3%)
  other arithmetic  2.26 us (1%)
    ppermute x7, waiting for transfers between devices, swapped(): lax.ppermute(value, axis, [(i, i ^ apart) for i in range(lax.axis_size(ax...  27.6 us
    ppermute x7, starting transfers between devices, swapped(): lax.ppermute(value, axis, [(i, i ^ apart) for i in range(lax.axis_size(ax...  21.1 us
    all_to_all x1, blocking collectives, local(): sums = lax.all_to_all(sums, group, split_axis=0, concat_axis=0, tiled=True)  19.4 us
    all_to_all x1, blocking collectives, local(): lax.all_to_all(sums, ('zh', 'zl'), split_axis=0, concat_axis=0, tiled=True)  17.1 us
    all_to_all x1, starting transfers between devices, local(): lax.all_to_all(sent, hi, split_axis=0, concat_axis=0, tiled=True)  15.4 us
    all_to_all x2, starting transfers between devices, from_everyone(): return lax.all_to_all(copies, axes, split_axis=0, concat_axis=0, tiled=True)  14.6 us
    all_to_all x1, blocking collectives, local(): lax.all_to_all(sums, ('y', *mp), split_axis=0, concat_axis=0, tiled=True)  12.9 us
    all_to_all x1, waiting for transfers between devices, local(): lax.all_to_all(sent, hi, split_axis=0, concat_axis=0, tiled=True)  9.76 us
  transfers between devices with their start and end apart: 10, of which 7 were waited for; matrix products, arithmetic and copies ran while one was open for 1% of the time, Pallas kernels for 4%

profile of v7, /device:TPU:1, one launch (start us, length us, event | category | flops | bytes accessed | tf_op | source)
XLA Modules:
  0.0 162.1 jit_solution(2101343481973048787)
XLA Ops:
  0.6 1.6 broadcast_in_dim.6
  2.2 6.4 %all-to-all-start = ((bf16[4,64,512]{2,1,0:T(8,128)(2,1)}), bf16[4,64,512]{2,1,0:T(8,128)(2,1)S(1)}, u32[]{:S(2)}, u32[]{:S(2)}) async-start(bf16[4,64,512]{2,1,0:T(8,128)(2,1)} %broadcast_in_dim.6), calls=%async_computation | async-start | bytes 524288 | tf_op jit(solution)/shard_map/all_to_all | solution.py:39
  8.6 0.0 copy-start.2
  8.6 1.6 copy-done.2
  10.2 3.2 %shard_map.50 = (bf16[512,512]{1,0:T(8,128)(2,1)S(1)}, bf16[512,512]{1,0:T(8,128)(2,1)S(1)}, bf16[512,512]{1,0:T(8,128)(2,1)}, bf16[512,512]{1,0:T(8,128)(2,1)}) custom-call(s32[1]{0:T(128)} %bitcast.me_ref, bf16[512,2048]{1,0:T(8,128)(2,1)S(1)} %copy-done.2), custom_call_target="tpu_custom_call" | custom-call | flops 1073741824 | bytes 4194304 | tf_op jit(solution)/shard_map/pallas_call | solution.py:63
  13.5 4.3 %collective-permute-start = (bf16[512,512]{1,0:T(8,128)(2,1)}, bf16[512,512]{1,0:T(8,128)(2,1)}, u32[]{:S(2)}, u32[]{:S(2)}) collective-permute-start(bf16[512,512]{1,0:T(8,128)(2,1)} %get-tuple-element.15.refs_2_), channel_id=1, source_target_pairs={{0,16},{8,24},{16,0},{24,8},{1,17},{9,25},{17,1},{25,9},{2,18},{10... | collective-permute-start | bytes 1572872 | tf_op jit(solution)/shard_map/ppermute | solution.py:286
  17.7 3.1 %collective-permute-start.1 = (bf16[512,512]{1,0:T(8,128)(2,1)}, bf16[512,512]{1,0:T(8,128)(2,1)}, u32[]{:S(2)}, u32[]{:S(2)}) collective-permute-start(bf16[512,512]{1,0:T(8,128)(2,1)} %get-tuple-element.16.refs_3_), channel_id=1, source_target_pairs={{0,24},{8,16},{16,8},{24,0},{1,25},{9,17},{17,9},{25,1},{2,26},{10... | collective-permute-start | bytes 1572872 | tf_op jit(solution)/shard_map/ppermute | solution.py:286
  20.8 1.9 %collective-permute-start.2 = (bf16[512,512]{1,0:T(8,128)(2,1)S(1)}, bf16[512,512]{1,0:T(8,128)(2,1)}, u32[]{:S(2)}, u32[]{:S(2)}) collective-permute-start(bf16[512,512]{1,0:T(8,128)(2,1)S(1)} %get-tuple-element.17.refs_1_), channel_id=1, source_target_pairs={{0,8},{8,0},{16,24},{24,16},{1,9},{9,1},{17,25},{25,17},{2,10},{10... | collective-permute-start | bytes 1572872 | tf_op jit(solution)/shard_map/ppermute | solution.py:286
  22.8 0.1 pad_add_fusion.spot_ref
  22.9 0.0 all-to-all-done
  22.9 1.6 broadcast_in_dim.7
  24.4 8.2 %all-to-all-start.1 = ((bf16[8,4,64,512]{3,2,1,0:T(8,128)(2,1)}), bf16[8,4,64,512]{3,2,1,0:T(8,128)(2,1)S(1)}, u32[]{:S(2)}, u32[]{:S(2)}) async-start(bf16[8,4,64,512]{3,2,1,0:T(8,128)(2,1)} %broadcast_in_dim.7), calls=%async_computation.1 | async-start | bytes 4194304 | tf_op jit(solution)/shard_map/all_to_all | solution.py:39
  32.6 20.2 %collective-permute-done.refs_0_.refs_2_ = bf16[512,512]{1,0:T(8,128)(2,1)} collective-permute-done((bf16[512,512]{1,0:T(8,128)(2,1)}, bf16[512,512]{1,0:T(8,128)(2,1)}, u32[]{:S(2)}, u32[]{:S(2)}) %collective-permute-start) | collective-permute-done | bytes 524320 | tf_op jit(solution)/shard_map/ppermute | solution.py:286
  52.8 0.0 collective-permute-done.1.refs_1_.refs_3_
  52.8 2.3 %collective-permute-done.2.refs_2_.refs_1_ = bf16[512,512]{1,0:T(8,128)(2,1)} collective-permute-done((bf16[512,512]{1,0:T(8,128)(2,1)S(1)}, bf16[512,512]{1,0:T(8,128)(2,1)}, u32[]{:S(2)}, u32[]{:S(2)}) %collective-permute-start.2) | collective-permute-done | bytes 524320 | tf_op jit(solution)/shard_map/ppermute | solution.py:286
  55.1 3.9 %all-to-all-done.1.grads_ref = bf16[8,4,64,512]{3,2,1,0:T(8,128)(2,1)S(1)} async-done(((bf16[8,4,64,512]{3,2,1,0:T(8,128)(2,1)}), bf16[8,4,64,512]{3,2,1,0:T(8,128)(2,1)S(1)}, u32[]{:S(2)}, u32[]{:S(2)}) %all-to-all-start.1) | async-done | bytes 2097184 | tf_op jit(solution)/shard_map/all_to_all | solution.py:39
  58.9 3.0 %shard_map.52 = (f32[512,512]{1,0:T(8,128)S(1)}, f32[512,512]{1,0:T(8,128)S(1)}, f32[512,512]{1,0:T(8,128)S(1)}, f32[512,512]{1,0:T(8,128)S(1)}, f32[32,1,128]{2,1,0:T(1,128)S(1)}) custom-call(s32[3]{0:T(128)S(1)} %pad_add_fusion.spot_ref, bf16[8,4,64,512]{3,2,1,0:T(8,128)(2,1)S(1)} %all-to-all-done.1.grads_ref, f32[8,128]{1,0:T(8,128)S(1)} %shard_map.51.late_ref, ...), custom_call_target="tpu_custom_call" | custom-call | flops 1073741824 | bytes 4194304 | tf_op jit(solution)/shard_map/pallas_call | solution.py:304
  61.9 19.4 %all_to_all.30.sums_ref = f32[32,1,128]{2,1,0:T(1,128)S(1)} all-to-all(f32[32,1,128]{2,1,0:T(1,128)S(1)} %get-tuple-element.19), channel_id=1, replica_groups=mesh['y'=4,'zh'=4,'zl'=4,'x'=4,'c'=2] {'zl','x','c'}, dimensions={0} | all-to-all | bytes 32768 | tf_op jit(solution)/shard_map/all_to_all | solution.py:311
  81.3 0.7 shard_map.53
  82.0 0.0 copy-start
  82.0 0.9 convert_element_type.10
  82.9 15.4 %all-to-all-start.3 = ((f16[16,32,512]{2,1,0:T(8,128)(2,1)}), f16[16,32,512]{2,1,0:T(8,128)(2,1)}, u32[]{:S(2)}, u32[]{:S(2)}) async-start(f16[16,32,512]{2,1,0:T(8,128)(2,1)} %bitcast.25), calls=%async_computation.3 | async-start | bytes 1048576 | tf_op jit(solution)/shard_map/all_to_all | solution.py:337
  98.3 0.0 copy-done
  98.3 2.5 %shard_map.54 = (f32[4,64,512]{2,1,0:T(8,128)S(1)}, f32[4,64,512]{2,1,0:T(8,128)S(1)}) custom-call(s32[3]{0:T(128)S(1)} %pad_add_fusion.spot_ref, bf16[16,4,32,512]{3,2,1,0:T(8,128)(2,1)S(1)} %bitcast.24, f32[8,128]{1,0:T(8,128)S(1)} %get-tuple-element.24.late_ref.inverse_ref, bf16[512,512]{1,0:T(8,128)(2,1)S(1)} %get-tuple-element.18.refs_0_, ...), custom_call_target="tpu_custom_call" | custom-call | flops 1073741824 | bytes 4194304 | tf_op jit(solution)/shard_map/pallas_call | solution.py:321
  100.8 2.8 %collective-permute-start.3 = (f32[4,64,512]{2,1,0:T(8,128)S(1)}, f32[4,64,512]{2,1,0:T(8,128)S(1)}, u32[]{:S(2)}, u32[]{:S(2)}) collective-permute-start(f32[4,64,512]{2,1,0:T(8,128)S(1)} %get-tuple-element.26), channel_id=1, source_target_pairs={{0,1},{1,0},{2,3},{3,2},{4,5},{5,4},{6,7},{7,6},{8,9},{9,8},{10,11... | collective-permute-start | bytes 1572872 | tf_op jit(solution)/shard_map/ppermute | solution.py:286
  103.6 1.5 collective-permute-done.3
  105.2 0.1 add.15
  105.3 2.2 %collective-permute-start.4 = (f32[64,512]{1,0:T(8,128)S(1)}, f32[64,512]{1,0:T(8,128)S(1)}, u32[]{:S(2)}, u32[]{:S(2)}) collective-permute-start(f32[64,512]{1,0:T(8,128)S(1)} %get-tuple-element.28), channel_id=1, source_target_pairs={{0,2},{2,0},{4,6},{6,4},{1,3},{3,1},{5,7},{7,5},{8,10},{10,8},{12,... | collective-permute-start | bytes 393224 | tf_op jit(solution)/shard_map/ppermute | solution.py:286
  107.5 2.8 %collective-permute-start.6 = (f32[64,512]{1,0:T(8,128)S(1)}, f32[64,512]{1,0:T(8,128)S(1)}, u32[]{:S(2)}, u32[]{:S(2)}) collective-permute-start(f32[64,512]{1,0:T(8,128)S(1)} %get-tuple-element.29), channel_id=1, source_target_pairs={{0,6},{2,4},{4,2},{6,0},{1,7},{3,5},{5,3},{7,1},{8,14},{10,12},{12... | collective-permute-start | bytes 393224 | tf_op jit(solution)/shard_map/ppermute | solution.py:286
  110.3 4.0 %collective-permute-start.5 = (f32[64,512]{1,0:T(8,128)S(1)}, f32[64,512]{1,0:T(8,128)S(1)}, u32[]{:S(2)}, u32[]{:S(2)}) collective-permute-start(f32[64,512]{1,0:T(8,128)S(1)} %get-tuple-element.30), channel_id=1, source_target_pairs={{0,4},{2,6},{4,0},{6,2},{1,5},{3,7},{5,1},{7,3},{8,12},{10,14},{12... | collective-permute-start | bytes 393224 | tf_op jit(solution)/shard_map/ppermute | solution.py:286
  114.3 0.0 collective-permute-done.4
  114.3 0.8 collective-permute-done.6
  115.1 2.8 %collective-permute-done.5 = f32[64,512]{1,0:T(8,128)S(1)} collective-permute-done((f32[64,512]{1,0:T(8,128)S(1)}, f32[64,512]{1,0:T(8,128)S(1)}, u32[]{:S(2)}, u32[]{:S(2)}) %collective-permute-start.5) | collective-permute-done | bytes 131104 | tf_op jit(solution)/shard_map/ppermute | solution.py:286
  117.9 0.0 copy-start.1
  117.9 9.8 %all-to-all-done.3 = f16[16,32,512]{2,1,0:T(8,128)(2,1)} async-done(((f16[16,32,512]{2,1,0:T(8,128)(2,1)}), f16[16,32,512]{2,1,0:T(8,128)(2,1)}, u32[]{:S(2)}, u32[]{:S(2)}) %all-to-all-start.3) | async-done | bytes 524320 | tf_op jit(solution)/shard_map/all_to_all | solution.py:337
  127.7 1.2 convert_element_type.11.nodes_ref
  128.9 1.6 shard_map.55
  130.5 0.0 copy-done.1
  130.5 12.9 %all_to_all.31.sums_ref = f32[32,2,128]{2,1,0:T(2,128)S(1)} all-to-all(f32[32,2,128]{2,1,0:T(2,128)S(1)} %shard_map.55), channel_id=1, replica_groups=mesh['y'=4,'zh'=4,'zl'=4,'x'=4,'c'=2] {'y','x','c'}, dimensions={0} | all-to-all | bytes 65536 | tf_op jit(solution)/shard_map/all_to_all | solution.py:346
  143.4 17.1 %all_to_all.32.sums_ref = f32[16,2,128]{2,1,0:T(2,128)S(1)} all-to-all(f32[16,2,128]{2,1,0:T(2,128)S(1)} %shard_map.56), channel_id=1, replica_groups=mesh['y'=4,'zh'=4,'zl'=4,'x'=4,'c'=2] {'zh','zl'}, dimensions={0} | all-to-all | bytes 32768 | tf_op jit(solution)/shard_map/all_to_all | solution.py:348
  160.5 1.6 %shard_map.57 = f32[32,512]{1,0:T(8,128)} custom-call(f32[16,2,128]{2,1,0:T(2,128)S(1)} %all_to_all.32.sums_ref, f32[16,32,512]{2,1,0:T(8,128)S(1)} %convert_element_type.11.nodes_ref), custom_call_target="tpu_custom_call" | custom-call | flops 524288 | bytes 1048576 | tf_op jit(solution)/shard_map/pallas_call | solution.py:349
  (4 shorter events, 0.1 us)
Async XLA Ops:
  2.2 20.7 %all-to-all-start = ((bf16[4,64,512]{2,1,0:T(8,128)(2,1)}), bf16[4,64,512]{2,1,0:T(8,128)(2,1)S(1)}, u32[]{:S(2)}, u32[]{:S(2)}) async-start(bf16[4,64,512]{2,1,0:T(8,128)(2,1)} %broadcast_in_dim.6), calls=%async_computation | async-start | bytes 524288 | tf_op jit(solution)/shard_map/all_to_all | solution.py:39
  8.6 1.6 copy-start.2
  13.5 39.3 %collective-permute-start = (bf16[512,512]{1,0:T(8,128)(2,1)}, bf16[512,512]{1,0:T(8,128)(2,1)}, u32[]{:S(2)}, u32[]{:S(2)}) collective-permute-start(bf16[512,512]{1,0:T(8,128)(2,1)} %get-tuple-element.15.refs_2_), channel_id=1, source_target_pairs={{0,16},{8,24},{16,0},{24,8},{1,17},{9,25},{17,1},{25,9},{2,18},{10... | collective-permute-start | bytes 1572872 | tf_op jit(solution)/shard_map/ppermute | solution.py:286
  17.7 35.0 %collective-permute-start.1 = (bf16[512,512]{1,0:T(8,128)(2,1)}, bf16[512,512]{1,0:T(8,128)(2,1)}, u32[]{:S(2)}, u32[]{:S(2)}) collective-permute-start(bf16[512,512]{1,0:T(8,128)(2,1)} %get-tuple-element.16.refs_3_), channel_id=1, source_target_pairs={{0,24},{8,16},{16,8},{24,0},{1,25},{9,17},{17,9},{25,1},{2,26},{10... | collective-permute-start | bytes 1572872 | tf_op jit(solution)/shard_map/ppermute | solution.py:286
  20.8 34.2 %collective-permute-start.2 = (bf16[512,512]{1,0:T(8,128)(2,1)S(1)}, bf16[512,512]{1,0:T(8,128)(2,1)}, u32[]{:S(2)}, u32[]{:S(2)}) collective-permute-start(bf16[512,512]{1,0:T(8,128)(2,1)S(1)} %get-tuple-element.17.refs_1_), channel_id=1, source_target_pairs={{0,8},{8,0},{16,24},{24,16},{1,9},{9,1},{17,25},{25,17},{2,10},{10... | collective-permute-start | bytes 1572872 | tf_op jit(solution)/shard_map/ppermute | solution.py:286
  24.4 34.5 %all-to-all-start.1 = ((bf16[8,4,64,512]{3,2,1,0:T(8,128)(2,1)}), bf16[8,4,64,512]{3,2,1,0:T(8,128)(2,1)S(1)}, u32[]{:S(2)}, u32[]{:S(2)}) async-start(bf16[8,4,64,512]{3,2,1,0:T(8,128)(2,1)} %broadcast_in_dim.7), calls=%async_computation.1 | async-start | bytes 4194304 | tf_op jit(solution)/shard_map/all_to_all | solution.py:39
  82.0 16.3 %copy-start = (bf16[2048,512]{1,0:T(8,128)(2,1)S(1)}, bf16[2048,512]{1,0:T(8,128)(2,1)}, u32[]{:S(2)}) copy-start(bf16[2048,512]{1,0:T(8,128)(2,1)} %param.4) | copy-start | bytes 6291460
  82.9 44.8 %all-to-all-start.3 = ((f16[16,32,512]{2,1,0:T(8,128)(2,1)}), f16[16,32,512]{2,1,0:T(8,128)(2,1)}, u32[]{:S(2)}, u32[]{:S(2)}) async-start(f16[16,32,512]{2,1,0:T(8,128)(2,1)} %bitcast.25), calls=%async_computation.3 | async-start | bytes 1048576 | tf_op jit(solution)/shard_map/all_to_all | solution.py:337
  100.8 4.4 %collective-permute-start.3 = (f32[4,64,512]{2,1,0:T(8,128)S(1)}, f32[4,64,512]{2,1,0:T(8,128)S(1)}, u32[]{:S(2)}, u32[]{:S(2)}) collective-permute-start(f32[4,64,512]{2,1,0:T(8,128)S(1)} %get-tuple-element.26), channel_id=1, source_target_pairs={{0,1},{1,0},{2,3},{3,2},{4,5},{5,4},{6,7},{7,6},{8,9},{9,8},{10,11... | collective-permute-start | bytes 1572872 | tf_op jit(solution)/shard_map/ppermute | solution.py:286
  105.3 9.0 %collective-permute-start.4 = (f32[64,512]{1,0:T(8,128)S(1)}, f32[64,512]{1,0:T(8,128)S(1)}, u32[]{:S(2)}, u32[]{:S(2)}) collective-permute-start(f32[64,512]{1,0:T(8,128)S(1)} %get-tuple-element.28), channel_id=1, source_target_pairs={{0,2},{2,0},{4,6},{6,4},{1,3},{3,1},{5,7},{7,5},{8,10},{10,8},{12,... | collective-permute-start | bytes 393224 | tf_op jit(solution)/shard_map/ppermute | solution.py:286
  107.5 7.6 %collective-permute-start.6 = (f32[64,512]{1,0:T(8,128)S(1)}, f32[64,512]{1,0:T(8,128)S(1)}, u32[]{:S(2)}, u32[]{:S(2)}) collective-permute-start(f32[64,512]{1,0:T(8,128)S(1)} %get-tuple-element.29), channel_id=1, source_target_pairs={{0,6},{2,4},{4,2},{6,0},{1,7},{3,5},{5,3},{7,1},{8,14},{10,12},{12... | collective-permute-start | bytes 393224 | tf_op jit(solution)/shard_map/ppermute | solution.py:286
  110.3 7.6 %collective-permute-start.5 = (f32[64,512]{1,0:T(8,128)S(1)}, f32[64,512]{1,0:T(8,128)S(1)}, u32[]{:S(2)}, u32[]{:S(2)}) collective-permute-start(f32[64,512]{1,0:T(8,128)S(1)} %get-tuple-element.30), channel_id=1, source_target_pairs={{0,4},{2,6},{4,0},{6,2},{1,5},{3,7},{5,1},{7,3},{8,12},{10,14},{12... | collective-permute-start | bytes 393224 | tf_op jit(solution)/shard_map/ppermute | solution.py:286
  117.9 12.5 %copy-start.1 = (bf16[64,512]{1,0:T(8,128)(2,1)}, bf16[64,512]{1,0:T(8,128)(2,1)S(1)}, u32[]{:S(2)}) copy-start(bf16[64,512]{1,0:T(8,128)(2,1)S(1)} %fusion.3.late_ref) | copy-start | bytes 196612

commit v8 on v4

--- a/solution.py
+++ b/solution.py
@@ -47,16 +47,18 @@
     def _():
         row = lax.broadcasted_iota(jnp.int32, (width, width), 0)
         col = lax.broadcasted_iota(jnp.int32, (width, width), 1)
-        block = row >> 5
-        place = (((block & 3) ^ me_ref[0]) << 7) + ((block >> 2) << 5) + (row & 31)
-        deal_ref[...] = jnp.where(place == col, 1.0, 0.0).astype(bf16)
+        block = col >> 5
+        place = (((block & 3) ^ me_ref[0]) << 7) + ((block >> 2) << 5) + (col & 31)
+        deal_ref[...] = jnp.where(place == row, 1.0, 0.0).astype(bf16)
         for copy in range(LEAVES):
             copies_ref[copy] = grad_ref[...]
 
     part = jnp.maximum(pre_ref[...], jnp.zeros((), bf16))
-    dealt = jnp.dot(part, deal_ref[...], preferred_element_type=f32).astype(bf16)
+    dealt = lax.dot_general(
+        deal_ref[...], part, (((1,), (1,)), ((), ())), preferred_element_type=f32
+    ).astype(bf16)
     for k in range(LEAVES):
-        out_refs[k][...] = dealt[:, k * 128 : (k + 1) * 128]
+        out_refs[k][...] = dealt[k * 128 : (k + 1) * 128, :]
 
 
 def deal(me, pre_act, out_grad):
@@ -73,11 +75,11 @@
                 pl.BlockSpec((shard, width), lambda g, me: (0, 0)),
             ],
             out_specs=[pl.BlockSpec((LEAVES, shard, width), lambda g, me: (0, 0, 0))]
-            + [pl.BlockSpec((tokens, group // LEAVES), lambda g, me: (0, g))] * LEAVES,
+            + [pl.BlockSpec((group // LEAVES, tokens), lambda g, me: (g, 0))] * LEAVES,
             scratch_shapes=[pltpu.VMEM((group, group), bf16)],
         ),
         out_shape=[jax.ShapeDtypeStruct((LEAVES, shard, width), bf16)]
-        + [jax.ShapeDtypeStruct((tokens, hidden // LEAVES), bf16)] * LEAVES,
+        + [jax.ShapeDtypeStruct((hidden // LEAVES, tokens), bf16)] * LEAVES,
         compiler_params=pltpu.CompilerParams(vmem_limit_bytes=63 * 1024 * 1024),
         cost_estimate=pl.CostEstimate(
             flops=2 * tokens * hidden * group, bytes_accessed=4 * tokens * hidden, transcendentals=0
@@ -89,11 +91,17 @@
     refs[-1][...] = jnp.zeros_like(refs[-1])
 
 
-def project_kernel(spot_ref, pre_ref, weight_ref, late_ref, mine_ref, theirs_ref, held_ref):
+def project_kernel(spot_ref, weight_ref, late_ref, *refs):
+    act_refs, (mine_ref, theirs_ref, held_ref) = refs[:LEAVES], refs[LEAVES:]
     count = mine_ref.shape[0]
-    x, core = spot_ref[1], spot_ref[2]
-    act = jnp.maximum(pre_ref[...], jnp.zeros((), bf16))
-    total = jnp.dot(act, weight_ref[...], preferred_element_type=f32)
+    me, x, core = spot_ref[0], spot_ref[1], spot_ref[2]
+    total = None
+    for k in range(LEAVES):
+        weight = weight_ref[:, me ^ k].reshape(act_refs[k].shape[0], -1)
+        part = lax.dot_general(
+            act_refs[k][...], weight, (((0,), (0,)), ((), ())), preferred_element_type=f32
+        )
+        total = part if total is None else total + part
     held_ref[...] = total.reshape(held_ref.shape)
     for k in range(count):
         mine_ref[k] = held_ref[x ^ k, core]
@@ -110,9 +118,7 @@
     me = spot_ref[0]
     for k in range(LEAVES):
         out_grad = grads_ref[:, me ^ k].reshape(peers * rows, width)
-        held[k][...] = lax.dot_general(
-            act_refs[k][...], out_grad, (((0,), (0,)), ((), ())), preferred_element_type=f32
-        )
+        held[k][...] = jnp.dot(act_refs[k][...], out_grad, preferred_element_type=f32)
     lane = lax.broadcasted_iota(jnp.int32, (1, 128), 1)
     whole = jnp.zeros((1, 128), f32)
     for a in range(LEAVES):
@@ -291,7 +297,7 @@
 
     copies, *dealt = deal(me, pre_act, out_grad)
     acts = {0: dealt[0]}
-    for k in (3, 2, 1):
+    for k in (2, 1, 3):
         acts[k] = swapped(dealt[k], "zl", k)
     shards = lax.all_to_all(copies, "zl", split_axis=0, concat_axis=0, tiled=True)
     grads = from_everyone(shards, mp)
@@ -301,7 +307,7 @@
         in_specs=[ANY] * (LEAVES - 1),
         compiler_params=pltpu.CompilerParams(vmem_limit_bytes=1024 * 1024),
         cost_estimate=pl.CostEstimate(flops=10**11, bytes_accessed=0, transcendentals=0),
-    )(acts[3], acts[2], acts[1])
+    )(acts[2], acts[1], acts[3])
 
     leaf_shape = jax.ShapeDtypeStruct((quarter, width), f32)
     group = ("zl", *mp)
@@ -325,11 +331,11 @@
     mine, theirs = call(
         project_kernel,
         [half, half],
-        [SMEM, VMEM, VMEM, VMEM],
+        [SMEM] + [VMEM] * (LEAVES + 2),
         flops=2 * tokens * hidden * width,
         size=4 * tokens * hidden,
         scratch=[pltpu.VMEM((along, 2, tokens // peers, width), f32)],
-    )(spot, pre_act, out_weight, inverse)
+    )(spot, out_weight.reshape(NODES, LEAVES, -1, width), inverse, *dealt)
     both = mine + swapped(theirs, "c", 1)
     projected = both[0]
     for k in range(1, along):
@@ -341,16 +347,15 @@
     nodes = lax.all_to_all(sent, hi, split_axis=0, concat_axis=0, tiled=True).astype(f32)
     share = 1.0 / (LEAVES * peers)
     sums = call(
-        functools.partial(second_gram_kernel, peers, share),
-        jax.ShapeDtypeStruct((peers, 2, 128), f32),
+        functools.partial(second_gram_kernel, peers * along, share),
+        jax.ShapeDtypeStruct((peers * along, 2, 128), f32),
         [SMEM, VMEM, VMEM, VMEM],
         flops=8 * quarter * quarter * width,
         size=4 * quarter * width,
     )(node, nodes.reshape(quarter, width), inverse, projected)
-    sums = lax.all_to_all(sums, mp, split_axis=0, concat_axis=0, tiled=True)
-    dp = ("y", "zh", "zl")
-    sums = call(pass_on_kernel, jax.ShapeDtypeStruct((LEAVES * NODES, 2, 128), f32), [VMEM])(sums)
-    sums = lax.all_to_all(sums, dp, split_axis=0, concat_axis=0, tiled=True)
+    sums = lax.all_to_all(sums, ("y", *mp), split_axis=0, concat_axis=0, tiled=True)
+    sums = call(pass_on_kernel, jax.ShapeDtypeStruct((NODES, 2, 128), f32), [VMEM])(sums)
+    sums = lax.all_to_all(sums, ("zh", "zl"), split_axis=0, concat_axis=0, tiled=True)
     combined = call(
         second_merge_kernel,
         jax.ShapeDtypeStruct((rows, width), f32),

time: 172 us -> 163 us (0.948)
  starting transfers between devices: 70.8 us -> 60.1 us
    all_to_all x1, starting transfers between devices: 28.3 us -> 17.1 us  [from_everyone(): return lax.all_to_all(copies, axes, split_axis=0, concat_axis=0, tiled=True)]
    all_to_all x1, waiting for transfers between devices: 12.7 us -> 15.8 us  [from_everyone(): return lax.all_to_all(copies, axes, split_axis=0, concat_axis=0, tiled=True)]
    ppermute x7, waiting for transfers between devices: 18.6 us -> 15.6 us  [swapped(): lax.ppermute(value, axis, [(i, i ^ apart) for i in range(lax.axis_size(ax...]
  transfers between devices with their start and end apart: 10 -> 10, of which waited for: 6 -> 7; matrix products, arithmetic and copies ran while one was open for 1% -> 1% of each run, Pallas kernels for 1% -> 1%
where the time goes in v8:
time: 163 us; the launch traced here: 162 us
  starting transfers between devices  60.1 us (37%)
  blocking collectives  42.1 us (26%)
  waiting for transfers between devices  39.8 us (24%)
  Pallas kernels  13.3 us (8%)
  local copies, waits for them, and re-layouts  3.69 us (2%)
  other arithmetic  2.25 us (1%)
    ppermute x7, starting transfers between devices, swapped(): lax.ppermute(value, axis, [(i, i ^ apart) for i in range(lax.axis_size(ax...  21.1 us
    all_to_all x1, blocking collectives, local(): lax.all_to_all(sums, ('zh', 'zl'), split_axis=0, concat_axis=0, tiled=True)  17.1 us
    all_to_all x1, starting transfers between devices, from_everyone(): return lax.all_to_all(copies, axes, split_axis=0, concat_axis=0, tiled=True)  17.1 us
    all_to_all x1, waiting for transfers between devices, from_everyone(): return lax.all_to_all(copies, axes, split_axis=0, concat_axis=0, tiled=True)  15.8 us
    ppermute x7, waiting for transfers between devices, swapped(): lax.ppermute(value, axis, [(i, i ^ apart) for i in range(lax.axis_size(ax...  15.6 us
    all_to_all x1, starting transfers between devices, local(): lax.all_to_all(sent, hi, split_axis=0, concat_axis=0, tiled=True)  15.5 us
    all_to_all x1, blocking collectives, local(): lax.all_to_all(sums, ('y', *mp), split_axis=0, concat_axis=0, tiled=True)  12.9 us
    all_to_all x1, blocking collectives, local(): sums = lax.all_to_all(sums, group, split_axis=0, concat_axis=0, tiled=True)  12.1 us
  transfers between devices with their start and end apart: 10, of which 7 were waited for; matrix products, arithmetic and copies ran while one was open for 1% of the time, Pallas kernels for 1%

profile of v8, /device:TPU:1, one launch (start us, length us, event | category | flops | bytes accessed | tf_op | source)
XLA Modules:
  0.0 162.0 jit_solution(11700552476223223776)
XLA Ops:
  0.6 4.7 %shard_map.50 = (bf16[4,64,512]{2,1,0:T(8,128)(2,1)}, bf16[512,512]{1,0:T(8,128)(2,1)}, bf16[512,512]{1,0:T(8,128)(2,1)}, bf16[512,512]{1,0:T(8,128)(2,1)}, bf16[512,512]{1,0:T(8,128)(2,1)}) custom-call(s32[1]{0:T(128)} %bitcast.me_ref, bf16[512,2048]{1,0:T(8,128)(2,1)} %pre_ref.1, bf16[64,512]{1,0:T(8,128)(2,1)} %grad_ref.1), custom_call_target="tpu_custom_call" | custom-call | flops 1073741824 | bytes 4194304 | tf_op jit(solution)/shard_map/pallas_call | solution.py:68
  5.3 6.4 %all-to-all-start = ((bf16[4,64,512]{2,1,0:T(8,128)(2,1)}), bf16[4,64,512]{2,1,0:T(8,128)(2,1)S(1)}, u32[]{:S(2)}, u32[]{:S(2)}) async-start(bf16[4,64,512]{2,1,0:T(8,128)(2,1)} %get-tuple-element.16), calls=%async_computation | async-start | bytes 524288 | tf_op jit(solution)/shard_map/all_to_all | solution.py:302
  11.7 4.3 %collective-permute-start = (bf16[512,512]{1,0:T(8,128)(2,1)}, bf16[512,512]{1,0:T(8,128)(2,1)S(1)}, u32[]{:S(2)}, u32[]{:S(2)}) collective-permute-start(bf16[512,512]{1,0:T(8,128)(2,1)} %get-tuple-element.17.refs_2_), channel_id=1, source_target_pairs={{0,16},{8,24},{16,0},{24,8},{1,17},{9,25},{17,1},{25,9},{2,18},{10... | collective-permute-start | bytes 1572872 | tf_op jit(solution)/shard_map/ppermute | solution.py:296
  16.0 3.1 %collective-permute-start.1 = (bf16[512,512]{1,0:T(8,128)(2,1)}, bf16[512,512]{1,0:T(8,128)(2,1)}, u32[]{:S(2)}, u32[]{:S(2)}) collective-permute-start(bf16[512,512]{1,0:T(8,128)(2,1)} %get-tuple-element.18.refs_1_), channel_id=1, source_target_pairs={{0,8},{8,0},{16,24},{24,16},{1,9},{9,1},{17,25},{25,17},{2,10},{10... | collective-permute-start | bytes 1572872 | tf_op jit(solution)/shard_map/ppermute | solution.py:296
  19.1 1.9 %collective-permute-start.2 = (bf16[512,512]{1,0:T(8,128)(2,1)}, bf16[512,512]{1,0:T(8,128)(2,1)}, u32[]{:S(2)}, u32[]{:S(2)}) collective-permute-start(bf16[512,512]{1,0:T(8,128)(2,1)} %get-tuple-element.19.refs_3_), channel_id=1, source_target_pairs={{0,24},{8,16},{16,8},{24,0},{1,25},{9,17},{17,9},{25,1},{2,26},{10... | collective-permute-start | bytes 1572872 | tf_op jit(solution)/shard_map/ppermute | solution.py:296
  21.0 0.1 pad_add_fusion.spot_ref
  21.1 0.0 all-to-all-done
  21.1 1.6 broadcast_in_dim.3
  22.7 17.1 %all-to-all-start.1 = ((bf16[8,4,64,512]{3,2,1,0:T(8,128)(2,1)}), bf16[8,4,64,512]{3,2,1,0:T(8,128)(2,1)S(1)}, u32[]{:S(2)}, u32[]{:S(2)}) async-start(bf16[8,4,64,512]{3,2,1,0:T(8,128)(2,1)} %broadcast_in_dim.3), calls=%async_computation.1 | async-start | bytes 4194304 | tf_op jit(solution)/shard_map/all_to_all | solution.py:39
  39.8 0.0 copy-start
  39.8 5.1 %collective-permute-done.refs_0_.refs_2_ = bf16[512,512]{1,0:T(8,128)(2,1)S(1)} collective-permute-done((bf16[512,512]{1,0:T(8,128)(2,1)}, bf16[512,512]{1,0:T(8,128)(2,1)S(1)}, u32[]{:S(2)}, u32[]{:S(2)}) %collective-permute-start) | collective-permute-done | bytes 524320 | tf_op jit(solution)/shard_map/ppermute | solution.py:296
  44.9 0.0 collective-permute-done.1.refs_1_
  44.9 5.4 %collective-permute-done.2.refs_2_.refs_3_ = bf16[512,512]{1,0:T(8,128)(2,1)} collective-permute-done((bf16[512,512]{1,0:T(8,128)(2,1)}, bf16[512,512]{1,0:T(8,128)(2,1)}, u32[]{:S(2)}, u32[]{:S(2)}) %collective-permute-start.2) | collective-permute-done | bytes 524320 | tf_op jit(solution)/shard_map/ppermute | solution.py:296
  50.3 15.8 %all-to-all-done.1.grads_ref = bf16[8,4,64,512]{3,2,1,0:T(8,128)(2,1)S(1)} async-done(((bf16[8,4,64,512]{3,2,1,0:T(8,128)(2,1)}), bf16[8,4,64,512]{3,2,1,0:T(8,128)(2,1)S(1)}, u32[]{:S(2)}, u32[]{:S(2)}) %all-to-all-start.1) | async-done | bytes 2097184 | tf_op jit(solution)/shard_map/all_to_all | solution.py:39
  66.1 0.0 copy-done
  66.1 2.8 %shard_map.52 = (f32[512,512]{1,0:T(8,128)S(1)}, f32[512,512]{1,0:T(8,128)S(1)}, f32[512,512]{1,0:T(8,128)S(1)}, f32[512,512]{1,0:T(8,128)S(1)}, f32[32,1,128]{2,1,0:T(1,128)S(1)}) custom-call(s32[3]{0:T(128)S(1)} %pad_add_fusion.spot_ref, bf16[8,4,64,512]{3,2,1,0:T(8,128)(2,1)S(1)} %all-to-all-done.1.grads_ref, f32[8,128]{1,0:T(8,128)S(1)} %shard_map.51.late_ref, ...), custom_call_target="tpu_custom_call" | custom-call | flops 1073741824 | bytes 4194304 | tf_op jit(solution)/shard_map/pallas_call | solution.py:314
  68.9 12.1 %all_to_all.30.sums_ref = f32[32,1,128]{2,1,0:T(1,128)S(1)} all-to-all(f32[32,1,128]{2,1,0:T(1,128)S(1)} %get-tuple-element.21), channel_id=1, replica_groups=mesh['y'=4,'zh'=4,'zl'=4,'x'=4,'c'=2] {'zl','x','c'}, dimensions={0} | all-to-all | bytes 32768 | tf_op jit(solution)/shard_map/all_to_all | solution.py:321
  81.0 0.7 shard_map.53
  81.7 0.0 copy-start.1
  81.7 0.0 copy-start.2
  81.7 0.9 convert_element_type.10
  82.6 15.5 %all-to-all-start.3 = ((f16[16,32,512]{2,1,0:T(8,128)(2,1)}), f16[16,32,512]{2,1,0:T(8,128)(2,1)}, u32[]{:S(2)}, u32[]{:S(2)}) async-start(f16[16,32,512]{2,1,0:T(8,128)(2,1)} %bitcast.25), calls=%async_computation.3 | async-start | bytes 1048576 | tf_op jit(solution)/shard_map/all_to_all | solution.py:347
  98.1 0.0 copy-done.1
  98.2 0.0 copy-done.2
  98.2 0.0 copy-start.3
  98.2 1.0 copy-done.3
  99.2 0.0 copy-start.4
  99.2 1.0 copy-done.4
  100.2 1.9 %shard_map.54 = (f32[4,64,512]{2,1,0:T(8,128)S(1)}, f32[4,64,512]{2,1,0:T(8,128)S(1)}) custom-call(s32[3]{0:T(128)S(1)} %pad_add_fusion.spot_ref, bf16[16,4,32,512]{3,2,1,0:T(8,128)(2,1)S(1)} %bitcast.24, f32[8,128]{1,0:T(8,128)S(1)} %get-tuple-element.26.late_ref.inverse_ref, bf16[512,512]{1,0:T(8,128)(2,1)S(1)} %copy-done, bf16[512,512]{1,0:T(8,128)(2,1)S(1)} %copy-done.2, ...), custom_call_target="tpu_custom_call" | custom-call | flops 1073741824 | bytes 4194304 | tf_op jit(solution)/shard_map/pallas_call | solution.py:331
  102.1 2.8 %collective-permute-start.3 = (f32[4,64,512]{2,1,0:T(8,128)S(1)}, f32[4,64,512]{2,1,0:T(8,128)S(1)}, u32[]{:S(2)}, u32[]{:S(2)}) collective-permute-start(f32[4,64,512]{2,1,0:T(8,128)S(1)} %get-tuple-element.28), channel_id=1, source_target_pairs={{0,1},{1,0},{2,3},{3,2},{4,5},{5,4},{6,7},{7,6},{8,9},{9,8},{10,11... | collective-permute-start | bytes 1572872 | tf_op jit(solution)/shard_map/ppermute | solution.py:296
  105.0 1.5 collective-permute-done.3
  106.5 0.1 add.15
  106.6 2.2 %collective-permute-start.4 = (f32[64,512]{1,0:T(8,128)S(1)}, f32[64,512]{1,0:T(8,128)S(1)}, u32[]{:S(2)}, u32[]{:S(2)}) collective-permute-start(f32[64,512]{1,0:T(8,128)S(1)} %get-tuple-element.30), channel_id=1, source_target_pairs={{0,2},{2,0},{4,6},{6,4},{1,3},{3,1},{5,7},{7,5},{8,10},{10,8},{12,... | collective-permute-start | bytes 393224 | tf_op jit(solution)/shard_map/ppermute | solution.py:296
  108.8 2.8 %collective-permute-start.6 = (f32[64,512]{1,0:T(8,128)S(1)}, f32[64,512]{1,0:T(8,128)S(1)}, u32[]{:S(2)}, u32[]{:S(2)}) collective-permute-start(f32[64,512]{1,0:T(8,128)S(1)} %get-tuple-element.31), channel_id=1, source_target_pairs={{0,6},{2,4},{4,2},{6,0},{1,7},{3,5},{5,3},{7,1},{8,14},{10,12},{12... | collective-permute-start | bytes 393224 | tf_op jit(solution)/shard_map/ppermute | solution.py:296
  111.6 4.0 %collective-permute-start.5 = (f32[64,512]{1,0:T(8,128)S(1)}, f32[64,512]{1,0:T(8,128)S(1)}, u32[]{:S(2)}, u32[]{:S(2)}) collective-permute-start(f32[64,512]{1,0:T(8,128)S(1)} %get-tuple-element.32), channel_id=1, source_target_pairs={{0,4},{2,6},{4,0},{6,2},{1,5},{3,7},{5,1},{7,3},{8,12},{10,14},{12... | collective-permute-start | bytes 393224 | tf_op jit(solution)/shard_map/ppermute | solution.py:296
  115.6 0.0 collective-permute-done.4
  115.6 0.8 collective-permute-done.6
  116.4 2.8 %collective-permute-done.5 = f32[64,512]{1,0:T(8,128)S(1)} collective-permute-done((f32[64,512]{1,0:T(8,128)S(1)}, f32[64,512]{1,0:T(8,128)S(1)}, u32[]{:S(2)}, u32[]{:S(2)}) %collective-permute-start.5) | collective-permute-done | bytes 131104 | tf_op jit(solution)/shard_map/ppermute | solution.py:296
  119.3 0.0 copy-start.5
  119.3 8.3 %all-to-all-done.3 = f16[16,32,512]{2,1,0:T(8,128)(2,1)} async-done(((f16[16,32,512]{2,1,0:T(8,128)(2,1)}), f16[16,32,512]{2,1,0:T(8,128)(2,1)}, u32[]{:S(2)}, u32[]{:S(2)}) %all-to-all-start.3) | async-done | bytes 524320 | tf_op jit(solution)/shard_map/all_to_all | solution.py:347
  127.6 1.2 convert_element_type.11.nodes_ref
  128.8 1.6 shard_map.55
  130.3 0.0 copy-done.5
  130.4 12.9 %all_to_all.31.sums_ref = f32[32,2,128]{2,1,0:T(2,128)S(1)} all-to-all(f32[32,2,128]{2,1,0:T(2,128)S(1)} %shard_map.55), channel_id=1, replica_groups=mesh['y'=4,'zh'=4,'zl'=4,'x'=4,'c'=2] {'y','x','c'}, dimensions={0} | all-to-all | bytes 65536 | tf_op jit(solution)/shard_map/all_to_all | solution.py:356
  143.3 17.1 %all_to_all.32.sums_ref = f32[16,2,128]{2,1,0:T(2,128)S(1)} all-to-all(f32[16,2,128]{2,1,0:T(2,128)S(1)} %shard_map.56), channel_id=1, replica_groups=mesh['y'=4,'zh'=4,'zl'=4,'x'=4,'c'=2] {'zh','zl'}, dimensions={0} | all-to-all | bytes 32768 | tf_op jit(solution)/shard_map/all_to_all | solution.py:358
  160.4 1.6 %shard_map.57 = f32[32,512]{1,0:T(8,128)} custom-call(f32[16,2,128]{2,1,0:T(2,128)S(1)} %all_to_all.32.sums_ref, f32[16,32,512]{2,1,0:T(8,128)S(1)} %convert_element_type.11.nodes_ref), custom_call_target="tpu_custom_call" | custom-call | flops 524288 | bytes 1048576 | tf_op jit(solution)/shard_map/pallas_call | solution.py:359
  (4 shorter events, 0.1 us)
Async XLA Ops:
  5.3 15.8 %all-to-all-start = ((bf16[4,64,512]{2,1,0:T(8,128)(2,1)}), bf16[4,64,512]{2,1,0:T(8,128)(2,1)S(1)}, u32[]{:S(2)}, u32[]{:S(2)}) async-start(bf16[4,64,512]{2,1,0:T(8,128)(2,1)} %get-tuple-element.16), calls=%async_computation | async-start | bytes 524288 | tf_op jit(solution)/shard_map/all_to_all | solution.py:302
  11.7 33.2 %collective-permute-start = (bf16[512,512]{1,0:T(8,128)(2,1)}, bf16[512,512]{1,0:T(8,128)(2,1)S(1)}, u32[]{:S(2)}, u32[]{:S(2)}) collective-permute-start(bf16[512,512]{1,0:T(8,128)(2,1)} %get-tuple-element.17.refs_2_), channel_id=1, source_target_pairs={{0,16},{8,24},{16,0},{24,8},{1,17},{9,25},{17,1},{25,9},{2,18},{10... | collective-permute-start | bytes 1572872 | tf_op jit(solution)/shard_map/ppermute | solution.py:296
  16.0 28.9 %collective-permute-start.1 = (bf16[512,512]{1,0:T(8,128)(2,1)}, bf16[512,512]{1,0:T(8,128)(2,1)}, u32[]{:S(2)}, u32[]{:S(2)}) collective-permute-start(bf16[512,512]{1,0:T(8,128)(2,1)} %get-tuple-element.18.refs_1_), channel_id=1, source_target_pairs={{0,8},{8,0},{16,24},{24,16},{1,9},{9,1},{17,25},{25,17},{2,10},{10... | collective-permute-start | bytes 1572872 | tf_op jit(solution)/shard_map/ppermute | solution.py:296
  19.1 31.2 %collective-permute-start.2 = (bf16[512,512]{1,0:T(8,128)(2,1)}, bf16[512,512]{1,0:T(8,128)(2,1)}, u32[]{:S(2)}, u32[]{:S(2)}) collective-permute-start(bf16[512,512]{1,0:T(8,128)(2,1)} %get-tuple-element.19.refs_3_), channel_id=1, source_target_pairs={{0,24},{8,16},{16,8},{24,0},{1,25},{9,17},{17,9},{25,1},{2,26},{10... | collective-permute-start | bytes 1572872 | tf_op jit(solution)/shard_map/ppermute | solution.py:296
  22.7 43.4 %all-to-all-start.1 = ((bf16[8,4,64,512]{3,2,1,0:T(8,128)(2,1)}), bf16[8,4,64,512]{3,2,1,0:T(8,128)(2,1)S(1)}, u32[]{:S(2)}, u32[]{:S(2)}) async-start(bf16[8,4,64,512]{3,2,1,0:T(8,128)(2,1)} %broadcast_in_dim.3), calls=%async_computation.1 | async-start | bytes 4194304 | tf_op jit(solution)/shard_map/all_to_all | solution.py:39
  39.8 26.3 %copy-start = (bf16[512,512]{1,0:T(8,128)(2,1)S(1)}, bf16[512,512]{1,0:T(8,128)(2,1)}, u32[]{:S(2)}) copy-start(bf16[512,512]{1,0:T(8,128)(2,1)} %get-tuple-element.20.refs_0_) | copy-start | bytes 1572868
  81.7 16.4 %copy-start.1 = (bf16[2048,512]{1,0:T(8,128)(2,1)S(1)}, bf16[2048,512]{1,0:T(8,128)(2,1)}, u32[]{:S(2)}) copy-start(bf16[2048,512]{1,0:T(8,128)(2,1)} %param.4) | copy-start | bytes 6291460
  81.7 16.4 %copy-start.2 = (bf16[512,512]{1,0:T(8,128)(2,1)S(1)}, bf16[512,512]{1,0:T(8,128)(2,1)}, u32[]{:S(2)}) copy-start(bf16[512,512]{1,0:T(8,128)(2,1)} %get-tuple-element.18.refs_1_) | copy-start | bytes 1572868
  82.6 45.0 %all-to-all-start.3 = ((f16[16,32,512]{2,1,0:T(8,128)(2,1)}), f16[16,32,512]{2,1,0:T(8,128)(2,1)}, u32[]{:S(2)}, u32[]{:S(2)}) async-start(f16[16,32,512]{2,1,0:T(8,128)(2,1)} %bitcast.25), calls=%async_computation.3 | async-start | bytes 1048576 | tf_op jit(solution)/shard_map/all_to_all | solution.py:347
  98.2 1.0 copy-start.3
  99.2 1.0 copy-start.4
  102.1 4.4 %collective-permute-start.3 = (f32[4,64,512]{2,1,0:T(8,128)S(1)}, f32[4,64,512]{2,1,0:T(8,128)S(1)}, u32[]{:S(2)}, u32[]{:S(2)}) collective-permute-start(f32[4,64,512]{2,1,0:T(8,128)S(1)} %get-tuple-element.28), channel_id=1, source_target_pairs={{0,1},{1,0},{2,3},{3,2},{4,5},{5,4},{6,7},{7,6},{8,9},{9,8},{10,11... | collective-permute-start | bytes 1572872 | tf_op jit(solution)/shard_map/ppermute | solution.py:296
  106.6 9.0 %collective-permute-start.4 = (f32[64,512]{1,0:T(8,128)S(1)}, f32[64,512]{1,0:T(8,128)S(1)}, u32[]{:S(2)}, u32[]{:S(2)}) collective-permute-start(f32[64,512]{1,0:T(8,128)S(1)} %get-tuple-element.30), channel_id=1, source_target_pairs={{0,2},{2,0},{4,6},{6,4},{1,3},{3,1},{5,7},{7,5},{8,10},{10,8},{12,... | collective-permute-start | bytes 393224 | tf_op jit(solution)/shard_map/ppermute | solution.py:296
  108.8 7.6 %collective-permute-start.6 = (f32[64,512]{1,0:T(8,128)S(1)}, f32[64,512]{1,0:T(8,128)S(1)}, u32[]{:S(2)}, u32[]{:S(2)}) collective-permute-start(f32[64,512]{1,0:T(8,128)S(1)} %get-tuple-element.31), channel_id=1, source_target_pairs={{0,6},{2,4},{4,2},{6,0},{1,7},{3,5},{5,3},{7,1},{8,14},{10,12},{12... | collective-permute-start | bytes 393224 | tf_op jit(solution)/shard_map/ppermute | solution.py:296
  111.6 7.6 %collective-permute-start.5 = (f32[64,512]{1,0:T(8,128)S(1)}, f32[64,512]{1,0:T(8,128)S(1)}, u32[]{:S(2)}, u32[]{:S(2)}) collective-permute-start(f32[64,512]{1,0:T(8,128)S(1)} %get-tuple-element.32), channel_id=1, source_target_pairs={{0,4},{2,6},{4,0},{6,2},{1,5},{3,7},{5,1},{7,3},{8,12},{10,14},{12... | collective-permute-start | bytes 393224 | tf_op jit(solution)/shard_map/ppermute | solution.py:296
  119.3 11.1 %copy-start.5 = (bf16[64,512]{1,0:T(8,128)(2,1)}, bf16[64,512]{1,0:T(8,128)(2,1)S(1)}, u32[]{:S(2)}) copy-start(bf16[64,512]{1,0:T(8,128)(2,1)S(1)} %fusion.3.late_ref) | copy-start | bytes 196612

commit v9 on v7

--- a/solution.py
+++ b/solution.py
@@ -109,16 +109,19 @@
         held[k][...] = lax.dot_general(
             act_refs[k][...], out_grad, (((0,), (0,)), ((), ())), preferred_element_type=f32
         )
+    pairs = [(a, b) for a in range(LEAVES) for b in range(a, LEAVES)]
+    totals = [jnp.zeros((8, 128), f32) for _ in pairs]
+    for row in range(0, held[0].shape[0], 8):
+        strip = [leaf_ref[row : row + 8, :] for leaf_ref in held]
+        totals = [total + lanes_of(strip[a] * strip[b]) for total, (a, b) in zip(totals, pairs)]
     lane = lax.broadcasted_iota(jnp.int32, (1, 128), 1)
     whole = jnp.zeros((1, 128), f32)
-    for a in range(LEAVES):
-        for b in range(a, LEAVES):
-            lanes = lanes_of(jnp.sum(held[a][...] * held[b][...], axis=0, keepdims=True))
-            value = jnp.sum(lanes, axis=1, keepdims=True)
-            here = lane == LEAVES * (a ^ me) + (b ^ me)
-            if a != b:
-                here = here | (lane == LEAVES * (b ^ me) + (a ^ me))
-            whole = jnp.where(here, value, whole)
+    for total, (a, b) in zip(totals, pairs):
+        value = jnp.sum(jnp.sum(total, axis=0, keepdims=True), axis=1, keepdims=True)
+        here = lane == LEAVES * (a ^ me) + (b ^ me)
+        if a != b:
+            here = here | (lane == LEAVES * (b ^ me) + (a ^ me))
+        whole = jnp.where(here, value, whole)
     for copy in range(out_ref.shape[0]):
         out_ref[copy] = whole
 
@@ -289,7 +292,7 @@
     grads = from_everyone(shards, mp)
     dealt = deal(me, pre_act)
     acts = {0: dealt[0]}
-    for k in (2, 3, 1):
+    for k in (3, 2, 1):
         acts[k] = swapped(dealt[k], "zl", k)
     arrived = pl.pallas_call(
         arrived_kernel,
@@ -297,7 +300,7 @@
         in_specs=[ANY] * (LEAVES - 1),
         compiler_params=pltpu.CompilerParams(vmem_limit_bytes=1024 * 1024),
         cost_estimate=pl.CostEstimate(flops=10**11, bytes_accessed=0, transcendentals=0),
-    )(acts[2], acts[3], acts[1])
+    )(acts[3], acts[2], acts[1])
 
     leaf_shape = jax.ShapeDtypeStruct((quarter, width), f32)
     group = ("zl", *mp)

time: 163 us -> 163 us (level)
  blocking collectives: 49.4 us -> 44 us
  waiting for transfers between devices: 41.2 us -> 46.5 us
    ppermute x7, waiting for transfers between devices: 27.6 us -> 36.8 us  [swapped(): lax.ppermute(value, axis, [(i, i ^ apart) for i in range(lax.axis_size(ax...]
    all_to_all x1, blocking collectives: 19.4 us -> 14 us  [local(): sums = lax.all_to_all(sums, group, split_axis=0, concat_axis=0, tiled=True)]
    all_to_all x2, waiting for transfers between devices: 3.88 us -> 0.01 us  [from_everyone(): return lax.all_to_all(copies, axes, split_axis=0, concat_axis=0, tiled=True)]
  transfers between devices with their start and end apart: 10 -> 10, of which waited for: 7 -> 5; matrix products, arithmetic and copies ran while one was open for 1% -> 1% of each run, Pallas kernels for 4% -> 4%
where the time goes in v9:
time: 163 us; the launch traced here: 162 us
  starting transfers between devices  51.1 us (31%)
  waiting for transfers between devices  46.5 us (29%)
  blocking collectives  44 us (27%)
  Pallas kernels  12.6 us (8%)
  local copies, waits for them, and re-layouts  4.77 us (3%)
  other arithmetic  2.26 us (1%)
    ppermute x7, waiting for transfers between devices, swapped(): lax.ppermute(value, axis, [(i, i ^ apart) for i in range(lax.axis_size(ax...  36.8 us
    ppermute x7, starting transfers between devices, swapped(): lax.ppermute(value, axis, [(i, i ^ apart) for i in range(lax.axis_size(ax...  21.1 us
    all_to_all x1, blocking collectives, local(): lax.all_to_all(sums, ('zh', 'zl'), split_axis=0, concat_axis=0, tiled=True)  17.1 us
    all_to_all x1, starting transfers between devices, local(): lax.all_to_all(sent, hi, split_axis=0, concat_axis=0, tiled=True)  15.4 us
    all_to_all x2, starting transfers between devices, from_everyone(): return lax.all_to_all(copies, axes, split_axis=0, concat_axis=0, tiled=True)  14.6 us
    all_to_all x1, blocking collectives, local(): sums = lax.all_to_all(sums, group, split_axis=0, concat_axis=0, tiled=True)  14 us
    all_to_all x1, blocking collectives, local(): lax.all_to_all(sums, ('y', *mp), split_axis=0, concat_axis=0, tiled=True)  12.9 us
    all_to_all x1, waiting for transfers between devices, local(): lax.all_to_all(sent, hi, split_axis=0, concat_axis=0, tiled=True)  9.76 us
  transfers between devices with their start and end apart: 10, of which 5 were waited for; matrix products, arithmetic and copies ran while one was open for 1% of the time, Pallas kernels for 4%

profile of v9, /device:TPU:1, one launch (start us, length us, event | category | flops | bytes accessed | tf_op | source)
XLA Modules:
  0.0 162.1 jit_solution(14615204304344772514)
XLA Ops:
  0.6 1.6 broadcast_in_dim.6
  2.2 6.4 %all-to-all-start = ((bf16[4,64,512]{2,1,0:T(8,128)(2,1)}), bf16[4,64,512]{2,1,0:T(8,128)(2,1)S(1)}, u32[]{:S(2)}, u32[]{:S(2)}) async-start(bf16[4,64,512]{2,1,0:T(8,128)(2,1)} %broadcast_in_dim.6), calls=%async_computation | async-start | bytes 524288 | tf_op jit(solution)/shard_map/all_to_all | solution.py:39
  8.6 0.0 copy-start.2
  8.6 1.6 copy-done.2
  10.2 3.2 %shard_map.50 = (bf16[512,512]{1,0:T(8,128)(2,1)S(1)}, bf16[512,512]{1,0:T(8,128)(2,1)S(1)}, bf16[512,512]{1,0:T(8,128)(2,1)}, bf16[512,512]{1,0:T(8,128)(2,1)}) custom-call(s32[1]{0:T(128)} %bitcast.me_ref, bf16[512,2048]{1,0:T(8,128)(2,1)S(1)} %copy-done.2), custom_call_target="tpu_custom_call" | custom-call | flops 1073741824 | bytes 4194304 | tf_op jit(solution)/shard_map/pallas_call | solution.py:63
  13.5 5.2 %collective-permute-start = (bf16[512,512]{1,0:T(8,128)(2,1)}, bf16[512,512]{1,0:T(8,128)(2,1)}, u32[]{:S(2)}, u32[]{:S(2)}) collective-permute-start(bf16[512,512]{1,0:T(8,128)(2,1)} %get-tuple-element.15.refs_3_), channel_id=1, source_target_pairs={{0,24},{8,16},{16,8},{24,0},{1,25},{9,17},{17,9},{25,1},{2,26},{10... | collective-permute-start | bytes 1572872 | tf_op jit(solution)/shard_map/ppermute | solution.py:289
  18.6 1.9 %collective-permute-start.1 = (bf16[512,512]{1,0:T(8,128)(2,1)}, bf16[512,512]{1,0:T(8,128)(2,1)}, u32[]{:S(2)}, u32[]{:S(2)}) collective-permute-start(bf16[512,512]{1,0:T(8,128)(2,1)} %get-tuple-element.16.refs_2_), channel_id=1, source_target_pairs={{0,16},{8,24},{16,0},{24,8},{1,17},{9,25},{17,1},{25,9},{2,18},{10... | collective-permute-start | bytes 1572872 | tf_op jit(solution)/shard_map/ppermute | solution.py:289
  20.6 2.2 %collective-permute-start.2 = (bf16[512,512]{1,0:T(8,128)(2,1)S(1)}, bf16[512,512]{1,0:T(8,128)(2,1)}, u32[]{:S(2)}, u32[]{:S(2)}) collective-permute-start(bf16[512,512]{1,0:T(8,128)(2,1)S(1)} %get-tuple-element.17.refs_1_), channel_id=1, source_target_pairs={{0,8},{8,0},{16,24},{24,16},{1,9},{9,1},{17,25},{25,17},{2,10},{10... | collective-permute-start | bytes 1572872 | tf_op jit(solution)/shard_map/ppermute | solution.py:289
  22.8 0.1 pad_add_fusion.spot_ref
  22.9 0.0 all-to-all-done
  22.9 1.6 broadcast_in_dim.7
  24.4 8.2 %all-to-all-start.1 = ((bf16[8,4,64,512]{3,2,1,0:T(8,128)(2,1)}), bf16[8,4,64,512]{3,2,1,0:T(8,128)(2,1)S(1)}, u32[]{:S(2)}, u32[]{:S(2)}) async-start(bf16[8,4,64,512]{3,2,1,0:T(8,128)(2,1)} %broadcast_in_dim.7), calls=%async_computation.1 | async-start | bytes 4194304 | tf_op jit(solution)/shard_map/all_to_all | solution.py:39
  32.6 0.0 collective-permute-done.refs_0_.refs_3_
  32.6 31.7 %collective-permute-done.1.refs_1_.refs_2_ = bf16[512,512]{1,0:T(8,128)(2,1)} collective-permute-done((bf16[512,512]{1,0:T(8,128)(2,1)}, bf16[512,512]{1,0:T(8,128)(2,1)}, u32[]{:S(2)}, u32[]{:S(2)}) %collective-permute-start.1) | collective-permute-done | bytes 524320 | tf_op jit(solution)/shard_map/ppermute | solution.py:289
  64.3 0.0 collective-permute-done.2.refs_2_.refs_1_
  64.3 0.0 all-to-all-done.1.grads_ref
  64.3 2.9 %shard_map.52 = (f32[512,512]{1,0:T(8,128)S(1)}, f32[512,512]{1,0:T(8,128)S(1)}, f32[512,512]{1,0:T(8,128)S(1)}, f32[512,512]{1,0:T(8,128)S(1)}, f32[32,1,128]{2,1,0:T(1,128)S(1)}) custom-call(s32[3]{0:T(128)S(1)} %pad_add_fusion.spot_ref, bf16[8,4,64,512]{3,2,1,0:T(8,128)(2,1)S(1)} %all-to-all-done.1.grads_ref, f32[8,128]{1,0:T(8,128)S(1)} %shard_map.51.late_ref, ...), custom_call_target="tpu_custom_call" | custom-call | flops 1073741824 | bytes 4194304 | tf_op jit(solution)/shard_map/pallas_call | solution.py:307
  67.2 14.0 %all_to_all.30.sums_ref = f32[32,1,128]{2,1,0:T(1,128)S(1)} all-to-all(f32[32,1,128]{2,1,0:T(1,128)S(1)} %get-tuple-element.19), channel_id=1, replica_groups=mesh['y'=4,'zh'=4,'zl'=4,'x'=4,'c'=2] {'zl','x','c'}, dimensions={0} | all-to-all | bytes 32768 | tf_op jit(solution)/shard_map/all_to_all | solution.py:314
  81.2 0.7 shard_map.53
  81.9 0.0 copy-start
  81.9 0.9 convert_element_type.10
  82.8 15.4 %all-to-all-start.3 = ((f16[16,32,512]{2,1,0:T(8,128)(2,1)}), f16[16,32,512]{2,1,0:T(8,128)(2,1)}, u32[]{:S(2)}, u32[]{:S(2)}) async-start(f16[16,32,512]{2,1,0:T(8,128)(2,1)} %bitcast.25), calls=%async_computation.3 | async-start | bytes 1048576 | tf_op jit(solution)/shard_map/all_to_all | solution.py:340
  98.2 0.0 copy-done
  98.2 2.5 %shard_map.54 = (f32[4,64,512]{2,1,0:T(8,128)S(1)}, f32[4,64,512]{2,1,0:T(8,128)S(1)}) custom-call(s32[3]{0:T(128)S(1)} %pad_add_fusion.spot_ref, bf16[16,4,32,512]{3,2,1,0:T(8,128)(2,1)S(1)} %bitcast.24, f32[8,128]{1,0:T(8,128)S(1)} %get-tuple-element.24.late_ref.inverse_ref, bf16[512,512]{1,0:T(8,128)(2,1)S(1)} %get-tuple-element.18.refs_0_, ...), custom_call_target="tpu_custom_call" | custom-call | flops 1073741824 | bytes 4194304 | tf_op jit(solution)/shard_map/pallas_call | solution.py:324
  100.7 2.8 %collective-permute-start.3 = (f32[4,64,512]{2,1,0:T(8,128)S(1)}, f32[4,64,512]{2,1,0:T(8,128)S(1)}, u32[]{:S(2)}, u32[]{:S(2)}) collective-permute-start(f32[4,64,512]{2,1,0:T(8,128)S(1)} %get-tuple-element.26), channel_id=1, source_target_pairs={{0,1},{1,0},{2,3},{3,2},{4,5},{5,4},{6,7},{7,6},{8,9},{9,8},{10,11... | collective-permute-start | bytes 1572872 | tf_op jit(solution)/shard_map/ppermute | solution.py:289
  103.6 1.5 collective-permute-done.3
  105.1 0.1 add.15
  105.2 2.2 %collective-permute-start.4 = (f32[64,512]{1,0:T(8,128)S(1)}, f32[64,512]{1,0:T(8,128)S(1)}, u32[]{:S(2)}, u32[]{:S(2)}) collective-permute-start(f32[64,512]{1,0:T(8,128)S(1)} %get-tuple-element.28), channel_id=1, source_target_pairs={{0,2},{2,0},{4,6},{6,4},{1,3},{3,1},{5,7},{7,5},{8,10},{10,8},{12,... | collective-permute-start | bytes 393224 | tf_op jit(solution)/shard_map/ppermute | solution.py:289
  107.4 2.8 %collective-permute-start.6 = (f32[64,512]{1,0:T(8,128)S(1)}, f32[64,512]{1,0:T(8,128)S(1)}, u32[]{:S(2)}, u32[]{:S(2)}) collective-permute-start(f32[64,512]{1,0:T(8,128)S(1)} %get-tuple-element.29), channel_id=1, source_target_pairs={{0,6},{2,4},{4,2},{6,0},{1,7},{3,5},{5,3},{7,1},{8,14},{10,12},{12... | collective-permute-start | bytes 393224 | tf_op jit(solution)/shard_map/ppermute | solution.py:289
  110.2 4.0 %collective-permute-start.5 = (f32[64,512]{1,0:T(8,128)S(1)}, f32[64,512]{1,0:T(8,128)S(1)}, u32[]{:S(2)}, u32[]{:S(2)}) collective-permute-start(f32[64,512]{1,0:T(8,128)S(1)} %get-tuple-element.30), channel_id=1, source_target_pairs={{0,4},{2,6},{4,0},{6,2},{1,5},{3,7},{5,1},{7,3},{8,12},{10,14},{12... | collective-permute-start | bytes 393224 | tf_op jit(solution)/shard_map/ppermute | solution.py:289
  114.2 0.0 collective-permute-done.4
  114.2 0.8 collective-permute-done.6
  115.0 2.8 %collective-permute-done.5 = f32[64,512]{1,0:T(8,128)S(1)} collective-permute-done((f32[64,512]{1,0:T(8,128)S(1)}, f32[64,512]{1,0:T(8,128)S(1)}, u32[]{:S(2)}, u32[]{:S(2)}) %collective-permute-start.5) | collective-permute-done | bytes 131104 | tf_op jit(solution)/shard_map/ppermute | solution.py:289
  117.8 0.0 copy-start.1
  117.9 9.8 %all-to-all-done.3 = f16[16,32,512]{2,1,0:T(8,128)(2,1)} async-done(((f16[16,32,512]{2,1,0:T(8,128)(2,1)}), f16[16,32,512]{2,1,0:T(8,128)(2,1)}, u32[]{:S(2)}, u32[]{:S(2)}) %all-to-all-start.3) | async-done | bytes 524320 | tf_op jit(solution)/shard_map/all_to_all | solution.py:340
  127.6 1.2 convert_element_type.11.nodes_ref
  128.8 1.6 shard_map.55
  130.4 0.0 copy-done.1
  130.4 12.9 %all_to_all.31.sums_ref = f32[32,2,128]{2,1,0:T(2,128)S(1)} all-to-all(f32[32,2,128]{2,1,0:T(2,128)S(1)} %shard_map.55), channel_id=1, replica_groups=mesh['y'=4,'zh'=4,'zl'=4,'x'=4,'c'=2] {'y','x','c'}, dimensions={0} | all-to-all | bytes 65536 | tf_op jit(solution)/shard_map/all_to_all | solution.py:349
  143.3 17.1 %all_to_all.32.sums_ref = f32[16,2,128]{2,1,0:T(2,128)S(1)} all-to-all(f32[16,2,128]{2,1,0:T(2,128)S(1)} %shard_map.56), channel_id=1, replica_groups=mesh['y'=4,'zh'=4,'zl'=4,'x'=4,'c'=2] {'zh','zl'}, dimensions={0} | all-to-all | bytes 32768 | tf_op jit(solution)/shard_map/all_to_all | solution.py:351
  160.4 1.6 %shard_map.57 = f32[32,512]{1,0:T(8,128)} custom-call(f32[16,2,128]{2,1,0:T(2,128)S(1)} %all_to_all.32.sums_ref, f32[16,32,512]{2,1,0:T(8,128)S(1)} %convert_element_type.11.nodes_ref), custom_call_target="tpu_custom_call" | custom-call | flops 524288 | bytes 1048576 | tf_op jit(solution)/shard_map/pallas_call | solution.py:352
  (4 shorter events, 0.1 us)
Async XLA Ops:
  2.2 20.7 %all-to-all-start = ((bf16[4,64,512]{2,1,0:T(8,128)(2,1)}), bf16[4,64,512]{2,1,0:T(8,128)(2,1)S(1)}, u32[]{:S(2)}, u32[]{:S(2)}) async-start(bf16[4,64,512]{2,1,0:T(8,128)(2,1)} %broadcast_in_dim.6), calls=%async_computation | async-start | bytes 524288 | tf_op jit(solution)/shard_map/all_to_all | solution.py:39
  8.6 1.6 copy-start.2
  13.5 19.2 %collective-permute-start = (bf16[512,512]{1,0:T(8,128)(2,1)}, bf16[512,512]{1,0:T(8,128)(2,1)}, u32[]{:S(2)}, u32[]{:S(2)}) collective-permute-start(bf16[512,512]{1,0:T(8,128)(2,1)} %get-tuple-element.15.refs_3_), channel_id=1, source_target_pairs={{0,24},{8,16},{16,8},{24,0},{1,25},{9,17},{17,9},{25,1},{2,26},{10... | collective-permute-start | bytes 1572872 | tf_op jit(solution)/shard_map/ppermute | solution.py:289
  18.6 45.7 %collective-permute-start.1 = (bf16[512,512]{1,0:T(8,128)(2,1)}, bf16[512,512]{1,0:T(8,128)(2,1)}, u32[]{:S(2)}, u32[]{:S(2)}) collective-permute-start(bf16[512,512]{1,0:T(8,128)(2,1)} %get-tuple-element.16.refs_2_), channel_id=1, source_target_pairs={{0,16},{8,24},{16,0},{24,8},{1,17},{9,25},{17,1},{25,9},{2,18},{10... | collective-permute-start | bytes 1572872 | tf_op jit(solution)/shard_map/ppermute | solution.py:289
  20.6 43.7 %collective-permute-start.2 = (bf16[512,512]{1,0:T(8,128)(2,1)S(1)}, bf16[512,512]{1,0:T(8,128)(2,1)}, u32[]{:S(2)}, u32[]{:S(2)}) collective-permute-start(bf16[512,512]{1,0:T(8,128)(2,1)S(1)} %get-tuple-element.17.refs_1_), channel_id=1, source_target_pairs={{0,8},{8,0},{16,24},{24,16},{1,9},{9,1},{17,25},{25,17},{2,10},{10... | collective-permute-start | bytes 1572872 | tf_op jit(solution)/shard_map/ppermute | solution.py:289
  24.4 39.9 %all-to-all-start.1 = ((bf16[8,4,64,512]{3,2,1,0:T(8,128)(2,1)}), bf16[8,4,64,512]{3,2,1,0:T(8,128)(2,1)S(1)}, u32[]{:S(2)}, u32[]{:S(2)}) async-start(bf16[8,4,64,512]{3,2,1,0:T(8,128)(2,1)} %broadcast_in_dim.7), calls=%async_computation.1 | async-start | bytes 4194304 | tf_op jit(solution)/shard_map/all_to_all | solution.py:39
  81.9 16.3 %copy-start = (bf16[2048,512]{1,0:T(8,128)(2,1)S(1)}, bf16[2048,512]{1,0:T(8,128)(2,1)}, u32[]{:S(2)}) copy-start(bf16[2048,512]{1,0:T(8,128)(2,1)} %param.4) | copy-start | bytes 6291460
  82.8 44.8 %all-to-all-start.3 = ((f16[16,32,512]{2,1,0:T(8,128)(2,1)}), f16[16,32,512]{2,1,0:T(8,128)(2,1)}, u32[]{:S(2)}, u32[]{:S(2)}) async-start(f16[16,32,512]{2,1,0:T(8,128)(2,1)} %bitcast.25), calls=%async_computation.3 | async-start | bytes 1048576 | tf_op jit(solution)/shard_map/all_to_all | solution.py:340
  100.7 4.4 %collective-permute-start.3 = (f32[4,64,512]{2,1,0:T(8,128)S(1)}, f32[4,64,512]{2,1,0:T(8,128)S(1)}, u32[]{:S(2)}, u32[]{:S(2)}) collective-permute-start(f32[4,64,512]{2,1,0:T(8,128)S(1)} %get-tuple-element.26), channel_id=1, source_target_pairs={{0,1},{1,0},{2,3},{3,2},{4,5},{5,4},{6,7},{7,6},{8,9},{9,8},{10,11... | collective-permute-start | bytes 1572872 | tf_op jit(solution)/shard_map/ppermute | solution.py:289
  105.2 9.0 %collective-permute-start.4 = (f32[64,512]{1,0:T(8,128)S(1)}, f32[64,512]{1,0:T(8,128)S(1)}, u32[]{:S(2)}, u32[]{:S(2)}) collective-permute-start(f32[64,512]{1,0:T(8,128)S(1)} %get-tuple-element.28), channel_id=1, source_target_pairs={{0,2},{2,0},{4,6},{6,4},{1,3},{3,1},{5,7},{7,5},{8,10},{10,8},{12,... | collective-permute-start | bytes 393224 | tf_op jit(solution)/shard_map/ppermute | solution.py:289
  107.4 7.6 %collective-permute-start.6 = (f32[64,512]{1,0:T(8,128)S(1)}, f32[64,512]{1,0:T(8,128)S(1)}, u32[]{:S(2)}, u32[]{:S(2)}) collective-permute-start(f32[64,512]{1,0:T(8,128)S(1)} %get-tuple-element.29), channel_id=1, source_target_pairs={{0,6},{2,4},{4,2},{6,0},{1,7},{3,5},{5,3},{7,1},{8,14},{10,12},{12... | collective-permute-start | bytes 393224 | tf_op jit(solution)/shard_map/ppermute | solution.py:289
  110.2 7.6 %collective-permute-start.5 = (f32[64,512]{1,0:T(8,128)S(1)}, f32[64,512]{1,0:T(8,128)S(1)}, u32[]{:S(2)}, u32[]{:S(2)}) collective-permute-start(f32[64,512]{1,0:T(8,128)S(1)} %get-tuple-element.30), channel_id=1, source_target_pairs={{0,4},{2,6},{4,0},{6,2},{1,5},{3,7},{5,1},{7,3},{8,12},{10,14},{12... | collective-permute-start | bytes 393224 | tf_op jit(solution)/shard_map/ppermute | solution.py:289
  117.8 12.5 %copy-start.1 = (bf16[64,512]{1,0:T(8,128)(2,1)}, bf16[64,512]{1,0:T(8,128)(2,1)S(1)}, u32[]{:S(2)}) copy-start(bf16[64,512]{1,0:T(8,128)(2,1)S(1)} %fusion.3.late_ref) | copy-start | bytes 196612

commit v10 on v8

--- a/solution.py
+++ b/solution.py
@@ -39,7 +39,7 @@
     return lax.all_to_all(copies, axes, split_axis=0, concat_axis=0, tiled=True)
 
 
-def deal_kernel(me_ref, pre_ref, grad_ref, copies_ref, *refs):
+def deal_kernel(me_ref, pre_ref, grad_ref, copy_ref, *refs):
     out_refs, deal_ref = refs[:LEAVES], refs[LEAVES]
     width = pre_ref.shape[1]
 
@@ -50,8 +50,7 @@
         block = col >> 5
         place = (((block & 3) ^ me_ref[0]) << 7) + ((block >> 2) << 5) + (col & 31)
         deal_ref[...] = jnp.where(place == row, 1.0, 0.0).astype(bf16)
-        for copy in range(LEAVES):
-            copies_ref[copy] = grad_ref[...]
+        copy_ref[...] = grad_ref[...]
 
     part = jnp.maximum(pre_ref[...], jnp.zeros((), bf16))
     dealt = lax.dot_general(
@@ -74,11 +73,11 @@
                 pl.BlockSpec((tokens, group), lambda g, me: (0, g)),
                 pl.BlockSpec((shard, width), lambda g, me: (0, 0)),
             ],
-            out_specs=[pl.BlockSpec((LEAVES, shard, width), lambda g, me: (0, 0, 0))]
+            out_specs=[pl.BlockSpec((shard, width), lambda g, me: (0, 0))]
             + [pl.BlockSpec((group // LEAVES, tokens), lambda g, me: (g, 0))] * LEAVES,
             scratch_shapes=[pltpu.VMEM((group, group), bf16)],
         ),
-        out_shape=[jax.ShapeDtypeStruct((LEAVES, shard, width), bf16)]
+        out_shape=[jax.ShapeDtypeStruct((shard, width), bf16)]
         + [jax.ShapeDtypeStruct((hidden // LEAVES, tokens), bf16)] * LEAVES,
         compiler_params=pltpu.CompilerParams(vmem_limit_bytes=63 * 1024 * 1024),
         cost_estimate=pl.CostEstimate(
@@ -117,7 +116,7 @@
     peers, _, rows, width = grads_ref.shape
     me = spot_ref[0]
     for k in range(LEAVES):
-        out_grad = grads_ref[:, me ^ k].reshape(peers * rows, width)
+        out_grad = grads_ref[:, (0, 2, 1, 3)[k]].reshape(peers * rows, width)
         held[k][...] = jnp.dot(act_refs[k][...], out_grad, preferred_element_type=f32)
     lane = lax.broadcasted_iota(jnp.int32, (1, 128), 1)
     whole = jnp.zeros((1, 128), f32)
@@ -295,11 +294,12 @@
     def swapped(value, axis, apart):
         return lax.ppermute(value, axis, [(i, i ^ apart) for i in range(lax.axis_size(axis))])
 
-    copies, *dealt = deal(me, pre_act, out_grad)
+    copy, *dealt = deal(me, pre_act, out_grad)
     acts = {0: dealt[0]}
     for k in (2, 1, 3):
         acts[k] = swapped(dealt[k], "zl", k)
-    shards = lax.all_to_all(copies, "zl", split_axis=0, concat_axis=0, tiled=True)
+    pair = jnp.stack([copy, swapped(copy, "zl", 2)])
+    shards = jnp.concatenate([pair, swapped(pair, "zl", 1)])
     grads = from_everyone(shards, mp)
     arrived = pl.pallas_call(
         arrived_kernel,

time: 163 us -> 200 us (1.23)
  waiting for transfers between devices: 39.8 us -> 80.8 us
  starting transfers between devices: 60.1 us -> 52.1 us
    ppermute x7 -> x9, waiting for transfers between devices: 15.6 us -> 46.2 us  [swapped(): lax.ppermute(value, axis, [(i, i ^ apart) for i in range(lax.axis_size(ax...]
    all_to_all x1, waiting for transfers between devices: 15.8 us -> 26.3 us  [from_everyone(): return lax.all_to_all(copies, axes, split_axis=0, concat_axis=0, tiled=True)]
    all_to_all x1, starting transfers between devices: 17.1 us -> 6.85 us  [from_everyone(): return lax.all_to_all(copies, axes, split_axis=0, concat_axis=0, tiled=True)]
    ppermute x7 -> x9, starting transfers between devices: 21.1 us -> 30.2 us  [swapped(): lax.ppermute(value, axis, [(i, i ^ apart) for i in range(lax.axis_size(ax...]
    all_to_all x1 -> x0, starting transfers between devices: 6.44 us -> none  [local(): lax.all_to_all(copies, 'zl', split_axis=0, concat_axis=0, tiled=True)]
  transfers between devices with their start and end apart: 10 -> 11, of which waited for: 7 -> 7; matrix products, arithmetic and copies ran while one was open for 1% -> 2% of each run, Pallas kernels for 1% -> 1%
where the time goes in v10:
time: 200 us; the launch traced here: 199 us
  waiting for transfers between devices  80.8 us (40%)
  starting transfers between devices  52.1 us (26%)
  blocking collectives  44 us (22%)
  Pallas kernels  13.3 us (7%)
  other arithmetic  3.97 us (2%)
  local copies, waits for them, and re-layouts  3.69 us (2%)
    ppermute x9, waiting for transfers between devices, swapped(): lax.ppermute(value, axis, [(i, i ^ apart) for i in range(lax.axis_size(ax...  46.2 us
    ppermute x9, starting transfers between devices, swapped(): lax.ppermute(value, axis, [(i, i ^ apart) for i in range(lax.axis_size(ax...  30.2 us
    all_to_all x1, waiting for transfers between devices, from_everyone(): return lax.all_to_all(copies, axes, split_axis=0, concat_axis=0, tiled=True)  26.3 us
    all_to_all x1, blocking collectives, local(): lax.all_to_all(sums, ('zh', 'zl'), split_axis=0, concat_axis=0, tiled=True)  17.1 us
    all_to_all x1, starting transfers between devices, local(): lax.all_to_all(sent, hi, split_axis=0, concat_axis=0, tiled=True)  15 us
    all_to_all x1, blocking collectives, local(): sums = lax.all_to_all(sums, group, split_axis=0, concat_axis=0, tiled=True)  14 us
    all_to_all x1, blocking collectives, local(): lax.all_to_all(sums, ('y', *mp), split_axis=0, concat_axis=0, tiled=True)  12.9 us
    all_to_all x1, waiting for transfers between devices, local(): lax.all_to_all(sent, hi, split_axis=0, concat_axis=0, tiled=True)  8.33 us
  transfers between devices with their start and end apart: 11, of which 7 were waited for; matrix products, arithmetic and copies ran while one was open for 2% of the time, Pallas kernels for 1%

profile of v10, /device:TPU:1, one launch (start us, length us, event | category | flops | bytes accessed | tf_op | source)
XLA Modules:
  0.0 198.8 jit_solution(11350973230364910413)
XLA Ops:
  0.6 4.6 %shard_map.50 = (bf16[64,512]{1,0:T(8,128)(2,1)}, bf16[512,512]{1,0:T(8,128)(2,1)}, bf16[512,512]{1,0:T(8,128)(2,1)}, bf16[512,512]{1,0:T(8,128)(2,1)}, bf16[512,512]{1,0:T(8,128)(2,1)}) custom-call(s32[1]{0:T(128)} %bitcast.me_ref, bf16[512,2048]{1,0:T(8,128)(2,1)} %pre_ref.1, bf16[64,512]{1,0:T(8,128)(2,1)} %grad_ref.1), custom_call_target="tpu_custom_call" | custom-call | flops 1073741824 | bytes 4194304 | tf_op jit(solution)/shard_map/pallas_call | solution.py:67
  5.2 5.7 %collective-permute-start.2 = (bf16[512,512]{1,0:T(8,128)(2,1)}, bf16[512,512]{1,0:T(8,128)(2,1)S(1)}, u32[]{:S(2)}, u32[]{:S(2)}) collective-permute-start(bf16[512,512]{1,0:T(8,128)(2,1)} %get-tuple-element.17.refs_2_), channel_id=1, source_target_pairs={{0,16},{8,24},{16,0},{24,8},{1,17},{9,25},{17,1},{25,9},{2,18},{10... | collective-permute-start | bytes 1572872 | tf_op jit(solution)/shard_map/ppermute | solution.py:295
  11.0 3.5 %collective-permute-start.3 = (bf16[512,512]{1,0:T(8,128)(2,1)}, bf16[512,512]{1,0:T(8,128)(2,1)}, u32[]{:S(2)}, u32[]{:S(2)}) collective-permute-start(bf16[512,512]{1,0:T(8,128)(2,1)} %get-tuple-element.18.refs_1_), channel_id=1, source_target_pairs={{0,8},{8,0},{16,24},{24,16},{1,9},{9,1},{17,25},{25,17},{2,10},{10... | collective-permute-start | bytes 1572872 | tf_op jit(solution)/shard_map/ppermute | solution.py:295
  14.5 1.9 collective-permute-start.4
  16.5 3.1 %collective-permute-start = (bf16[64,512]{1,0:T(8,128)(2,1)}, bf16[64,512]{1,0:T(8,128)(2,1)S(1)}, u32[]{:S(2)}, u32[]{:S(2)}) collective-permute-start(bf16[64,512]{1,0:T(8,128)(2,1)} %get-tuple-element.16), channel_id=1, source_target_pairs={{0,16},{8,24},{16,0},{24,8},{1,17},{9,25},{17,1},{25,9},{2,18},{10... | collective-permute-start | bytes 196616 | tf_op jit(solution)/shard_map/ppermute | solution.py:295
  19.6 38.8 %collective-permute-done = bf16[64,512]{1,0:T(8,128)(2,1)S(1)} collective-permute-done((bf16[64,512]{1,0:T(8,128)(2,1)}, bf16[64,512]{1,0:T(8,128)(2,1)S(1)}, u32[]{:S(2)}, u32[]{:S(2)}) %collective-permute-start) | collective-permute-done | bytes 65568 | tf_op jit(solution)/shard_map/ppermute | solution.py:295
  58.4 0.9 pad_maximum_fusion.1
  59.2 4.2 %collective-permute-start.1 = (bf16[2,64,512]{2,1,0:T(8,128)(2,1)S(1)}, bf16[2,64,512]{2,1,0:T(8,128)(2,1)S(1)}, u32[]{:S(2)}, u32[]{:S(2)}) collective-permute-start(bf16[2,64,512]{2,1,0:T(8,128)(2,1)S(1)} %pad_maximum_fusion.1), channel_id=1, source_target_pairs={{0,8},{8,0},{16,24},{24,16},{1,9},{9,1},{17,25},{25,17},{2,10},{10... | collective-permute-start | bytes 393224 | tf_op jit(solution)/shard_map/ppermute | solution.py:295
  63.4 0.1 pad_add_fusion.spot_ref
  63.5 2.3 %collective-permute-done.1 = bf16[2,64,512]{2,1,0:T(8,128)(2,1)S(1)} collective-permute-done((bf16[2,64,512]{2,1,0:T(8,128)(2,1)S(1)}, bf16[2,64,512]{2,1,0:T(8,128)(2,1)S(1)}, u32[]{:S(2)}, u32[]{:S(2)}) %collective-permute-start.1) | collective-permute-done | bytes 131104 | tf_op jit(solution)/shard_map/ppermute | solution.py:295
  65.8 0.9 pad_maximum_fusion
  66.6 1.6 broadcast_in_dim.3
  68.2 6.8 %all-to-all-start = ((bf16[8,4,64,512]{3,2,1,0:T(8,128)(2,1)}), bf16[8,4,64,512]{3,2,1,0:T(8,128)(2,1)S(1)}, u32[]{:S(2)}, u32[]{:S(2)}) async-start(bf16[8,4,64,512]{3,2,1,0:T(8,128)(2,1)} %broadcast_in_dim.3), calls=%async_computation | async-start | bytes 4194304 | tf_op jit(solution)/shard_map/all_to_all | solution.py:39
  75.1 0.0 collective-permute-done.2.refs_0_.refs_2_
  75.1 0.0 collective-permute-done.3.refs_1_
  75.1 0.0 collective-permute-done.4.refs_2_.refs_3_
  75.1 26.3 %all-to-all-done.grads_ref = bf16[8,4,64,512]{3,2,1,0:T(8,128)(2,1)S(1)} async-done(((bf16[8,4,64,512]{3,2,1,0:T(8,128)(2,1)}), bf16[8,4,64,512]{3,2,1,0:T(8,128)(2,1)S(1)}, u32[]{:S(2)}, u32[]{:S(2)}) %all-to-all-start) | async-done | bytes 2097184 | tf_op jit(solution)/shard_map/all_to_all | solution.py:39
  101.4 0.0 copy-done
  101.4 2.8 %shard_map.52 = (f32[512,512]{1,0:T(8,128)S(1)}, f32[512,512]{1,0:T(8,128)S(1)}, f32[512,512]{1,0:T(8,128)S(1)}, f32[512,512]{1,0:T(8,128)S(1)}, f32[32,1,128]{2,1,0:T(1,128)S(1)}) custom-call(s32[3]{0:T(128)S(1)} %pad_add_fusion.spot_ref, bf16[8,4,64,512]{3,2,1,0:T(8,128)(2,1)S(1)} %all-to-all-done.grads_ref, f32[8,128]{1,0:T(8,128)S(1)} %shard_map.51.late_ref, ...), custom_call_target="tpu_custom_call" | custom-call | flops 1073741824 | bytes 4194304 | tf_op jit(solution)/shard_map/pallas_call | solution.py:314
  104.2 14.0 %all_to_all.25.sums_ref = f32[32,1,128]{2,1,0:T(1,128)S(1)} all-to-all(f32[32,1,128]{2,1,0:T(1,128)S(1)} %get-tuple-element.21), channel_id=1, replica_groups=mesh['y'=4,'zh'=4,'zl'=4,'x'=4,'c'=2] {'zl','x','c'}, dimensions={0} | all-to-all | bytes 32768 | tf_op jit(solution)/shard_map/all_to_all | solution.py:321
  118.2 0.7 shard_map.53
  118.9 0.0 copy-start.1
  118.9 0.0 copy-start.2
  118.9 0.9 convert_element_type.10
  119.8 15.0 %all-to-all-start.2 = ((f16[16,32,512]{2,1,0:T(8,128)(2,1)}), f16[16,32,512]{2,1,0:T(8,128)(2,1)}, u32[]{:S(2)}, u32[]{:S(2)}) async-start(f16[16,32,512]{2,1,0:T(8,128)(2,1)} %bitcast.27), calls=%async_computation.2 | async-start | bytes 1048576 | tf_op jit(solution)/shard_map/all_to_all | solution.py:347
  134.9 0.0 copy-done.1
  134.9 0.0 copy-done.2
  134.9 0.0 copy-start.3
  134.9 1.0 copy-done.3
  135.9 1.0 copy-done.4
  137.0 1.9 shard_map.54
  138.9 2.8 %collective-permute-start.5 = (f32[4,64,512]{2,1,0:T(8,128)S(1)}, f32[4,64,512]{2,1,0:T(8,128)S(1)}, u32[]{:S(2)}, u32[]{:S(2)}) collective-permute-start(f32[4,64,512]{2,1,0:T(8,128)S(1)} %get-tuple-element.28), channel_id=1, source_target_pairs={{0,1},{1,0},{2,3},{3,2},{4,5},{5,4},{6,7},{7,6},{8,9},{9,8},{10,11... | collective-permute-start | bytes 1572872 | tf_op jit(solution)/shard_map/ppermute | solution.py:295
  141.7 1.5 collective-permute-done.5
  143.2 0.1 add.15
  143.3 2.2 %collective-permute-start.6 = (f32[64,512]{1,0:T(8,128)S(1)}, f32[64,512]{1,0:T(8,128)S(1)}, u32[]{:S(2)}, u32[]{:S(2)}) collective-permute-start(f32[64,512]{1,0:T(8,128)S(1)} %get-tuple-element.30), channel_id=1, source_target_pairs={{0,2},{2,0},{4,6},{6,4},{1,3},{3,1},{5,7},{7,5},{8,10},{10,8},{12,... | collective-permute-start | bytes 393224 | tf_op jit(solution)/shard_map/ppermute | solution.py:295
  145.5 2.8 %collective-permute-start.8 = (f32[64,512]{1,0:T(8,128)S(1)}, f32[64,512]{1,0:T(8,128)S(1)}, u32[]{:S(2)}, u32[]{:S(2)}) collective-permute-start(f32[64,512]{1,0:T(8,128)S(1)} %get-tuple-element.31), channel_id=1, source_target_pairs={{0,6},{2,4},{4,2},{6,0},{1,7},{3,5},{5,3},{7,1},{8,14},{10,12},{12... | collective-permute-start | bytes 393224 | tf_op jit(solution)/shard_map/ppermute | solution.py:295
  148.3 4.0 %collective-permute-start.7 = (f32[64,512]{1,0:T(8,128)S(1)}, f32[64,512]{1,0:T(8,128)S(1)}, u32[]{:S(2)}, u32[]{:S(2)}) collective-permute-start(f32[64,512]{1,0:T(8,128)S(1)} %get-tuple-element.32), channel_id=1, source_target_pairs={{0,4},{2,6},{4,0},{6,2},{1,5},{3,7},{5,1},{7,3},{8,12},{10,14},{12... | collective-permute-start | bytes 393224 | tf_op jit(solution)/shard_map/ppermute | solution.py:295
  152.3 0.0 collective-permute-done.6
  152.4 0.8 collective-permute-done.8
  153.1 2.8 %collective-permute-done.7 = f32[64,512]{1,0:T(8,128)S(1)} collective-permute-done((f32[64,512]{1,0:T(8,128)S(1)}, f32[64,512]{1,0:T(8,128)S(1)}, u32[]{:S(2)}, u32[]{:S(2)}) %collective-permute-start.7) | collective-permute-done | bytes 131104 | tf_op jit(solution)/shard_map/ppermute | solution.py:295
  156.0 0.0 copy-start.5
  156.0 8.3 %all-to-all-done.2 = f16[16,32,512]{2,1,0:T(8,128)(2,1)} async-done(((f16[16,32,512]{2,1,0:T(8,128)(2,1)}), f16[16,32,512]{2,1,0:T(8,128)(2,1)}, u32[]{:S(2)}, u32[]{:S(2)}) %all-to-all-start.2) | async-done | bytes 524320 | tf_op jit(solution)/shard_map/all_to_all | solution.py:347
  164.3 1.2 convert_element_type.11.nodes_ref
  165.5 1.6 shard_map.55
  167.1 0.0 copy-done.5
  167.1 12.9 %all_to_all.26.sums_ref = f32[32,2,128]{2,1,0:T(2,128)S(1)} all-to-all(f32[32,2,128]{2,1,0:T(2,128)S(1)} %shard_map.55), channel_id=1, replica_groups=mesh['y'=4,'zh'=4,'zl'=4,'x'=4,'c'=2] {'y','x','c'}, dimensions={0} | all-to-all | bytes 65536 | tf_op jit(solution)/shard_map/all_to_all | solution.py:356
  180.0 17.1 %all_to_all.27.sums_ref = f32[16,2,128]{2,1,0:T(2,128)S(1)} all-to-all(f32[16,2,128]{2,1,0:T(2,128)S(1)} %shard_map.56), channel_id=1, replica_groups=mesh['y'=4,'zh'=4,'zl'=4,'x'=4,'c'=2] {'zh','zl'}, dimensions={0} | all-to-all | bytes 32768 | tf_op jit(solution)/shard_map/all_to_all | solution.py:358
  197.1 1.6 shard_map.57
  (6 shorter events, 0.1 us)
Async XLA Ops:
  5.2 69.8 %collective-permute-start.2 = (bf16[512,512]{1,0:T(8,128)(2,1)}, bf16[512,512]{1,0:T(8,128)(2,1)S(1)}, u32[]{:S(2)}, u32[]{:S(2)}) collective-permute-start(bf16[512,512]{1,0:T(8,128)(2,1)} %get-tuple-element.17.refs_2_), channel_id=1, source_target_pairs={{0,16},{8,24},{16,0},{24,8},{1,17},{9,25},{17,1},{25,9},{2,18},{10... | collective-permute-start | bytes 1572872 | tf_op jit(solution)/shard_map/ppermute | solution.py:295
  11.0 64.1 %collective-permute-start.3 = (bf16[512,512]{1,0:T(8,128)(2,1)}, bf16[512,512]{1,0:T(8,128)(2,1)}, u32[]{:S(2)}, u32[]{:S(2)}) collective-permute-start(bf16[512,512]{1,0:T(8,128)(2,1)} %get-tuple-element.18.refs_1_), channel_id=1, source_target_pairs={{0,8},{8,0},{16,24},{24,16},{1,9},{9,1},{17,25},{25,17},{2,10},{10... | collective-permute-start | bytes 1572872 | tf_op jit(solution)/shard_map/ppermute | solution.py:295
  14.5 60.6 %collective-permute-start.4 = (bf16[512,512]{1,0:T(8,128)(2,1)}, bf16[512,512]{1,0:T(8,128)(2,1)}, u32[]{:S(2)}, u32[]{:S(2)}) collective-permute-start(bf16[512,512]{1,0:T(8,128)(2,1)} %get-tuple-element.19.refs_3_), channel_id=1, source_target_pairs={{0,24},{8,16},{16,8},{24,0},{1,25},{9,17},{17,9},{25,1},{2,26},{10... | collective-permute-start | bytes 1572872 | tf_op jit(solution)/shard_map/ppermute | solution.py:295
  16.5 41.9 %collective-permute-start = (bf16[64,512]{1,0:T(8,128)(2,1)}, bf16[64,512]{1,0:T(8,128)(2,1)S(1)}, u32[]{:S(2)}, u32[]{:S(2)}) collective-permute-start(bf16[64,512]{1,0:T(8,128)(2,1)} %get-tuple-element.16), channel_id=1, source_target_pairs={{0,16},{8,24},{16,0},{24,8},{1,17},{9,25},{17,1},{25,9},{2,18},{10... | collective-permute-start | bytes 196616 | tf_op jit(solution)/shard_map/ppermute | solution.py:295
  59.2 6.5 %collective-permute-start.1 = (bf16[2,64,512]{2,1,0:T(8,128)(2,1)S(1)}, bf16[2,64,512]{2,1,0:T(8,128)(2,1)S(1)}, u32[]{:S(2)}, u32[]{:S(2)}) collective-permute-start(bf16[2,64,512]{2,1,0:T(8,128)(2,1)S(1)} %pad_maximum_fusion.1), channel_id=1, source_target_pairs={{0,8},{8,0},{16,24},{24,16},{1,9},{9,1},{17,25},{25,17},{2,10},{10... | collective-permute-start | bytes 393224 | tf_op jit(solution)/shard_map/ppermute | solution.py:295
  68.2 33.2 %all-to-all-start = ((bf16[8,4,64,512]{3,2,1,0:T(8,128)(2,1)}), bf16[8,4,64,512]{3,2,1,0:T(8,128)(2,1)S(1)}, u32[]{:S(2)}, u32[]{:S(2)}) async-start(bf16[8,4,64,512]{3,2,1,0:T(8,128)(2,1)} %broadcast_in_dim.3), calls=%async_computation | async-start | bytes 4194304 | tf_op jit(solution)/shard_map/all_to_all | solution.py:39
  75.1 26.3 %copy-start = (bf16[512,512]{1,0:T(8,128)(2,1)S(1)}, bf16[512,512]{1,0:T(8,128)(2,1)}, u32[]{:S(2)}) copy-start(bf16[512,512]{1,0:T(8,128)(2,1)} %get-tuple-element.20.refs_0_) | copy-start | bytes 1572868
  118.9 16.0 %copy-start.1 = (bf16[2048,512]{1,0:T(8,128)(2,1)S(1)}, bf16[2048,512]{1,0:T(8,128)(2,1)}, u32[]{:S(2)}) copy-start(bf16[2048,512]{1,0:T(8,128)(2,1)} %param.4) | copy-start | bytes 6291460
  118.9 16.0 %copy-start.2 = (bf16[512,512]{1,0:T(8,128)(2,1)S(1)}, bf16[512,512]{1,0:T(8,128)(2,1)}, u32[]{:S(2)}) copy-start(bf16[512,512]{1,0:T(8,128)(2,1)} %get-tuple-element.18.refs_1_) | copy-start | bytes 1572868
  119.8 44.5 %all-to-all-start.2 = ((f16[16,32,512]{2,1,0:T(8,128)(2,1)}), f16[16,32,512]{2,1,0:T(8,128)(2,1)}, u32[]{:S(2)}, u32[]{:S(2)}) async-start(f16[16,32,512]{2,1,0:T(8,128)(2,1)} %bitcast.27), calls=%async_computation.2 | async-start | bytes 1048576 | tf_op jit(solution)/shard_map/all_to_all | solution.py:347
  134.9 1.0 copy-start.3
  135.9 1.0 copy-start.4
  138.9 4.3 %collective-permute-start.5 = (f32[4,64,512]{2,1,0:T(8,128)S(1)}, f32[4,64,512]{2,1,0:T(8,128)S(1)}, u32[]{:S(2)}, u32[]{:S(2)}) collective-permute-start(f32[4,64,512]{2,1,0:T(8,128)S(1)} %get-tuple-element.28), channel_id=1, source_target_pairs={{0,1},{1,0},{2,3},{3,2},{4,5},{5,4},{6,7},{7,6},{8,9},{9,8},{10,11... | collective-permute-start | bytes 1572872 | tf_op jit(solution)/shard_map/ppermute | solution.py:295
  143.3 9.0 %collective-permute-start.6 = (f32[64,512]{1,0:T(8,128)S(1)}, f32[64,512]{1,0:T(8,128)S(1)}, u32[]{:S(2)}, u32[]{:S(2)}) collective-permute-start(f32[64,512]{1,0:T(8,128)S(1)} %get-tuple-element.30), channel_id=1, source_target_pairs={{0,2},{2,0},{4,6},{6,4},{1,3},{3,1},{5,7},{7,5},{8,10},{10,8},{12,... | collective-permute-start | bytes 393224 | tf_op jit(solution)/shard_map/ppermute | solution.py:295
  145.5 7.6 %collective-permute-start.8 = (f32[64,512]{1,0:T(8,128)S(1)}, f32[64,512]{1,0:T(8,128)S(1)}, u32[]{:S(2)}, u32[]{:S(2)}) collective-permute-start(f32[64,512]{1,0:T(8,128)S(1)} %get-tuple-element.31), channel_id=1, source_target_pairs={{0,6},{2,4},{4,2},{6,0},{1,7},{3,5},{5,3},{7,1},{8,14},{10,12},{12... | collective-permute-start | bytes 393224 | tf_op jit(solution)/shard_map/ppermute | solution.py:295
  148.3 7.6 %collective-permute-start.7 = (f32[64,512]{1,0:T(8,128)S(1)}, f32[64,512]{1,0:T(8,128)S(1)}, u32[]{:S(2)}, u32[]{:S(2)}) collective-permute-start(f32[64,512]{1,0:T(8,128)S(1)} %get-tuple-element.32), channel_id=1, source_target_pairs={{0,4},{2,6},{4,0},{6,2},{1,5},{3,7},{5,1},{7,3},{8,12},{10,14},{12... | collective-permute-start | bytes 393224 | tf_op jit(solution)/shard_map/ppermute | solution.py:295
  156.0 11.1 %copy-start.5 = (bf16[64,512]{1,0:T(8,128)(2,1)}, bf16[64,512]{1,0:T(8,128)(2,1)S(1)}, u32[]{:S(2)}) copy-start(bf16[64,512]{1,0:T(8,128)(2,1)S(1)} %fusion.3.late_ref) | copy-start | bytes 196612

commit v11 on v5

--- a/solution.py
+++ b/solution.py
@@ -39,6 +39,15 @@
     return lax.all_to_all(copies, axes, split_axis=0, concat_axis=0, tiled=True)
 
 
+def inner_of(me):
+    return (me ^ (me >> 1)) & 1
+
+
+def leaf_ids(me):
+    inner = inner_of(me)
+    return (me, me ^ (2 - inner), me ^ (1 + inner), me ^ 3)
+
+
 def deal_kernel(me_ref, pre_ref, *refs):
     out_refs, deal_ref = refs[:LEAVES], refs[LEAVES]
     width = pre_ref.shape[1]
@@ -48,7 +57,10 @@
         row = lax.broadcasted_iota(jnp.int32, (width, width), 0)
         col = lax.broadcasted_iota(jnp.int32, (width, width), 1)
         block = row >> 5
-        place = (((block & 3) ^ me_ref[0]) << 7) + ((block >> 2) << 5) + (row & 31)
+        apart = (block & 3) ^ me_ref[0]
+        turned = (apart >> 1) | ((apart & 1) << 1)
+        slot = apart + inner_of(me_ref[0]) * (turned - apart)
+        place = (slot << 7) + ((block >> 2) << 5) + (row & 31)
         deal_ref[...] = jnp.where(place == col, 1.0, 0.0).astype(bf16)
 
     part = jnp.maximum(pre_ref[...], jnp.zeros((), bf16))
@@ -99,9 +111,9 @@
 def first_gram_kernel(spot_ref, grads_ref, late_ref, *refs):
     act_refs, held, out_ref = refs[:LEAVES], refs[LEAVES:-1], refs[-1]
     peers, _, rows, width = grads_ref.shape
-    me = spot_ref[0]
+    ids = leaf_ids(spot_ref[0])
     for k in range(LEAVES):
-        out_grad = grads_ref[:, me ^ k].reshape(peers * rows, width)
+        out_grad = grads_ref[:, ids[k]].reshape(peers * rows, width)
         held[k][...] = lax.dot_general(
             act_refs[k][...], out_grad, (((0,), (0,)), ((), ())), preferred_element_type=f32
         )
@@ -111,9 +123,9 @@
         for b in range(a, LEAVES):
             lanes = lanes_of(jnp.sum(held[a][...] * held[b][...], axis=0, keepdims=True))
             value = jnp.sum(lanes, axis=1, keepdims=True)
-            here = lane == LEAVES * (a ^ me) + (b ^ me)
+            here = lane == LEAVES * ids[a] + ids[b]
             if a != b:
-                here = here | (lane == LEAVES * (b ^ me) + (a ^ me))
+                here = here | (lane == LEAVES * ids[b] + ids[a])
             whole = jnp.where(here, value, whole)
     for copy in range(out_ref.shape[0]):
         out_ref[copy] = whole
@@ -146,7 +158,7 @@
 
 def first_merge_kernel(me_ref, sums_ref, *refs):
     leaf_refs, node_ref, inverse_ref = refs[:LEAVES], refs[LEAVES], refs[LEAVES + 1]
-    me = me_ref[0]
+    ids = leaf_ids(me_ref[0])
     total = jnp.sum(sums_ref[...], axis=0)
     lane = lax.broadcasted_iota(jnp.int32, total.shape, 1)
     gram = [
@@ -163,9 +175,9 @@
     inverse_ref[...] = jnp.broadcast_to(bound * (1.0 / TOP), inverse_ref.shape)
     merged = None
     for k in range(LEAVES):
-        mine = coef[k]
-        for other in range(1, LEAVES):
-            mine = jnp.where(me == other, coef[k ^ other], mine)
+        mine = coef[0]
+        for leaf in range(1, LEAVES):
+            mine = jnp.where(ids[k] == leaf, coef[leaf], mine)
         term = (mine * scale) * leaf_refs[k][...]
         merged = term if merged is None else merged + term
     node_ref[...] = merged
@@ -285,15 +297,16 @@
     grads = from_everyone(shards, mp)
     dealt = deal(me, pre_act)
     acts = {0: dealt[0]}
-    for k in (3, 2, 1):
-        acts[k] = swapped(dealt[k], "zl", k)
+    acts[2] = lax.ppermute(dealt[2], "zl", [(0, 2), (3, 1), (1, 0), (2, 3)])
+    acts[3] = lax.ppermute(dealt[3], "zl", [(0, 3), (3, 0), (1, 2), (2, 1)])
+    acts[1] = lax.ppermute(dealt[1], "zl", [(0, 1), (3, 2), (1, 3), (2, 0)])
     arrived = pl.pallas_call(
         arrived_kernel,
         out_shape=jax.ShapeDtypeStruct((8, 128), f32),
         in_specs=[ANY] * (LEAVES - 1),
         compiler_params=pltpu.CompilerParams(vmem_limit_bytes=1024 * 1024),
         cost_estimate=pl.CostEstimate(flops=10**11, bytes_accessed=0, transcendentals=0),
-    )(acts[3], acts[2], acts[1])
+    )(acts[2], acts[3], acts[1])
 
     leaf_shape = jax.ShapeDtypeStruct((quarter, width), f32)
     group = ("zl", *mp)

time: 162 us -> 163 us (level)
    ppermute x0 -> x3, waiting for transfers between devices: none -> 32.2 us  [the longest x1 26.9 us: local(): acts[1] = lax.ppermute(dealt[1], 'zl', [(0, 1), (3, 2), (1, 3), (2, 0)])]
    ppermute x7 -> x4, waiting for transfers between devices: 36.6 us -> 4.99 us  [swapped(): lax.ppermute(value, axis, [(i, i ^ apart) for i in range(lax.axis_size(ax...]
    ppermute x0 -> x3, starting transfers between devices: none -> 9.54 us  [the longest x1 4.26 us: local(): acts[2] = lax.ppermute(dealt[2], 'zl', [(0, 2), (3, 1), (1, 0), (2, 3)])]
    ppermute x7 -> x4, starting transfers between devices: 21.1 us -> 11.8 us  [swapped(): lax.ppermute(value, axis, [(i, i ^ apart) for i in range(lax.axis_size(ax...]
  transfers between devices with their start and end apart: 10 -> 10, of which waited for: 5 -> 6; matrix products, arithmetic and copies ran while one was open for 1% -> 1% of each run, Pallas kernels for 3% -> 3%
where the time goes in v11:
time: 163 us; the launch traced here: 162 us
  starting transfers between devices  51.5 us (32%)
  waiting for transfers between devices  46.1 us (28%)
  blocking collectives  44.2 us (27%)
  Pallas kernels  12 us (7%)
  local copies, waits for them, and re-layouts  6.35 us (4%)
    ppermute x1, waiting for transfers between devices, local(): acts[1] = lax.ppermute(dealt[1], 'zl', [(0, 1), (3, 2), (1, 3), (2, 0)])  26.9 us
    all_to_all x1, blocking collectives, local(): sums = lax.all_to_all(sums, dp, split_axis=0, concat_axis=0, tiled=True)  21.7 us
    all_to_all x1, starting transfers between devices, local(): lax.all_to_all(sent, hi, split_axis=0, concat_axis=0, tiled=True)  15.3 us
    all_to_all x2, starting transfers between devices, from_everyone(): return lax.all_to_all(copies, axes, split_axis=0, concat_axis=0, tiled=True)  14.9 us
    all_to_all x1, blocking collectives, local(): sums = lax.all_to_all(sums, group, split_axis=0, concat_axis=0, tiled=True)  13.9 us
    ppermute x4, starting transfers between devices, swapped(): lax.ppermute(value, axis, [(i, i ^ apart) for i in range(lax.axis_size(ax...  11.8 us
    all_to_all x1, waiting for transfers between devices, local(): lax.all_to_all(sent, hi, split_axis=0, concat_axis=0, tiled=True)  8.9 us
    all_to_all x1, blocking collectives, local(): sums = lax.all_to_all(sums, mp, split_axis=0, concat_axis=0, tiled=True)  8.61 us
  transfers between devices with their start and end apart: 10, of which 6 were waited for; matrix products, arithmetic and copies ran while one was open for 1% of the time, Pallas kernels for 3%

profile of v11, /device:TPU:1, one launch (start us, length us, event | category | flops | bytes accessed | tf_op | source)
XLA Modules:
  0.0 162.1 jit_solution(17881313670077777373)
XLA Ops:
  0.6 1.6 broadcast_in_dim.6
  2.2 6.4 %all-to-all-start = ((bf16[4,64,512]{2,1,0:T(8,128)(2,1)}), bf16[4,64,512]{2,1,0:T(8,128)(2,1)S(1)}, u32[]{:S(2)}, u32[]{:S(2)}) async-start(bf16[4,64,512]{2,1,0:T(8,128)(2,1)} %broadcast_in_dim.6), calls=%async_computation | async-start | bytes 524288 | tf_op jit(solution)/shard_map/all_to_all | solution.py:39
  8.6 0.0 copy-start
  8.6 1.6 copy-done
  10.2 3.3 %shard_map.50 = (bf16[512,512]{1,0:T(8,128)(2,1)S(1)}, bf16[512,512]{1,0:T(8,128)(2,1)}, bf16[512,512]{1,0:T(8,128)(2,1)}, bf16[512,512]{1,0:T(8,128)(2,1)}) custom-call(s32[1]{0:T(128)} %bitcast.me_ref, bf16[512,2048]{1,0:T(8,128)(2,1)S(1)} %copy-done), custom_call_target="tpu_custom_call" | custom-call | flops 1073741824 | bytes 4194304 | tf_op jit(solution)/shard_map/pallas_call | solution.py:75
  13.6 4.3 %collective-permute-start = (bf16[512,512]{1,0:T(8,128)(2,1)}, bf16[512,512]{1,0:T(8,128)(2,1)S(1)}, u32[]{:S(2)}, u32[]{:S(2)}) collective-permute-start(bf16[512,512]{1,0:T(8,128)(2,1)} %get-tuple-element.15), channel_id=1, source_target_pairs={{0,16},{24,8},{8,0},{16,24},{1,17},{25,9},{9,1},{17,25},{2,18},{26... | collective-permute-start | bytes 1572872 | tf_op jit(solution)/shard_map/ppermute | solution.py:300
  17.8 3.1 %collective-permute-start.1 = (bf16[512,512]{1,0:T(8,128)(2,1)}, bf16[512,512]{1,0:T(8,128)(2,1)}, u32[]{:S(2)}, u32[]{:S(2)}) collective-permute-start(bf16[512,512]{1,0:T(8,128)(2,1)} %get-tuple-element.16), channel_id=1, source_target_pairs={{0,24},{24,0},{8,16},{16,8},{1,25},{25,1},{9,17},{17,9},{2,26},{26... | collective-permute-start | bytes 1572872 | tf_op jit(solution)/shard_map/ppermute | solution.py:301
  20.9 2.2 %collective-permute-start.2 = (bf16[512,512]{1,0:T(8,128)(2,1)}, bf16[512,512]{1,0:T(8,128)(2,1)}, u32[]{:S(2)}, u32[]{:S(2)}) collective-permute-start(bf16[512,512]{1,0:T(8,128)(2,1)} %get-tuple-element.17), channel_id=1, source_target_pairs={{0,8},{24,16},{8,24},{16,0},{1,9},{25,17},{9,25},{17,1},{2,10},{26... | collective-permute-start | bytes 1572872 | tf_op jit(solution)/shard_map/ppermute | solution.py:302
  23.1 0.1 pad_add_fusion.spot_ref
  23.2 0.0 all-to-all-done
  23.2 1.6 broadcast_in_dim.7
  24.8 8.4 %all-to-all-start.1 = ((bf16[8,4,64,512]{3,2,1,0:T(8,128)(2,1)}), bf16[8,4,64,512]{3,2,1,0:T(8,128)(2,1)S(1)}, u32[]{:S(2)}, u32[]{:S(2)}) async-start(bf16[8,4,64,512]{3,2,1,0:T(8,128)(2,1)} %broadcast_in_dim.7), calls=%async_computation.1 | async-start | bytes 4194304 | tf_op jit(solution)/shard_map/all_to_all | solution.py:39
  33.2 0.0 collective-permute-done.refs_0_.refs_2_
  33.2 5.3 %collective-permute-done.1.refs_1_.refs_3_ = bf16[512,512]{1,0:T(8,128)(2,1)} collective-permute-done((bf16[512,512]{1,0:T(8,128)(2,1)}, bf16[512,512]{1,0:T(8,128)(2,1)}, u32[]{:S(2)}, u32[]{:S(2)}) %collective-permute-start.1) | collective-permute-done | bytes 524320 | tf_op jit(solution)/shard_map/ppermute | solution.py:301
  38.5 26.9 %collective-permute-done.2.refs_2_.refs_1_ = bf16[512,512]{1,0:T(8,128)(2,1)} collective-permute-done((bf16[512,512]{1,0:T(8,128)(2,1)}, bf16[512,512]{1,0:T(8,128)(2,1)}, u32[]{:S(2)}, u32[]{:S(2)}) %collective-permute-start.2) | collective-permute-done | bytes 524320 | tf_op jit(solution)/shard_map/ppermute | solution.py:302
  65.4 0.0 all-to-all-done.1.grads_ref
  65.4 2.8 %shard_map.52 = (f32[512,512]{1,0:T(8,128)S(1)}, f32[512,512]{1,0:T(8,128)S(1)}, f32[512,512]{1,0:T(8,128)S(1)}, f32[512,512]{1,0:T(8,128)S(1)}, f32[32,1,128]{2,1,0:T(1,128)S(1)}) custom-call(s32[3]{0:T(128)S(1)} %pad_add_fusion.spot_ref, bf16[8,4,64,512]{3,2,1,0:T(8,128)(2,1)S(1)} %all-to-all-done.1.grads_ref, f32[8,128]{1,0:T(8,128)S(1)} %shard_map.51.late_ref, ...), custom_call_target="tpu_custom_call" | custom-call | flops 1073741824 | bytes 4194304 | tf_op jit(solution)/shard_map/pallas_call | solution.py:313
  68.2 13.9 %all_to_all.30.sums_ref = f32[32,1,128]{2,1,0:T(1,128)S(1)} all-to-all(f32[32,1,128]{2,1,0:T(1,128)S(1)} %get-tuple-element.19), channel_id=1, replica_groups=mesh['y'=4,'zh'=4,'zl'=4,'x'=4,'c'=2] {'zl','x','c'}, dimensions={0} | all-to-all | bytes 32768 | tf_op jit(solution)/shard_map/all_to_all | solution.py:320
  82.1 0.7 shard_map.53
  82.8 0.0 copy-start.1
  82.8 0.9 convert_element_type.10
  83.7 15.3 %all-to-all-start.3 = ((f16[16,32,512]{2,1,0:T(8,128)(2,1)}), f16[16,32,512]{2,1,0:T(8,128)(2,1)S(1)}, u32[]{:S(2)}, u32[]{:S(2)}) async-start(f16[16,32,512]{2,1,0:T(8,128)(2,1)} %bitcast.8), calls=%async_computation.3 | async-start | bytes 1048576 | tf_op jit(solution)/shard_map/all_to_all | solution.py:346
  99.0 0.0 copy-done.1
  99.0 0.0 copy-start.2
  99.0 1.6 copy-done.2
  100.6 1.9 %shard_map.54 = (f32[4,64,512]{2,1,0:T(8,128)S(1)}, f32[4,64,512]{2,1,0:T(8,128)S(1)}) custom-call(s32[3]{0:T(128)S(1)} %pad_add_fusion.spot_ref, bf16[512,2048]{1,0:T(8,128)(2,1)S(1)} %copy-done.1, bf16[2048,512]{1,0:T(8,128)(2,1)S(1)} %copy-done.2, f32[8,128]{1,0:T(8,128)S(1)} %get-tuple-element.24.late_ref.inverse_ref), custom_call_target="tpu_custom_call" | custom-call | flops 1073741824 | bytes 4194304 | tf_op jit(solution)/shard_map/pallas_call | solution.py:330
  102.5 2.8 %collective-permute-start.3 = (f32[4,64,512]{2,1,0:T(8,128)S(1)}, f32[4,64,512]{2,1,0:T(8,128)S(1)}, u32[]{:S(2)}, u32[]{:S(2)}) collective-permute-start(f32[4,64,512]{2,1,0:T(8,128)S(1)} %get-tuple-element.26), channel_id=1, source_target_pairs={{0,1},{1,0},{2,3},{3,2},{4,5},{5,4},{6,7},{7,6},{8,9},{9,8},{10,11... | collective-permute-start | bytes 1572872 | tf_op jit(solution)/shard_map/ppermute | solution.py:294
  105.3 1.5 collective-permute-done.3
  106.8 0.1 add.15
  106.9 2.2 %collective-permute-start.4 = (f32[64,512]{1,0:T(8,128)S(1)}, f32[64,512]{1,0:T(8,128)S(1)}, u32[]{:S(2)}, u32[]{:S(2)}) collective-permute-start(f32[64,512]{1,0:T(8,128)S(1)} %get-tuple-element.28), channel_id=1, source_target_pairs={{0,2},{2,0},{4,6},{6,4},{1,3},{3,1},{5,7},{7,5},{8,10},{10,8},{12,... | collective-permute-start | bytes 393224 | tf_op jit(solution)/shard_map/ppermute | solution.py:294
  109.1 2.8 %collective-permute-start.6 = (f32[64,512]{1,0:T(8,128)S(1)}, f32[64,512]{1,0:T(8,128)S(1)}, u32[]{:S(2)}, u32[]{:S(2)}) collective-permute-start(f32[64,512]{1,0:T(8,128)S(1)} %get-tuple-element.29), channel_id=1, source_target_pairs={{0,6},{2,4},{4,2},{6,0},{1,7},{3,5},{5,3},{7,1},{8,14},{10,12},{12... | collective-permute-start | bytes 393224 | tf_op jit(solution)/shard_map/ppermute | solution.py:294
  111.9 4.0 %collective-permute-start.5 = (f32[64,512]{1,0:T(8,128)S(1)}, f32[64,512]{1,0:T(8,128)S(1)}, u32[]{:S(2)}, u32[]{:S(2)}) collective-permute-start(f32[64,512]{1,0:T(8,128)S(1)} %get-tuple-element.30), channel_id=1, source_target_pairs={{0,4},{2,6},{4,0},{6,2},{1,5},{3,7},{5,1},{7,3},{8,12},{10,14},{12... | collective-permute-start | bytes 393224 | tf_op jit(solution)/shard_map/ppermute | solution.py:294
  115.9 0.0 collective-permute-done.4
  115.9 0.7 collective-permute-done.6
  116.6 2.8 %collective-permute-done.5 = f32[64,512]{1,0:T(8,128)S(1)} collective-permute-done((f32[64,512]{1,0:T(8,128)S(1)}, f32[64,512]{1,0:T(8,128)S(1)}, u32[]{:S(2)}, u32[]{:S(2)}) %collective-permute-start.5) | collective-permute-done | bytes 131104 | tf_op jit(solution)/shard_map/ppermute | solution.py:294
  119.5 0.0 copy-start.3
  119.5 8.9 %all-to-all-done.3 = f16[16,32,512]{2,1,0:T(8,128)(2,1)S(1)} async-done(((f16[16,32,512]{2,1,0:T(8,128)(2,1)}), f16[16,32,512]{2,1,0:T(8,128)(2,1)S(1)}, u32[]{:S(2)}, u32[]{:S(2)}) %all-to-all-start.3) | async-done | bytes 524320 | tf_op jit(solution)/shard_map/all_to_all | solution.py:346
  128.4 0.1 convert_element_type.11.nodes_ref
  128.5 1.6 shard_map.55
  130.1 0.0 copy-done.3
  130.1 8.6 %all_to_all.31.sums_ref = f32[8,2,128]{2,1,0:T(2,128)S(1)} all-to-all(f32[8,2,128]{2,1,0:T(2,128)S(1)} %shard_map.55), channel_id=1, replica_groups=mesh['y'=4,'zh'=4,'zl'=4,'x'=4,'c'=2] {'x','c'}, dimensions={0} | all-to-all | bytes 16384 | tf_op jit(solution)/shard_map/all_to_all | solution.py:355
  138.7 21.7 %all_to_all.32.sums_ref = f32[64,2,128]{2,1,0:T(2,128)S(1)} all-to-all(f32[64,2,128]{2,1,0:T(2,128)S(1)} %shard_map.56), channel_id=1, replica_groups=mesh['y'=4,'zh'=4,'zl'=4,'x'=4,'c'=2] {'y','zh','zl'}, dimensions={0} | all-to-all | bytes 131072 | tf_op jit(solution)/shard_map/all_to_all | solution.py:358
  160.4 1.7 %shard_map.57 = f32[32,512]{1,0:T(8,128)} custom-call(f32[64,2,128]{2,1,0:T(2,128)S(1)} %all_to_all.32.sums_ref, f32[16,32,512]{2,1,0:T(8,128)S(1)} %convert_element_type.11.nodes_ref), custom_call_target="tpu_custom_call" | custom-call | flops 524288 | bytes 1048576 | tf_op jit(solution)/shard_map/pallas_call | solution.py:359
  (4 shorter events, 0.1 us)
Async XLA Ops:
  2.2 21.0 %all-to-all-start = ((bf16[4,64,512]{2,1,0:T(8,128)(2,1)}), bf16[4,64,512]{2,1,0:T(8,128)(2,1)S(1)}, u32[]{:S(2)}, u32[]{:S(2)}) async-start(bf16[4,64,512]{2,1,0:T(8,128)(2,1)} %broadcast_in_dim.6), calls=%async_computation | async-start | bytes 524288 | tf_op jit(solution)/shard_map/all_to_all | solution.py:39
  8.6 1.6 copy-start
  13.6 19.7 %collective-permute-start = (bf16[512,512]{1,0:T(8,128)(2,1)}, bf16[512,512]{1,0:T(8,128)(2,1)S(1)}, u32[]{:S(2)}, u32[]{:S(2)}) collective-permute-start(bf16[512,512]{1,0:T(8,128)(2,1)} %get-tuple-element.15), channel_id=1, source_target_pairs={{0,16},{24,8},{8,0},{16,24},{1,17},{25,9},{9,1},{17,25},{2,18},{26... | collective-permute-start | bytes 1572872 | tf_op jit(solution)/shard_map/ppermute | solution.py:300
  17.8 20.7 %collective-permute-start.1 = (bf16[512,512]{1,0:T(8,128)(2,1)}, bf16[512,512]{1,0:T(8,128)(2,1)}, u32[]{:S(2)}, u32[]{:S(2)}) collective-permute-start(bf16[512,512]{1,0:T(8,128)(2,1)} %get-tuple-element.16), channel_id=1, source_target_pairs={{0,24},{24,0},{8,16},{16,8},{1,25},{25,1},{9,17},{17,9},{2,26},{26... | collective-permute-start | bytes 1572872 | tf_op jit(solution)/shard_map/ppermute | solution.py:301
  20.9 44.5 %collective-permute-start.2 = (bf16[512,512]{1,0:T(8,128)(2,1)}, bf16[512,512]{1,0:T(8,128)(2,1)}, u32[]{:S(2)}, u32[]{:S(2)}) collective-permute-start(bf16[512,512]{1,0:T(8,128)(2,1)} %get-tuple-element.17), channel_id=1, source_target_pairs={{0,8},{24,16},{8,24},{16,0},{1,9},{25,17},{9,25},{17,1},{2,10},{26... | collective-permute-start | bytes 1572872 | tf_op jit(solution)/shard_map/ppermute | solution.py:302
  24.8 40.6 %all-to-all-start.1 = ((bf16[8,4,64,512]{3,2,1,0:T(8,128)(2,1)}), bf16[8,4,64,512]{3,2,1,0:T(8,128)(2,1)S(1)}, u32[]{:S(2)}, u32[]{:S(2)}) async-start(bf16[8,4,64,512]{3,2,1,0:T(8,128)(2,1)} %broadcast_in_dim.7), calls=%async_computation.1 | async-start | bytes 4194304 | tf_op jit(solution)/shard_map/all_to_all | solution.py:39
  82.8 16.2 %copy-start.1 = (bf16[512,2048]{1,0:T(8,128)(2,1)S(1)}, bf16[512,2048]{1,0:T(8,128)(2,1)}, u32[]{:S(2)}) copy-start(bf16[512,2048]{1,0:T(8,128)(2,1)} %pre_ref.3) | copy-start | bytes 6291460
  83.7 44.7 %all-to-all-start.3 = ((f16[16,32,512]{2,1,0:T(8,128)(2,1)}), f16[16,32,512]{2,1,0:T(8,128)(2,1)S(1)}, u32[]{:S(2)}, u32[]{:S(2)}) async-start(f16[16,32,512]{2,1,0:T(8,128)(2,1)} %bitcast.8), calls=%async_computation.3 | async-start | bytes 1048576 | tf_op jit(solution)/shard_map/all_to_all | solution.py:346
  99.0 1.6 copy-start.2
  102.5 4.4 %collective-permute-start.3 = (f32[4,64,512]{2,1,0:T(8,128)S(1)}, f32[4,64,512]{2,1,0:T(8,128)S(1)}, u32[]{:S(2)}, u32[]{:S(2)}) collective-permute-start(f32[4,64,512]{2,1,0:T(8,128)S(1)} %get-tuple-element.26), channel_id=1, source_target_pairs={{0,1},{1,0},{2,3},{3,2},{4,5},{5,4},{6,7},{7,6},{8,9},{9,8},{10,11... | collective-permute-start | bytes 1572872 | tf_op jit(solution)/shard_map/ppermute | solution.py:294
  106.9 9.0 %collective-permute-start.4 = (f32[64,512]{1,0:T(8,128)S(1)}, f32[64,512]{1,0:T(8,128)S(1)}, u32[]{:S(2)}, u32[]{:S(2)}) collective-permute-start(f32[64,512]{1,0:T(8,128)S(1)} %get-tuple-element.28), channel_id=1, source_target_pairs={{0,2},{2,0},{4,6},{6,4},{1,3},{3,1},{5,7},{7,5},{8,10},{10,8},{12,... | collective-permute-start | bytes 393224 | tf_op jit(solution)/shard_map/ppermute | solution.py:294
  109.1 7.5 %collective-permute-start.6 = (f32[64,512]{1,0:T(8,128)S(1)}, f32[64,512]{1,0:T(8,128)S(1)}, u32[]{:S(2)}, u32[]{:S(2)}) collective-permute-start(f32[64,512]{1,0:T(8,128)S(1)} %get-tuple-element.29), channel_id=1, source_target_pairs={{0,6},{2,4},{4,2},{6,0},{1,7},{3,5},{5,3},{7,1},{8,14},{10,12},{12... | collective-permute-start | bytes 393224 | tf_op jit(solution)/shard_map/ppermute | solution.py:294
  111.9 7.5 %collective-permute-start.5 = (f32[64,512]{1,0:T(8,128)S(1)}, f32[64,512]{1,0:T(8,128)S(1)}, u32[]{:S(2)}, u32[]{:S(2)}) collective-permute-start(f32[64,512]{1,0:T(8,128)S(1)} %get-tuple-element.30), channel_id=1, source_target_pairs={{0,4},{2,6},{4,0},{6,2},{1,5},{3,7},{5,1},{7,3},{8,12},{10,14},{12... | collective-permute-start | bytes 393224 | tf_op jit(solution)/shard_map/ppermute | solution.py:294
  119.5 10.6 %copy-start.3 = (bf16[64,512]{1,0:T(8,128)(2,1)}, bf16[64,512]{1,0:T(8,128)(2,1)S(1)}, u32[]{:S(2)}) copy-start(bf16[64,512]{1,0:T(8,128)(2,1)S(1)} %fusion.3.late_ref) | copy-start | bytes 196612

commit v12 on v5

--- a/solution.py
+++ b/solution.py
@@ -32,6 +32,14 @@
         compiler_params=pltpu.CompilerParams(vmem_limit_bytes=LIMIT),
         cost_estimate=pl.CostEstimate(flops=flops, bytes_accessed=size, transcendentals=0),
     )
+
+
+def copies_kernel(array_ref, out_ref, done):
+    copies = [pltpu.make_async_copy(array_ref, out_ref.at[k], done.at[k]) for k in range(LEAVES)]
+    for copy in copies:
+        copy.start()
+    for copy in copies:
+        copy.wait()
 
 
 def from_everyone(array, axes):
@@ -281,7 +289,14 @@
     def swapped(value, axis, apart):
         return lax.ppermute(value, axis, [(i, i ^ apart) for i in range(lax.axis_size(axis))])
 
-    shards = from_everyone(out_grad, "zl")
+    copies = pl.pallas_call(
+        copies_kernel,
+        out_shape=jax.ShapeDtypeStruct((LEAVES, *out_grad.shape), bf16),
+        in_specs=[ANY],
+        out_specs=ANY,
+        scratch_shapes=[pltpu.SemaphoreType.DMA((LEAVES,))],
+    )(out_grad)
+    shards = lax.all_to_all(copies, "zl", split_axis=0, concat_axis=0, tiled=True)
     grads = from_everyone(shards, mp)
     dealt = deal(me, pre_act)
     acts = {0: dealt[0]}

time: 162 us -> 169 us (1.043)
  Pallas kernels: 11.9 us -> 21 us
    pallas_call x0 -> x1, Pallas kernels: none -> 9.08 us  [local(): pl.pallas_call(copies_kernel, out_shape=jax.ShapeDtypeStruct((LEAVES, *ou...]
    all_to_all x0 -> x1, starting transfers between devices: none -> 6.46 us  [local(): lax.all_to_all(copies, 'zl', split_axis=0, concat_axis=0, tiled=True)]
    all_to_all x2 -> x1, starting transfers between devices: 14.6 us -> 8.19 us  [from_everyone(): return lax.all_to_all(copies, axes, split_axis=0, concat_axis=0, tiled=True)]
where the time goes in v12:
time: 169 us
  starting transfers between devices  51 us (30%)
  waiting for transfers between devices  45.5 us (27%)
  blocking collectives  44.3 us (26%)
  Pallas kernels  21 us (12%)
  local copies, waits for them, and re-layouts  4.79 us (3%)
    ppermute x7, waiting for transfers between devices, swapped(): lax.ppermute(value, axis, [(i, i ^ apart) for i in range(lax.axis_size(ax...  36.6 us
    all_to_all x1, blocking collectives, local(): sums = lax.all_to_all(sums, dp, split_axis=0, concat_axis=0, tiled=True)  21.7 us
    ppermute x7, starting transfers between devices, swapped(): lax.ppermute(value, axis, [(i, i ^ apart) for i in range(lax.axis_size(ax...  21.1 us
    all_to_all x1, starting transfers between devices, local(): lax.all_to_all(sent, hi, split_axis=0, concat_axis=0, tiled=True)  15.3 us
    all_to_all x1, blocking collectives, local(): sums = lax.all_to_all(sums, group, split_axis=0, concat_axis=0, tiled=True)  14 us
    pallas_call x1, Pallas kernels, local(): pl.pallas_call(copies_kernel, out_shape=jax.ShapeDtypeStruct((LEAVES, *ou...  9.08 us
    all_to_all x1, waiting for transfers between devices, local(): lax.all_to_all(sent, hi, split_axis=0, concat_axis=0, tiled=True)  8.9 us
    all_to_all x1, blocking collectives, local(): sums = lax.all_to_all(sums, mp, split_axis=0, concat_axis=0, tiled=True)  8.61 us
  transfers between devices with their start and end apart: 10, of which 5 were waited for; matrix products, arithmetic and copies ran while one was open for 1% of the time, Pallas kernels for 3%

profile of v12, /device:TPU:1, one launch (start us, length us, event | category | flops | bytes accessed | tf_op | source)
XLA Modules:
  0.0 168.7 jit_solution(6928319578518956539)
XLA Ops:
  0.6 9.1 %shard_map.50 = bf16[4,64,512]{2,1,0:T(8,128)(2,1)} custom-call(bf16[64,512]{1,0:T(8,128)(2,1)} %array_ref.1), custom_call_target="tpu_custom_call" | custom-call | tf_op jit(solution)/shard_map/pallas_call | solution.py:292
  9.7 6.5 %all-to-all-start = ((bf16[4,64,512]{2,1,0:T(8,128)(2,1)}), bf16[4,64,512]{2,1,0:T(8,128)(2,1)S(1)}, u32[]{:S(2)}, u32[]{:S(2)}) async-start(bf16[4,64,512]{2,1,0:T(8,128)(2,1)} %shard_map.50), calls=%async_computation | async-start | bytes 524288 | tf_op jit(solution)/shard_map/all_to_all | solution.py:299
  16.2 0.0 copy-start
  16.2 1.6 copy-done
  17.8 3.3 %shard_map.51 = (bf16[512,512]{1,0:T(8,128)(2,1)S(1)}, bf16[512,512]{1,0:T(8,128)(2,1)}, bf16[512,512]{1,0:T(8,128)(2,1)}, bf16[512,512]{1,0:T(8,128)(2,1)}) custom-call(s32[1]{0:T(128)} %bitcast.me_ref, bf16[512,2048]{1,0:T(8,128)(2,1)S(1)} %copy-done), custom_call_target="tpu_custom_call" | custom-call | flops 1073741824 | bytes 4194304 | tf_op jit(solution)/shard_map/pallas_call | solution.py:71
  21.0 5.2 %collective-permute-start = (bf16[512,512]{1,0:T(8,128)(2,1)}, bf16[512,512]{1,0:T(8,128)(2,1)S(1)}, u32[]{:S(2)}, u32[]{:S(2)}) collective-permute-start(bf16[512,512]{1,0:T(8,128)(2,1)} %get-tuple-element.15), channel_id=1, source_target_pairs={{0,24},{8,16},{16,8},{24,0},{1,25},{9,17},{17,9},{25,1},{2,26},{10... | collective-permute-start | bytes 1572872 | tf_op jit(solution)/shard_map/ppermute | solution.py:290
  26.2 1.9 %collective-permute-start.1 = (bf16[512,512]{1,0:T(8,128)(2,1)}, bf16[512,512]{1,0:T(8,128)(2,1)}, u32[]{:S(2)}, u32[]{:S(2)}) collective-permute-start(bf16[512,512]{1,0:T(8,128)(2,1)} %get-tuple-element.16), channel_id=1, source_target_pairs={{0,16},{8,24},{16,0},{24,8},{1,17},{9,25},{17,1},{25,9},{2,18},{10... | collective-permute-start | bytes 1572872 | tf_op jit(solution)/shard_map/ppermute | solution.py:290
  28.1 2.2 %collective-permute-start.2 = (bf16[512,512]{1,0:T(8,128)(2,1)}, bf16[512,512]{1,0:T(8,128)(2,1)}, u32[]{:S(2)}, u32[]{:S(2)}) collective-permute-start(bf16[512,512]{1,0:T(8,128)(2,1)} %get-tuple-element.17), channel_id=1, source_target_pairs={{0,8},{8,0},{16,24},{24,16},{1,9},{9,1},{17,25},{25,17},{2,10},{10... | collective-permute-start | bytes 1572872 | tf_op jit(solution)/shard_map/ppermute | solution.py:290
  30.3 0.1 pad_add_fusion.spot_ref
  30.4 0.0 all-to-all-done
  30.4 1.6 broadcast_in_dim.3
  32.0 8.2 %all-to-all-start.1 = ((bf16[8,4,64,512]{3,2,1,0:T(8,128)(2,1)}), bf16[8,4,64,512]{3,2,1,0:T(8,128)(2,1)S(1)}, u32[]{:S(2)}, u32[]{:S(2)}) async-start(bf16[8,4,64,512]{3,2,1,0:T(8,128)(2,1)} %broadcast_in_dim.3), calls=%async_computation.1 | async-start | bytes 4194304 | tf_op jit(solution)/shard_map/all_to_all | solution.py:47
  40.2 0.0 collective-permute-done.refs_0_.refs_3_
  40.2 31.6 %collective-permute-done.1.refs_1_.refs_2_ = bf16[512,512]{1,0:T(8,128)(2,1)} collective-permute-done((bf16[512,512]{1,0:T(8,128)(2,1)}, bf16[512,512]{1,0:T(8,128)(2,1)}, u32[]{:S(2)}, u32[]{:S(2)}) %collective-permute-start.1) | collective-permute-done | bytes 524320 | tf_op jit(solution)/shard_map/ppermute | solution.py:290
  71.8 0.0 collective-permute-done.2.refs_2_.refs_1_
  71.8 0.0 all-to-all-done.1.grads_ref
  71.8 2.8 %shard_map.53 = (f32[512,512]{1,0:T(8,128)S(1)}, f32[512,512]{1,0:T(8,128)S(1)}, f32[512,512]{1,0:T(8,128)S(1)}, f32[512,512]{1,0:T(8,128)S(1)}, f32[32,1,128]{2,1,0:T(1,128)S(1)}) custom-call(s32[3]{0:T(128)S(1)} %pad_add_fusion.spot_ref, bf16[8,4,64,512]{3,2,1,0:T(8,128)(2,1)S(1)} %all-to-all-done.1.grads_ref, f32[8,128]{1,0:T(8,128)S(1)} %shard_map.52.late_ref, ...), custom_call_target="tpu_custom_call" | custom-call | flops 1073741824 | bytes 4194304 | tf_op jit(solution)/shard_map/pallas_call | solution.py:315
  74.6 14.0 %all_to_all.30.sums_ref = f32[32,1,128]{2,1,0:T(1,128)S(1)} all-to-all(f32[32,1,128]{2,1,0:T(1,128)S(1)} %get-tuple-element.19), channel_id=1, replica_groups=mesh['y'=4,'zh'=4,'zl'=4,'x'=4,'c'=2] {'zl','x','c'}, dimensions={0} | all-to-all | bytes 32768 | tf_op jit(solution)/shard_map/all_to_all | solution.py:322
  88.6 0.7 shard_map.54
  89.3 0.0 copy-start.1
  89.4 0.9 convert_element_type.10
  90.3 15.3 %all-to-all-start.3 = ((f16[16,32,512]{2,1,0:T(8,128)(2,1)}), f16[16,32,512]{2,1,0:T(8,128)(2,1)S(1)}, u32[]{:S(2)}, u32[]{:S(2)}) async-start(f16[16,32,512]{2,1,0:T(8,128)(2,1)} %bitcast.8), calls=%async_computation.3 | async-start | bytes 1048576 | tf_op jit(solution)/shard_map/all_to_all | solution.py:348
  105.6 0.0 copy-done.1
  105.6 0.0 copy-start.2
  105.6 1.6 copy-done.2
  107.2 1.9 %shard_map.55 = (f32[4,64,512]{2,1,0:T(8,128)S(1)}, f32[4,64,512]{2,1,0:T(8,128)S(1)}) custom-call(s32[3]{0:T(128)S(1)} %pad_add_fusion.spot_ref, bf16[512,2048]{1,0:T(8,128)(2,1)S(1)} %copy-done.1, bf16[2048,512]{1,0:T(8,128)(2,1)S(1)} %copy-done.2, f32[8,128]{1,0:T(8,128)S(1)} %get-tuple-element.24.late_ref.inverse_ref), custom_call_target="tpu_custom_call" | custom-call | flops 1073741824 | bytes 4194304 | tf_op jit(solution)/shard_map/pallas_call | solution.py:332
  109.0 2.8 %collective-permute-start.3 = (f32[4,64,512]{2,1,0:T(8,128)S(1)}, f32[4,64,512]{2,1,0:T(8,128)S(1)}, u32[]{:S(2)}, u32[]{:S(2)}) collective-permute-start(f32[4,64,512]{2,1,0:T(8,128)S(1)} %get-tuple-element.26), channel_id=1, source_target_pairs={{0,1},{1,0},{2,3},{3,2},{4,5},{5,4},{6,7},{7,6},{8,9},{9,8},{10,11... | collective-permute-start | bytes 1572872 | tf_op jit(solution)/shard_map/ppermute | solution.py:290
  111.9 1.5 collective-permute-done.3
  113.4 0.1 add.15
  113.5 2.2 %collective-permute-start.4 = (f32[64,512]{1,0:T(8,128)S(1)}, f32[64,512]{1,0:T(8,128)S(1)}, u32[]{:S(2)}, u32[]{:S(2)}) collective-permute-start(f32[64,512]{1,0:T(8,128)S(1)} %get-tuple-element.28), channel_id=1, source_target_pairs={{0,2},{2,0},{4,6},{6,4},{1,3},{3,1},{5,7},{7,5},{8,10},{10,8},{12,... | collective-permute-start | bytes 393224 | tf_op jit(solution)/shard_map/ppermute | solution.py:290
  115.7 2.8 %collective-permute-start.6 = (f32[64,512]{1,0:T(8,128)S(1)}, f32[64,512]{1,0:T(8,128)S(1)}, u32[]{:S(2)}, u32[]{:S(2)}) collective-permute-start(f32[64,512]{1,0:T(8,128)S(1)} %get-tuple-element.29), channel_id=1, source_target_pairs={{0,6},{2,4},{4,2},{6,0},{1,7},{3,5},{5,3},{7,1},{8,14},{10,12},{12... | collective-permute-start | bytes 393224 | tf_op jit(solution)/shard_map/ppermute | solution.py:290
  118.5 4.0 %collective-permute-start.5 = (f32[64,512]{1,0:T(8,128)S(1)}, f32[64,512]{1,0:T(8,128)S(1)}, u32[]{:S(2)}, u32[]{:S(2)}) collective-permute-start(f32[64,512]{1,0:T(8,128)S(1)} %get-tuple-element.30), channel_id=1, source_target_pairs={{0,4},{2,6},{4,0},{6,2},{1,5},{3,7},{5,1},{7,3},{8,12},{10,14},{12... | collective-permute-start | bytes 393224 | tf_op jit(solution)/shard_map/ppermute | solution.py:290
  122.5 0.0 collective-permute-done.4
  122.5 0.7 collective-permute-done.6
  123.2 2.8 %collective-permute-done.5 = f32[64,512]{1,0:T(8,128)S(1)} collective-permute-done((f32[64,512]{1,0:T(8,128)S(1)}, f32[64,512]{1,0:T(8,128)S(1)}, u32[]{:S(2)}, u32[]{:S(2)}) %collective-permute-start.5) | collective-permute-done | bytes 131104 | tf_op jit(solution)/shard_map/ppermute | solution.py:290
  126.0 0.0 copy-start.3
  126.1 8.9 %all-to-all-done.3 = f16[16,32,512]{2,1,0:T(8,128)(2,1)S(1)} async-done(((f16[16,32,512]{2,1,0:T(8,128)(2,1)}), f16[16,32,512]{2,1,0:T(8,128)(2,1)S(1)}, u32[]{:S(2)}, u32[]{:S(2)}) %all-to-all-start.3) | async-done | bytes 524320 | tf_op jit(solution)/shard_map/all_to_all | solution.py:348
  135.0 0.1 convert_element_type.11.nodes_ref
  135.1 1.6 shard_map.56
  136.7 0.0 copy-done.3
  136.7 8.6 %all_to_all.31.sums_ref = f32[8,2,128]{2,1,0:T(2,128)S(1)} all-to-all(f32[8,2,128]{2,1,0:T(2,128)S(1)} %shard_map.56), channel_id=1, replica_groups=mesh['y'=4,'zh'=4,'zl'=4,'x'=4,'c'=2] {'x','c'}, dimensions={0} | all-to-all | bytes 16384 | tf_op jit(solution)/shard_map/all_to_all | solution.py:357
  145.3 21.7 %all_to_all.32.sums_ref = f32[64,2,128]{2,1,0:T(2,128)S(1)} all-to-all(f32[64,2,128]{2,1,0:T(2,128)S(1)} %shard_map.57), channel_id=1, replica_groups=mesh['y'=4,'zh'=4,'zl'=4,'x'=4,'c'=2] {'y','zh','zl'}, dimensions={0} | all-to-all | bytes 131072 | tf_op jit(solution)/shard_map/all_to_all | solution.py:360
  167.0 1.7 %shard_map.58 = f32[32,512]{1,0:T(8,128)} custom-call(f32[64,2,128]{2,1,0:T(2,128)S(1)} %all_to_all.32.sums_ref, f32[16,32,512]{2,1,0:T(8,128)S(1)} %convert_element_type.11.nodes_ref), custom_call_target="tpu_custom_call" | custom-call | flops 524288 | bytes 1048576 | tf_op jit(solution)/shard_map/pallas_call | solution.py:361
  (4 shorter events, 0.1 us)
Async XLA Ops:
  9.7 20.7 %all-to-all-start = ((bf16[4,64,512]{2,1,0:T(8,128)(2,1)}), bf16[4,64,512]{2,1,0:T(8,128)(2,1)S(1)}, u32[]{:S(2)}, u32[]{:S(2)}) async-start(bf16[4,64,512]{2,1,0:T(8,128)(2,1)} %shard_map.50), calls=%async_computation | async-start | bytes 524288 | tf_op jit(solution)/shard_map/all_to_all | solution.py:299
  16.2 1.6 copy-start
  21.0 19.1 %collective-permute-start = (bf16[512,512]{1,0:T(8,128)(2,1)}, bf16[512,512]{1,0:T(8,128)(2,1)S(1)}, u32[]{:S(2)}, u32[]{:S(2)}) collective-permute-start(bf16[512,512]{1,0:T(8,128)(2,1)} %get-tuple-element.15), channel_id=1, source_target_pairs={{0,24},{8,16},{16,8},{24,0},{1,25},{9,17},{17,9},{25,1},{2,26},{10... | collective-permute-start | bytes 1572872 | tf_op jit(solution)/shard_map/ppermute | solution.py:290
  26.2 45.6 %collective-permute-start.1 = (bf16[512,512]{1,0:T(8,128)(2,1)}, bf16[512,512]{1,0:T(8,128)(2,1)}, u32[]{:S(2)}, u32[]{:S(2)}) collective-permute-start(bf16[512,512]{1,0:T(8,128)(2,1)} %get-tuple-element.16), channel_id=1, source_target_pairs={{0,16},{8,24},{16,0},{24,8},{1,17},{9,25},{17,1},{25,9},{2,18},{10... | collective-permute-start | bytes 1572872 | tf_op jit(solution)/shard_map/ppermute | solution.py:290
  28.1 43.7 %collective-permute-start.2 = (bf16[512,512]{1,0:T(8,128)(2,1)}, bf16[512,512]{1,0:T(8,128)(2,1)}, u32[]{:S(2)}, u32[]{:S(2)}) collective-permute-start(bf16[512,512]{1,0:T(8,128)(2,1)} %get-tuple-element.17), channel_id=1, source_target_pairs={{0,8},{8,0},{16,24},{24,16},{1,9},{9,1},{17,25},{25,17},{2,10},{10... | collective-permute-start | bytes 1572872 | tf_op jit(solution)/shard_map/ppermute | solution.py:290
  32.0 39.8 %all-to-all-start.1 = ((bf16[8,4,64,512]{3,2,1,0:T(8,128)(2,1)}), bf16[8,4,64,512]{3,2,1,0:T(8,128)(2,1)S(1)}, u32[]{:S(2)}, u32[]{:S(2)}) async-start(bf16[8,4,64,512]{3,2,1,0:T(8,128)(2,1)} %broadcast_in_dim.3), calls=%async_computation.1 | async-start | bytes 4194304 | tf_op jit(solution)/shard_map/all_to_all | solution.py:47
  89.3 16.2 %copy-start.1 = (bf16[512,2048]{1,0:T(8,128)(2,1)S(1)}, bf16[512,2048]{1,0:T(8,128)(2,1)}, u32[]{:S(2)}) copy-start(bf16[512,2048]{1,0:T(8,128)(2,1)} %pre_ref.3) | copy-start | bytes 6291460
  90.3 44.7 %all-to-all-start.3 = ((f16[16,32,512]{2,1,0:T(8,128)(2,1)}), f16[16,32,512]{2,1,0:T(8,128)(2,1)S(1)}, u32[]{:S(2)}, u32[]{:S(2)}) async-start(f16[16,32,512]{2,1,0:T(8,128)(2,1)} %bitcast.8), calls=%async_computation.3 | async-start | bytes 1048576 | tf_op jit(solution)/shard_map/all_to_all | solution.py:348
  105.6 1.6 copy-start.2
  109.0 4.4 %collective-permute-start.3 = (f32[4,64,512]{2,1,0:T(8,128)S(1)}, f32[4,64,512]{2,1,0:T(8,128)S(1)}, u32[]{:S(2)}, u32[]{:S(2)}) collective-permute-start(f32[4,64,512]{2,1,0:T(8,128)S(1)} %get-tuple-element.26), channel_id=1, source_target_pairs={{0,1},{1,0},{2,3},{3,2},{4,5},{5,4},{6,7},{7,6},{8,9},{9,8},{10,11... | collective-permute-start | bytes 1572872 | tf_op jit(solution)/shard_map/ppermute | solution.py:290
  113.5 9.0 %collective-permute-start.4 = (f32[64,512]{1,0:T(8,128)S(1)}, f32[64,512]{1,0:T(8,128)S(1)}, u32[]{:S(2)}, u32[]{:S(2)}) collective-permute-start(f32[64,512]{1,0:T(8,128)S(1)} %get-tuple-element.28), channel_id=1, source_target_pairs={{0,2},{2,0},{4,6},{6,4},{1,3},{3,1},{5,7},{7,5},{8,10},{10,8},{12,... | collective-permute-start | bytes 393224 | tf_op jit(solution)/shard_map/ppermute | solution.py:290
  115.7 7.5 %collective-permute-start.6 = (f32[64,512]{1,0:T(8,128)S(1)}, f32[64,512]{1,0:T(8,128)S(1)}, u32[]{:S(2)}, u32[]{:S(2)}) collective-permute-start(f32[64,512]{1,0:T(8,128)S(1)} %get-tuple-element.29), channel_id=1, source_target_pairs={{0,6},{2,4},{4,2},{6,0},{1,7},{3,5},{5,3},{7,1},{8,14},{10,12},{12... | collective-permute-start | bytes 393224 | tf_op jit(solution)/shard_map/ppermute | solution.py:290
  118.5 7.5 %collective-permute-start.5 = (f32[64,512]{1,0:T(8,128)S(1)}, f32[64,512]{1,0:T(8,128)S(1)}, u32[]{:S(2)}, u32[]{:S(2)}) collective-permute-start(f32[64,512]{1,0:T(8,128)S(1)} %get-tuple-element.30), channel_id=1, source_target_pairs={{0,4},{2,6},{4,0},{6,2},{1,5},{3,7},{5,1},{7,3},{8,12},{10,14},{12... | collective-permute-start | bytes 393224 | tf_op jit(solution)/shard_map/ppermute | solution.py:290
  126.0 10.6 %copy-start.3 = (bf16[64,512]{1,0:T(8,128)(2,1)}, bf16[64,512]{1,0:T(8,128)(2,1)S(1)}, u32[]{:S(2)}) copy-start(bf16[64,512]{1,0:T(8,128)(2,1)S(1)} %fusion.3.late_ref) | copy-start | bytes 196612
